TPU v7x, 32 devices: a whole 2x2x4 slice. The times are simulated.
32 devices in a mesh: gx: 4 (over y, core), gy: 8 (over z, x).
Axes of the slice: x: 2, y: 2, z: 4, core: 2. Of those that a mesh axis runs over, the one named last changes fastest.
Arguments:
- velocity: float32 [3, 384, 256, 256], P(None, 'gx', 'gy'), may hold values from -6 to 6
- inflow: float32 [3, 256, 256], P(None, 'gy'), may hold values from -5 to 5
- positions: int32 [4, 64, 3, 256], P('gx'), may hold values from 0 to 381, as said below
- tiles: int32 [4, 64, 2], P('gx'), may hold values from 0 to 7, as said below
- coefs: float32 [4, 64, 256], P('gx'), may hold values from 2 to 20
- counts: int32 [4], P('gx'), may hold values from 1 to 64, as said below
Outputs:
- velocity_next: float32 [3, 384, 256, 256], P(None, 'gx', 'gy')
- blade_force: float32 [4, 64, 3, 256], P('gx')
Inputs may be any that keep to these rules, and one draw needn't show every extreme that they name: `positions`: for a record of tile row r, coordinate 0 is one value for all its points, from r * 96 + 2 to r * 96 + 93; coordinate 2 lies from 2 to 253; the points of a record lie on a straight segment in y and z. tiles[r, s, 1] is 2 or 3; the first listed y tile is the lowest y tile that holds a cell within 2 in y of some point of the record, or the tile after it. Records of row r with index below counts[r] are live; some row is full and some row has one live record.
All inputs are finite; a program needn't handle non-finite values.
Results may differ from a plain program's by a relative error of at most 0.00008.
Values sent between devices are 32-bit elements; how exact they have to be, the bound alone decides.
No kernel may reach another device: no remote copies, remote signals or barrier semaphores. Data moves between devices by JAX's collectives and lax.ppermute only.
A program may use at most 128 MiB of HBM per device.

v0:
```python
import math

import jax
import jax.numpy as jnp
from jax import lax
from jax.experimental import pallas as pl
from jax.experimental.pallas import tpu as pltpu
from jax.sharding import PartitionSpec as P

RAD = 2
VISCOSITY = 0.05
TIME_STEP = 0.1
WIDTH_EPS = 1.5
ROOT_PI = 1.7724538509055159
TAP = [math.exp(-((d / WIDTH_EPS) ** 2)) / (WIDTH_EPS * ROOT_PI) for d in range(RAD + 1)]
HIGH = [float(jnp.bfloat16(tap)) for tap in TAP]
LOW = [float(jnp.bfloat16(tap - high)) for tap, high in zip(TAP, HIGH)]
LANES = 128
SUB = 8
PACKED = 32
BATCH = 4
VMEM_LIMIT = 5 * 2**20

WHOLE = pl.BlockSpec(memory_space=pltpu.VMEM)
SCALAR = pl.BlockSpec(memory_space=pltpu.SMEM)
ANYWHERE = pl.BlockSpec(memory_space=pl.ANY)


def params(limit=VMEM_LIMIT):
    return pltpu.CompilerParams(vmem_limit_bytes=limit)


def cost(flops, nbytes):
    return pl.CostEstimate(flops=flops, bytes_accessed=nbytes, transcendentals=0)


def resident(x):
    return pltpu.with_memory_space_constraint(x, pltpu.VMEM)


def streamed(x):
    return pltpu.with_memory_space_constraint(x, pltpu.HBM)


def split(x):
    high = x.astype(jnp.bfloat16)
    low = (x - high.astype(jnp.float32)).astype(jnp.bfloat16)
    return jnp.concatenate([high, low], axis=0)


def along_z(point_z, start):
    points = point_z.shape[-1]
    row = lax.broadcasted_iota(jnp.int32, (PACKED, points), 0).astype(jnp.bfloat16)
    place = (point_z - start).astype(jnp.float32)
    place = jnp.broadcast_to(place, (PACKED, points)).astype(jnp.bfloat16)
    dist = jnp.abs(row - place)
    near = [dist == float(d) for d in range(RAD + 1)]
    out = []
    for taps in (HIGH, LOW):
        value = jnp.zeros_like(row)
        for d in range(RAD, -1, -1):
            value = jnp.where(near[d], jnp.full_like(row, taps[d]), value)
        out.append(value)
    return out


def wrapped(point_y, base, total_y):
    near = point_y - base
    near = jnp.where(near > total_y // 2, near - total_y, near)
    return jnp.where(near < -(total_y // 2), near + total_y, near)


def along_y(point_y, base, cells_y, total_y):
    near = wrapped(point_y, base, total_y)
    dist = jnp.abs(lax.broadcasted_iota(jnp.int32, (cells_y, point_y.shape[-1]), 0) - near)
    return jnp.where(
        dist == 0, TAP[0], jnp.where(dist == 1, TAP[1], jnp.where(dist == 2, TAP[2], 0.0))
    )


def make_plan(hubs, tiles, touch, counts, start, plan, bucket, held):
    tile_y, groups_y = lax.axis_index("gy"), lax.axis_size("gy")
    records, chunks = tiles.shape[1], held.shape[0]
    for k in range(chunks):
        held[k] = 0

    def place(r, carry):
        offset = tile_y - tiles[0, r]
        offset = jnp.where(offset < 0, offset + groups_y, offset)

        @pl.when(jnp.logical_and(offset < tiles[1, r], touch[r, 1] >= 0))
        def _():
            k = (hubs[r, 0] - start + RAD) // SUB
            bucket[k, held[k]] = r
            held[k] = held[k] + 1

        return carry

    lax.fori_loop(0, jnp.minimum(counts[0], records), place, 0)

    def flatten(k, found):
        def move(j, found):
            r = bucket[k, j]
            plan[1 + found] = r
            plan[1 + records + found] = hubs[r, 0] - start
            return found + 1

        return lax.fori_loop(0, held[k], move, found)

    plan[0] = lax.fori_loop(0, chunks, flatten, jnp.int32(0))


def pair(plan, t):
    records = (plan.shape[0] - 1) // 2
    first = 2 * t
    second = jnp.minimum(first + 1, plan[0] - 1)
    return [(n, plan[1 + n], plan[1 + records + n]) for n in (first, second)], second > first


def sampled_rows(field, weight_y, weight_z, picks):
    cells_y = field.shape[2]
    rows = 3 * cells_y
    parts = []
    for t, r, hub in picks:
        planes = []
        for c in range(3):
            plane = TAP[0] * field[c, hub]
            plane += TAP[1] * (field[c, hub - 1] + field[c, hub + 1])
            plane += TAP[2] * (field[c, hub - 2] + field[c, hub + 2])
            planes.append(plane)
        parts.append(split(jnp.concatenate(planes, axis=0)))
    out = []
    for (t, r, hub), part in zip(picks, parts):
        picked = jnp.dot(part, weight_z[t, 0], preferred_element_type=jnp.float32)
        rest = jnp.dot(part[:rows], weight_z[t, 1], preferred_element_type=jnp.float32)
        picked = picked[:rows] + (picked[rows:] + rest)
        weight = weight_y[t]
        out.append(
            [
                jnp.sum(picked[c * cells_y : (c + 1) * cells_y] * weight, axis=0, keepdims=True)
                for c in range(3)
            ]
        )
    return out


def pack_edges(field, edge_west, edge_east, pack_low, pack_high):
    cells_x, cells_y, depth = field.shape[1:]
    for c in range(3):
        edge_west[c] = field[c, 0]
        edge_east[c] = field[c, cells_x - 1]

    def step(t, carry):
        cells = [(c, t * BATCH + k) for k in range(BATCH) for c in range(3)]
        rows = [
            (field[c, i, pl.ds(0, 1), :], field[c, i, pl.ds(cells_y - 1, 1), :]) for c, i in cells
        ]
        for (c, i), (low, high) in zip(cells, rows):
            pack_low[c * cells_x + i] = low
            pack_high[c * cells_x + i] = high
        return carry

    lax.fori_loop(0, cells_x // BATCH, step, 0)


def load_sample(
    velocity, positions, tiles_hbm, coefs_hbm, counts,
    field, pack_low, pack_high, edge_west, edge_east, weight_y, weight_z, strength, plan,
    point_y, point_z, hubs, tiles, places, coefs, flags, touch, bucket, held, small_sems, touch_sem, sems,
):
    cells_x, cells_y, depth = field.shape[1:]
    records, points = coefs.shape
    chunks = cells_x // SUB
    first_row = 3 * cells_x
    start = lax.axis_index("gx") * cells_x

    def chunk(k):
        planes = pl.ds(k * SUB, SUB)
        return pltpu.make_async_copy(velocity.at[:, planes], field.at[:, planes], sems.at[k])

    small = [
        (positions.at[pl.ds(1, 2)], places),
        (positions.at[0, :, pl.ds(0, LANES)], hubs),
        (tiles_hbm, tiles),
        (coefs_hbm, coefs),
    ]
    small = [
        pltpu.make_async_copy(source, target, small_sems.at[n])
        for n, (source, target) in enumerate(small)
    ]
    total_y = cells_y * lax.axis_size("gy")
    base = lax.axis_index("gy") * cells_y
    for copy in small:
        copy.start()
    for k in range(chunks):
        chunk(k).start()
    small[0].wait()
    near = wrapped(places[0], base, total_y)
    inside = jnp.logical_and(near >= -RAD, near < cells_y + RAD)
    height = places[1].astype(jnp.float32)
    lowest = jnp.min(jnp.where(inside, height, float(depth)), axis=1, keepdims=True)
    highest = jnp.max(jnp.where(inside, height, -1.0), axis=1, keepdims=True)
    column = lax.broadcasted_iota(jnp.int32, flags.shape, 1)
    flags[...] = jnp.where(column == 0, lowest, highest).astype(jnp.int32)
    touch_copy = pltpu.make_async_copy(flags, touch, touch_sem)
    touch_copy.start()

    def clear(n, carry):
        for k in range(SUB):
            pack_low[first_row + n * SUB + k] = jnp.zeros((1, points), jnp.float32)
            pack_high[first_row + n * SUB + k] = jnp.zeros((1, points), jnp.float32)
        return carry

    lax.fori_loop(0, 3 * records // SUB, clear, 0)
    for copy in small[1:]:
        copy.wait()
    for first in range(0, records, SUB):
        here = range(first, first + SUB)
        rows = [
            (places[0, pl.ds(r, 1), :], places[1, pl.ds(r, 1), :], coefs[pl.ds(r, 1), :])
            for r in here
        ]
        for r, (y, z, coef) in zip(here, rows):
            point_y[r], point_z[r], strength[r] = y, z, coef
    touch_copy.wait()
    make_plan(hubs, tiles, touch, counts, start, plan, bucket, held)

    def weigh(t, carry):
        r = plan[1 + t]
        weight_y[t] = along_y(point_y[r], base, cells_y, total_y)
        weight_z[t] = jnp.zeros(weight_z.shape[1:], weight_z.dtype)

        def block(k, carry):
            rows = pl.ds(pl.multiple_of(k * PACKED, PACKED), PACKED)
            weight_z[t, 0, rows], weight_z[t, 1, rows] = along_z(point_z[r], k * PACKED)
            return carry

        first = (touch[r, 0] - RAD) // PACKED
        lax.fori_loop(first, (touch[r, 1] + RAD) // PACKED + 1, block, 0)
        return carry

    lax.fori_loop(0, plan[0], weigh, 0)

    def wait_to(ready, wanted):
        def step(k, carry):
            chunk(k).wait()
            return carry

        lax.fori_loop(ready, wanted, step, 0)
        return jnp.maximum(ready, wanted)

    def step(t, ready):
        picks, _ = pair(plan, t)
        ready = wait_to(ready, (picks[1][2] + RAD) // SUB + 1)
        for (_, r, _), rows in zip(picks, sampled_rows(field, weight_y, weight_z, picks)):
            for c in range(3):
                pack_low[first_row + 3 * r + c] = rows[c]
                pack_high[first_row + 3 * r + c] = rows[c]
        return ready

    ready = lax.fori_loop(0, (plan[0] + 1) // 2, step, jnp.int32(0))
    wait_to(ready, chunks)
    pack_edges(field, edge_west, edge_east, pack_low, pack_high)


def fix_west(factor, target, own, inflow, ghost):
    first = lax.axis_index("gx") == 0
    for c in range(3):
        west = jnp.where(first, inflow[c], ghost[c])
        coef = factor * TIME_STEP * VISCOSITY + (0.5 * factor * TIME_STEP) * own[0]
        target[c, 0] = target[c, 0] + (west - own[c]) * coef


def fix_east(factor, target, own, ghost):
    last = lax.axis_index("gx") == lax.axis_size("gx") - 1
    end = target.shape[1] - 1
    for c in range(3):
        east = jnp.where(last, own[c], ghost[c])
        coef = factor * TIME_STEP * VISCOSITY - (0.5 * factor * TIME_STEP) * own[0]
        target[c, end] = target[c, end] + (east - own[c]) * coef


def fix_rows(factor, target, own_low, own_high, got_low, got_high, t):
    cells_x, cells_y = target.shape[1:3]
    spread = factor * TIME_STEP * VISCOSITY
    half = 0.5 * factor * TIME_STEP
    shape = (SUB, target.shape[3])
    row = lax.broadcasted_iota(jnp.int32, shape, 0)
    low, high = pl.ds(0, SUB), pl.ds(cells_y - SUB, SUB)

    def wide(x):
        return jnp.broadcast_to(x, shape)

    for first in range(0, SUB, 2):
        values = []
        for k in range(first, first + 2):
            i = t * SUB + k
            south = jnp.where(row == 0, spread + half * wide(own_low[cells_x + i]), 0.0)
            north = jnp.where(row == SUB - 1, spread - half * wide(own_high[cells_x + i]), 0.0)
            for c in range(3):
                n = c * cells_x + i
                values.append((c, i, low, target[c, i, low, :] + wide(got_low[n]) * south))
                values.append((c, i, high, target[c, i, high, :] + wide(got_high[n]) * north))
        for c, i, rows, value in values:
            target[c, i, rows, :] = value


def slabs_of(weight_y, weight_z, strength, own, low, high, cells, scales, picks):
    cells_x, cells_y, depth = cells
    count = 3 * cells_y
    across = (((1,), (1,)), ((), ()))
    spread = []
    for (t, r, hub), scale in zip(picks, scales):
        rows = [3 * cells_x + 3 * r + c for c in range(3)]
        total = [own[n] + (low[n] + high[n]) for n in rows]
        speed = jnp.sqrt(total[0] * total[0] + total[1] * total[1] + total[2] * total[2])
        pull = strength[r] * (-scale) * speed
        weight = weight_y[t]
        spread.append(split(jnp.concatenate([weight * (pull * x) for x in total], axis=0)))
    slabs = []
    for (t, r, hub), part in zip(picks, spread):
        slab = lax.dot_general(part, weight_z[t, 0], across, preferred_element_type=jnp.float32)
        rest = lax.dot_general(
            part[:count], weight_z[t, 1], across, preferred_element_type=jnp.float32
        )
        slabs.append(slab[:count] + (slab[count:] + rest))
    return slabs


def add_slab(field, slab, hub):
    cells_y = field.shape[2]
    for c in range(3):
        part = slab[c * cells_y : (c + 1) * cells_y]
        terms = [tap * part for tap in TAP]
        reach = range(-RAD, RAD + 1)
        values = [field[c, hub + d] + terms[abs(d)] for d in reach]
        for d, value in zip(reach, values):
            field[c, hub + d] = value


def spread_pair(t, scale, field, plan, points, own, low, high):
    picks, both = pair(plan, t)
    scales = [scale, jnp.where(both, scale, 0.0)]
    slabs = slabs_of(*points, own, low, high, field.shape[1:], scales, picks)
    for (_, _, hub), slab in zip(picks, slabs):
        add_slab(field, slab, hub)


def spread_sample(
    section_in, inflow, ghost_low, ghost_high, own_low, own_high, own_west, own_east, got_low, got_high,
    plan, weight_y, weight_z, strength,
    section, section_out, stored_y, stored_z, pack_low, pack_high, edge_west, edge_east,
    share_out, sem, sem_y, sem_z,
):
    cells_x = section.shape[1]
    records = strength.shape[0]
    share = share_out.shape[2] // 3
    first_row = 3 * cells_x

    def copies(t):
        return (
            pltpu.make_async_copy(weight_y.at[t], stored_y.at[t], sem_y.at[t]),
            pltpu.make_async_copy(weight_z.at[t], stored_z.at[t], sem_z.at[t]),
        )

    def start_store(t, carry):
        for copy in copies(t):
            copy.start()
        return carry

    def wait_store(t, carry):
        for copy in copies(t):
            copy.wait()
        return carry

    lax.fori_loop(0, plan[0], start_store, 0)

    def fix_step(t, carry):
        fix_rows(1.0, section, own_low, own_high, got_low, got_high, t)
        return carry

    fix_west(1.0, section, own_west, inflow, ghost_low)
    fix_east(1.0, section, own_east, ghost_high)
    lax.fori_loop(0, cells_x // SUB, fix_step, 0)

    def spread_step(t, carry):
        points = (weight_y, weight_z, strength)
        spread_pair(t, TIME_STEP, section, plan, points, own_low, got_low, got_high)
        return carry

    lax.fori_loop(0, (plan[0] + 1) // 2, spread_step, 0)
    copy = pltpu.make_async_copy(section, section_out, sem)
    copy.start()
    pack_edges(section, edge_west, edge_east, pack_low, pack_high)

    def clear(r, carry):
        rows = [own_low[first_row + 3 * r + c] for c in range(3)]
        zero = jnp.zeros_like(rows[0])
        for c in range(3):
            pack_low[first_row + 3 * r + c] = zero
            pack_high[first_row + 3 * r + c] = zero
            share_out[r // share, 0, 3 * (r % share) + c] = rows[c]
            share_out[r // share, 1, 3 * (r % share) + c] = zero
        return carry

    lax.fori_loop(0, records, clear, 0)

    def sample_step(t, carry):
        picks, _ = pair(plan, t)
        for (_, r, _), rows in zip(picks, sampled_rows(section, weight_y, weight_z, picks)):
            for c in range(3):
                pack_low[first_row + 3 * r + c] = rows[c]
                pack_high[first_row + 3 * r + c] = rows[c]
                share_out[r // share, 1, 3 * (r % share) + c] = rows[c]
        return carry

    lax.fori_loop(0, (plan[0] + 1) // 2, sample_step, 0)
    lax.fori_loop(0, plan[0], wait_store, 0)
    copy.wait()


def share_force(parts, strength, counts, after, after_low, after_high, result):
    groups, _, rows = parts.shape[:3]
    share = rows // 3
    mine = lax.axis_index("gy") * share
    values = []
    for s in range(share):
        live = mine + s < counts[0]
        pull = jnp.where(live, -0.5 * strength[mine + s], 0.0)
        total = [0.0, 0.0, 0.0]
        for stage in range(2):
            value = []
            for c in range(3):
                n = 3 * s + c
                x = parts[0, stage, n]
                for g in range(1, groups):
                    x += parts[g, stage, n]
                value.append(x)
            speed = jnp.sqrt(value[0] * value[0] + value[1] * value[1] + value[2] * value[2])
            total = [acc + speed * x for acc, x in zip(total, value)]
        values.extend((3 * s + c, pull * total[c]) for c in range(3))
        if s % 2 == 1 or s + 1 == share:
            for n, value in values:
                for g in range(groups):
                    result[g, n] = value
            values = []


def spread_next(
    following, inflow, ghost_low, ghost_high, own_low, own_high, own_west, own_east, got_low, got_high,
    plan, stored_y, stored_z, strength, after,
    result, field, weight_y, weight_z, in_sems, out_sems, sem_y, sem_z,
):
    chunks = field.shape[1] // SUB
    factor = 0.5

    def chunk_in(k):
        planes = pl.ds(k * SUB, SUB)
        return pltpu.make_async_copy(following.at[:, planes], field.at[:, planes], in_sems.at[k])

    def chunk_out(k):
        planes = pl.ds(k * SUB, SUB)
        return pltpu.make_async_copy(field.at[:, planes], result.at[:, planes], out_sems.at[k])

    def wait_to(ready, wanted):
        def step(k, carry):
            chunk_in(k).wait()
            fix_rows(factor, field, own_low, own_high, got_low, got_high, k)

            @pl.when(k == 0)
            def _():
                fix_west(factor, field, own_west, inflow, ghost_low)

            @pl.when(k == chunks - 1)
            def _():
                fix_east(factor, field, own_east, ghost_high)

            return carry

        lax.fori_loop(ready, wanted, step, 0)
        return jnp.maximum(ready, wanted)

    def send_to(sent, done):
        def step(k, carry):
            chunk_out(k).start()
            return carry

        lax.fori_loop(sent, done, step, 0)
        return jnp.maximum(sent, done)

    def weights(t):
        return (
            pltpu.make_async_copy(stored_y.at[t], weight_y.at[t], sem_y.at[t]),
            pltpu.make_async_copy(stored_z.at[t], weight_z.at[t], sem_z.at[t]),
        )

    def start_weights(t, carry):
        for copy in weights(t):
            copy.start()
        return carry

    found = plan[0]
    for k in range(chunks):
        chunk_in(k).start()
        lax.fori_loop(k * found // chunks, (k + 1) * found // chunks, start_weights, 0)

    def step(t, carry):
        ready, sent = carry
        picks, both = pair(plan, t)
        for copy in weights(picks[0][0]):
            copy.wait()

        @pl.when(both)
        def _():
            for copy in weights(picks[1][0]):
                copy.wait()

        ready = wait_to(ready, (picks[1][2] + RAD) // SUB + 1)
        sent = send_to(sent, (picks[0][2] + RAD) // SUB - 1)
        points = (weight_y, weight_z, strength)
        spread_pair(t, factor * TIME_STEP, field, plan, points, own_low, got_low, got_high)
        return ready, sent

    zero = jnp.int32(0)
    ready, sent = lax.fori_loop(0, (plan[0] + 1) // 2, step, (zero, zero))
    sent = send_to(sent, ready)

    def finish(k, carry):
        wait_to(k, k + 1)
        chunk_out(k).start()
        return carry

    lax.fori_loop(ready, chunks, finish, 0)
    for k in range(chunks):
        chunk_out(k).wait()


def fill_shifts(shifts):
    depth = shifts.shape[1]
    source = lax.broadcasted_iota(jnp.int32, (depth, depth), 0)
    cell = lax.broadcasted_iota(jnp.int32, (depth, depth), 1)
    upper = jnp.where(source == cell + 1, 1.0, 0.0)
    lower = jnp.where(source == cell - 1, 1.0, 0.0)
    difference = (upper - lower).astype(shifts.dtype)
    shifts[0:depth] = difference
    shifts[depth : 2 * depth] = difference
    shifts[2 * depth : 3 * depth] = (upper + lower).astype(shifts.dtype)


def along_depth(i, field, shifts, slot):
    depth = shifts.shape[1]
    x = jnp.concatenate([field[c, i + k] for k in range(2) for c in range(3)], axis=0)
    high = x.astype(jnp.bfloat16)
    low = (x - high.astype(jnp.float32)).astype(jnp.bfloat16)
    slot[0] = jnp.dot(
        jnp.concatenate([high, low], axis=1),
        shifts[0 : 2 * depth],
        preferred_element_type=jnp.float32,
    )
    slot[1] = jnp.dot(
        high, shifts[2 * depth : 3 * depth], preferred_element_type=jnp.float32
    )


def advance(i, k, factor, field, slot, target, finish):
    cells_x, cells_y, depth = field.shape[1:]
    groups, halves = cells_y // SUB, depth // LANES
    row = lax.broadcasted_iota(jnp.int32, (SUB, LANES), 0)
    first_row, last_row = row == 0, row == SUB - 1
    spread = factor * TIME_STEP * VISCOSITY
    centre = factor * (1.0 - 6.0 * TIME_STEP * VISCOSITY)
    zero = jnp.zeros((SUB, LANES), jnp.float32)
    loaded = {}
    here = i + k
    west, east = jnp.maximum(here - 1, 0), jnp.minimum(here + 1, cells_x - 1)

    def at(c, g, h):
        if (c, g, h) not in loaded:
            loaded[c, g, h] = field[c, here, pl.ds(g * SUB, SUB), pl.ds(h * LANES, LANES)]
        return loaded[c, g, h]

    values = []
    for g in range(groups):
        for h in range(halves):
            rows, cols = pl.ds(g * SUB, SUB), pl.ds(h * LANES, LANES)
            q = [at(c, g, h) for c in range(3)]
            speeds = [(0.5 * factor * TIME_STEP) * x for x in q]
            less = [spread - s for s in speeds[:2]]
            more = [spread + s for s in speeds[:2]]
            if g == 0:
                more[1] = jnp.where(first_row, zero, more[1])
            if g == groups - 1:
                less[1] = jnp.where(last_row, zero, less[1])
            for c in range(3):
                x = q[c]
                above, below = x, x
                if g + 1 < groups:
                    above = jnp.where(first_row, at(c, g + 1, h), x)
                if g > 0:
                    below = jnp.where(last_row, at(c, g - 1, h), x)
                above, below = pltpu.roll(above, SUB - 1, 0), pltpu.roll(below, 1, 0)
                place = pl.ds((3 * k + c) * cells_y + g * SUB, SUB)
                total = centre * x
                total += field[c, east, rows, cols] * less[0]
                total += field[c, west, rows, cols] * more[0]
                total += above * less[1] + below * more[1]
                total += spread * slot[1, place, cols] - speeds[2] * slot[0, place, cols]
                values.append((c, rows, cols, finish(c, here, rows, cols, total)))
        if g % 2 == 1 or g + 1 == groups:
            for c, rows, cols, value in values:
                target[c, here, rows, cols] = value
            values = []


def advance_four(i, factor, field, shifts, slots, target, finish):
    last = field.shape[1] - 2
    for n in range(2):
        now, later = slots[n], slots[1 - n]
        along_depth(jnp.minimum(i + 2, last), field, shifts, later)
        for k in range(2):
            advance(i, k, factor, field, now, target, finish)
        i = i + 2


def advance_first(field, section, shifts, slot_a, slot_b):
    fill_shifts(shifts)
    along_depth(0, field, shifts, slot_a)

    def step(t, carry):
        advance_four(
            4 * t, 1.0, field, shifts, (slot_a, slot_b), section,
            lambda c, i, rows, cols, value: value,
        )
        return carry

    lax.fori_loop(0, field.shape[1] // 4, step, 0)


def advance_second(
    section_hbm, velocity, following, token,
    section, field, result, shifts, slot_a, slot_b, in_sems, old_sems, out_sems,
):
    chunks = section.shape[1] // SUB

    def planes(k):
        return pl.ds(k * SUB, SUB)

    def chunk_in(k):
        return pltpu.make_async_copy(
            section_hbm.at[:, planes(k)], section.at[:, planes(k)], in_sems.at[k]
        )

    def chunk_old(k):
        return pltpu.make_async_copy(
            velocity.at[:, planes(k)], field.at[:, planes(k)], old_sems.at[k]
        )

    def chunk_out(k):
        return pltpu.make_async_copy(
            result.at[:, planes(k)], following.at[:, planes(k)], out_sems.at[k]
        )

    def finish(c, i, rows, cols, value):
        return value + 0.5 * field[c, i, rows, cols]

    for k in range(chunks):
        chunk_in(k).start()
        chunk_old(k).start()
    token[...] = jnp.zeros_like(token)
    fill_shifts(shifts)
    chunk_in(0).wait()
    along_depth(0, section, shifts, slot_a)

    def step(k, carry):
        @pl.when(k + 1 < chunks)
        def _():
            chunk_in(k + 1).wait()

        chunk_old(k).wait()
        for n in range(0, SUB, 4):
            advance_four(
                k * SUB + n, 0.5, section, shifts, (slot_a, slot_b), result, finish
            )
        chunk_out(k).start()
        return carry

    lax.fori_loop(0, chunks, step, 0)
    for k in range(chunks):
        chunk_out(k).wait()


def shifted(x, axis, step, periodic):
    count = lax.axis_size(axis)
    pairs = [(i, (i + step) % count) for i in range(count)]
    if not periodic:
        pairs = [(s, t) for s, t in pairs if t - s == step]
    return lax.ppermute(x, axis, pairs)


def exchange(pack_low, pack_high, edge_west, edge_east):
    got_low = shifted(pack_high, "gy", 1, True)
    got_high = shifted(pack_low, "gy", -1, True)
    ghost_low = shifted(edge_east, "gx", 1, False)
    ghost_high = shifted(edge_west, "gx", -1, False)
    return ghost_low, ghost_high, got_low, got_high


def local(velocity, inflow, positions, tiles, coefs, counts):
    f32, i32 = jnp.float32, jnp.int32
    whole = velocity.shape
    _, cells_x, cells_y, depth = whole
    groups_y = lax.axis_size("gy")
    positions = positions[0].transpose(1, 0, 2)
    tiles, coefs = tiles[0].T, coefs[0]
    records, points = coefs.shape
    share = records // groups_y
    chunks = cells_x // SUB
    size = 4 * math.prod(whole)
    held = pltpu.VMEM(whole, f32)
    stored = pltpu.HBM(whole, f32)
    array = jax.ShapeDtypeStruct
    pack = array((3 * cells_x + 3 * records, 1, points), f32)
    edge = array((3, cells_y, depth), f32)
    per_record = (records, 1, points)
    y_shape, z_shape = (records, cells_y, points), (records, 2, depth, points)
    y_bytes, z_bytes = 4 * math.prod(y_shape), 2 * math.prod(z_shape)
    products = [pltpu.VMEM((3 * depth, depth), jnp.bfloat16)]
    products += [pltpu.VMEM((2, 6 * cells_y, depth), f32)] * 2
    record_sems = pltpu.SemaphoreType.DMA((records,))
    chunk_sems = pltpu.SemaphoreType.DMA((chunks,))

    field, *own_a, weight_y, weight_z, strength, plan = pl.pallas_call(
        load_sample,
        out_shape=(
            held, pack, pack, edge, edge,
            pltpu.VMEM(y_shape, f32), pltpu.VMEM(z_shape, jnp.bfloat16),
            array(per_record, f32),
            array((1 + 2 * records,), i32),
        ),
        in_specs=[ANYWHERE] * 4 + [SCALAR],
        out_specs=(WHOLE,) * 8 + (SCALAR,),
        scratch_shapes=[
            pltpu.VMEM(per_record, i32),
            pltpu.VMEM(per_record, i32),
            pltpu.SMEM((records, LANES), i32),
            pltpu.SMEM((2, records), i32),
            pltpu.VMEM((2, records, points), i32),
            pltpu.VMEM((records, points), f32),
            pltpu.VMEM((records, LANES), i32),
            pltpu.SMEM((records, LANES), i32),
            pltpu.SMEM((chunks, records), i32),
            pltpu.SMEM((chunks,), i32),
            pltpu.SemaphoreType.DMA((4,)),
            pltpu.SemaphoreType.DMA,
            chunk_sems,
        ],
        compiler_params=params(),
        cost_estimate=cost(2 * 10**9, 4 * size),
        name="load_sample",
    )(streamed(velocity), streamed(positions), streamed(tiles), streamed(coefs), counts)
    weight_y, weight_z = resident(weight_y), resident(weight_z)
    ghosts_a = exchange(*own_a)

    section = pl.pallas_call(
        advance_first,
        out_shape=held,
        in_specs=[WHOLE],
        out_specs=WHOLE,
        scratch_shapes=products,
        compiler_params=params(),
        cost_estimate=cost(10**9, 4 * size),
        name="advance_first",
    )(resident(field))

    _, section, stored_y, stored_z, *own_b, shares = pl.pallas_call(
        spread_sample,
        out_shape=(
            held, stored, pltpu.HBM(y_shape, f32), pltpu.HBM(z_shape, jnp.bfloat16),
            pack, pack, edge, edge,
            array((groups_y, 2, 3 * share, 1, points), f32),
        ),
        in_specs=[WHOLE] * 10 + [SCALAR] + [WHOLE] * 3,
        out_specs=(WHOLE,) + (ANYWHERE,) * 3 + (WHOLE,) * 5,
        input_output_aliases={0: 0},
        scratch_shapes=[pltpu.SemaphoreType.DMA, record_sems, record_sems],
        compiler_params=params(),
        cost_estimate=cost(2 * 10**9, 4 * size),
        name="spread_sample",
    )(
        resident(section), inflow, *ghosts_a[:2], *own_a, *ghosts_a[2:],
        plan, weight_y, weight_z, strength,
    )
    shares = lax.all_to_all(shares, "gy", 0, 0)
    ghosts_b = exchange(*own_b)

    following, token = pl.pallas_call(
        advance_second,
        out_shape=(stored, array((SUB, LANES), f32)),
        in_specs=[ANYWHERE] * 2,
        out_specs=(ANYWHERE, WHOLE),
        scratch_shapes=[pltpu.VMEM(whole, f32)] * 3 + products + [chunk_sems] * 3,
        compiler_params=params(VMEM_LIMIT + 3 * size),
        cost_estimate=cost(10**9, 4 * size),
        name="advance_second",
    )(streamed(section), streamed(velocity))

    forces = pl.pallas_call(
        share_force,
        out_shape=array((groups_y, 3 * share, 1, points), f32),
        in_specs=[WHOLE, WHOLE, SCALAR] + [ANYWHERE] * 3,
        out_specs=WHOLE,
        compiler_params=params(),
        cost_estimate=cost(10**6, 10**6),
        name="share_force",
    )(shares, strength, counts, token, *ghosts_b[:2])
    all_forces = lax.all_to_all(forces, "gy", 0, 0)

    velocity_next = pl.pallas_call(
        spread_next,
        out_shape=stored,
        in_specs=[ANYWHERE] + [WHOLE] * 9 + [SCALAR, ANYWHERE, ANYWHERE, WHOLE, ANYWHERE],
        out_specs=ANYWHERE,
        scratch_shapes=[
            pltpu.VMEM(whole, f32),
            pltpu.VMEM(y_shape, f32),
            pltpu.VMEM(z_shape, jnp.bfloat16),
            chunk_sems, chunk_sems, record_sems, record_sems,
        ],
        compiler_params=params(VMEM_LIMIT + size + y_bytes + z_bytes),
        cost_estimate=cost(2 * 10**9, 4 * size),
        name="spread_next",
    )(
        streamed(following), inflow, *ghosts_b[:2], *own_b, *ghosts_b[2:],
        plan, streamed(stored_y), streamed(stored_z), strength, forces,
    )
    return (velocity_next, all_forces.reshape(1, records, 3, points))


def solution(mesh):
    return jax.shard_map(
        local,
        mesh=mesh,
        in_specs=(
            P(None, "gx", "gy", None),
            P(None, "gy", None),
            P("gx", None, None, None),
            P("gx", None, None),
            P("gx", None, None),
            P("gx"),
        ),
        out_specs=(P(None, "gx", "gy", None), P("gx", None, None, None)),
        check_vma=False,
    )
```

profile of v0, /device:TPU:1, one launch (start us, length us, event | category | flops | bytes accessed | tf_op | source)
XLA Modules:
  0.0 92.8 jit_solution(5845800066450557127)
XLA Ops:
  1.3 11.6 %load_sample.1 = (f32[3,96,32,256]{3,2,1,0:T(8,128)S(1)}, f32[480,1,256]{2,1,0:T(1,128)S(1)}, f32[480,1,256]{2,1,0:T(1,128)S(1)}, f32[3,32,256]{2,1,0:T(8,128)S(...) custom-call(f32[3,96,32,256]{3,2,1,0:T(8,128)} %velocity.3, ...), custom_call_target="tpu_custom_call" | custom-call | flops 2000000000 | bytes 37748736 | tf_op jit(solution)/shard_map/load_sample/pallas_call | solution.py:732
  12.9 4.6 %collective-permute-start.3 = (f32[480,1,256]{2,1,0:T(1,128)S(1)}, f32[480,1,256]{2,1,0:T(1,128)S(1)}, u32[]{:S(2)}, u32[]{:S(2)}) collective-permute-start(f32[480,1,256]{2,1,0:T(1,128)S(1)} %get-tuple-element.24.own_low), channel_id=1, source_target_pairs={{0,7},{1,0},{2,1},{3,2},{4,3},{5,4},{6,5},{7,6},{8,15},{9,8},{10,9... | collective-permute-start | bytes 1474568 | tf_op jit(solution)/shard_map/ppermute | solution.py:697
  17.5 0.0 collective-permute-start.2
  17.5 1.9 %collective-permute-start = (f32[3,32,256]{2,1,0:T(8,128)S(1)}, f32[3,32,256]{2,1,0:T(8,128)S(1)}, u32[]{:S(2)}, u32[]{:S(2)}) collective-permute-start(f32[3,32,256]{2,1,0:T(8,128)S(1)} %get-tuple-element.22.own_east), channel_id=1, source_target_pairs={{0,8},{8,16},{16,24},{1,9},{9,17},{17,25},{2,10},{10,18},{18,26},{... | collective-permute-start | bytes 294920 | tf_op jit(solution)/shard_map/ppermute | solution.py:697
  19.4 2.4 %collective-permute-start.1 = (f32[3,32,256]{2,1,0:T(8,128)S(1)}, f32[3,32,256]{2,1,0:T(8,128)S(1)}, u32[]{:S(2)}, u32[]{:S(2)}) collective-permute-start(f32[3,32,256]{2,1,0:T(8,128)S(1)} %get-tuple-element.23.own_west), channel_id=1, source_target_pairs={{8,0},{16,8},{24,16},{9,1},{17,9},{25,17},{10,2},{18,10},{26,18},{... | collective-permute-start | bytes 294920 | tf_op jit(solution)/shard_map/ppermute | solution.py:697
  21.8 0.0 copy-start
  21.8 10.5 %advance_first.1.section_in = f32[3,96,32,256]{3,2,1,0:T(8,128)S(1)} custom-call(f32[3,96,32,256]{3,2,1,0:T(8,128)S(1)} %get-tuple-element.21.field), custom_call_target="tpu_custom_call" | custom-call | flops 1000000000 | bytes 37748736 | tf_op jit(solution)/shard_map/advance_first/pallas_call | solution.py:764
  32.3 0.0 collective-permute-done.ghost_low
  32.3 0.0 collective-permute-done.1.ghost_high
  32.3 3.7 %collective-permute-done.3.got_high = f32[480,1,256]{2,1,0:T(1,128)S(1)} collective-permute-done((f32[480,1,256]{2,1,0:T(1,128)S(1)}, f32[480,1,256]{2,1,0:T(1,128)S(1)}, u32[]{:S(2)}, u32[]{:S(2)}) %collective-permute-start.3) | collective-permute-done | bytes 491552 | tf_op jit(solution)/shard_map/ppermute | solution.py:697
  36.0 0.7 collective-permute-done.2.got_low
  36.7 0.0 copy-done
  36.7 11.0 %spread_sample.1 = (f32[3,96,32,256]{3,2,1,0:T(8,128)S(1)}, f32[3,96,32,256]{3,2,1,0:T(8,128)}, f32[64,32,256]{2,1,0:T(8,128)}, bf16[64,2,256,256]{3,2,1,0:T(8,1...) custom-call(f32[3,96,32,256]{3,2,1,0:T(8,128)S(1)} %advance_first.1., ...), custom_call_target="tpu_custom_call", output_to_operand_aliasing={{0}: (0, {})} | custom-call | flops 2000000000 | bytes 37748736 | tf_op jit(solution)/shard_map/spread_sample/pallas_call | solution.py:775
  47.7 5.5 %all-to-all-start = ((f32[8,2,24,1,256]{4,3,2,1,0:T(1,128)}), f32[8,2,24,1,256]{4,3,2,1,0:T(1,128)S(1)}, u32[]{:S(2)}, u32[]{:S(2)}) async-start(f32[8,2,24,1,256]{4,3,2,1,0:T(1,128)} %get-tuple-element.38), calls=%async_computation | async-start | bytes 786432 | tf_op jit(solution)/shard_map/all_to_all | solution.py:793
  53.3 4.2 %collective-permute-start.7 = (f32[480,1,256]{2,1,0:T(1,128)S(1)}, f32[480,1,256]{2,1,0:T(1,128)S(1)}, u32[]{:S(2)}, u32[]{:S(2)}) collective-permute-start(f32[480,1,256]{2,1,0:T(1,128)S(1)} %get-tuple-element.34.own_low), channel_id=1, source_target_pairs={{0,7},{1,0},{2,1},{3,2},{4,3},{5,4},{6,5},{7,6},{8,15},{9,8},{10,9... | collective-permute-start | bytes 1474568 | tf_op jit(solution)/shard_map/ppermute | solution.py:697
  57.4 0.0 collective-permute-start.6
  57.4 1.9 %collective-permute-start.4 = (f32[3,32,256]{2,1,0:T(8,128)S(1)}, f32[3,32,256]{2,1,0:T(8,128)S(1)}, u32[]{:S(2)}, u32[]{:S(2)}) collective-permute-start(f32[3,32,256]{2,1,0:T(8,128)S(1)} %get-tuple-element.32.own_east), channel_id=1, source_target_pairs={{0,8},{8,16},{16,24},{1,9},{9,17},{17,25},{2,10},{10,18},{18,26},{... | collective-permute-start | bytes 294920 | tf_op jit(solution)/shard_map/ppermute | solution.py:697
  59.3 2.4 %collective-permute-start.5 = (f32[3,32,256]{2,1,0:T(8,128)S(1)}, f32[3,32,256]{2,1,0:T(8,128)S(1)}, u32[]{:S(2)}, u32[]{:S(2)}) collective-permute-start(f32[3,32,256]{2,1,0:T(8,128)S(1)} %get-tuple-element.33.own_west), channel_id=1, source_target_pairs={{8,0},{16,8},{24,16},{9,1},{17,9},{25,17},{10,2},{18,10},{26,18},{... | collective-permute-start | bytes 294920 | tf_op jit(solution)/shard_map/ppermute | solution.py:697
  61.8 12.6 %advance_second.1 = (f32[3,96,32,256]{3,2,1,0:T(8,128)}, f32[8,128]{1,0:T(8,128)S(1)}) custom-call(f32[3,96,32,256]{3,2,1,0:T(8,128)} %get-tuple-element.30.section_hbm, f32[3,96,32,256]{3,2,1,0:T(8,128)} %velocity.3), custom_call_target="tpu_custom_call" | custom-call | flops 1000000000 | bytes 37748736 | tf_op jit(solution)/shard_map/advance_second/pallas_call | solution.py:796
  74.3 0.0 collective-permute-done.4.after_low.ghost_low
  74.4 0.0 collective-permute-done.5.after_high.ghost_high
  74.4 0.0 all-to-all-done.parts
  74.4 0.8 share_force.1.after
  75.2 5.4 %all-to-all-start.1 = ((f32[8,24,1,256]{3,2,1,0:T(1,128)}), f32[8,24,1,256]{3,2,1,0:T(1,128)S(1)}, u32[]{:S(2)}, u32[]{:S(2)}) async-start(f32[8,24,1,256]{3,2,1,0:T(1,128)} %share_force.1.after), calls=%async_computation.1 | async-start | bytes 393216 | tf_op jit(solution)/shard_map/all_to_all | solution.py:816
  80.6 0.3 collective-permute-done.7.got_high
  80.9 0.0 collective-permute-done.6.got_low
  80.9 11.2 %spread_next.1 = f32[3,96,32,256]{3,2,1,0:T(8,128)} custom-call(f32[3,96,32,256]{3,2,1,0:T(8,128)} %get-tuple-element.31.following, f32[3,32,256]{2,1,0:T(8,128)S(1)} %copy-done, f32[3,32,256]{2,1,0:T(8,128)S(1)} %collective-permute-done.4.after_low.ghost_low, f32[3,32,256]{2,1,0:T(8,128)S(1)} %collective-permute-done.5.after_high.ghost_high, ...), custom_call_target="tpu_custom_call" | custom-call | flops 2000000000 | bytes 37748736 | tf_op jit(solution)/shard_map/spread_next/pallas_call | solution.py:818
  92.1 0.0 all-to-all-done.1
  92.1 0.7 copy.9
Async XLA Ops:
  12.9 23.2 %collective-permute-start.3 = (f32[480,1,256]{2,1,0:T(1,128)S(1)}, f32[480,1,256]{2,1,0:T(1,128)S(1)}, u32[]{:S(2)}, u32[]{:S(2)}) collective-permute-start(f32[480,1,256]{2,1,0:T(1,128)S(1)} %get-tuple-element.24.own_low), channel_id=1, source_target_pairs={{0,7},{1,0},{2,1},{3,2},{4,3},{5,4},{6,5},{7,6},{8,15},{9,8},{10,9... | collective-permute-start | bytes 1474568 | tf_op jit(solution)/shard_map/ppermute | solution.py:697
  17.5 19.2 %collective-permute-start.2 = (f32[480,1,256]{2,1,0:T(1,128)S(1)}, f32[480,1,256]{2,1,0:T(1,128)S(1)}, u32[]{:S(2)}, u32[]{:S(2)}) collective-permute-start(f32[480,1,256]{2,1,0:T(1,128)S(1)} %get-tuple-element.25.own_high), channel_id=1, source_target_pairs={{0,1},{1,2},{2,3},{3,4},{4,5},{5,6},{6,7},{7,0},{8,9},{9,10},{10,1... | collective-permute-start | bytes 1474568 | tf_op jit(solution)/shard_map/ppermute | solution.py:697
  17.5 14.8 %collective-permute-start = (f32[3,32,256]{2,1,0:T(8,128)S(1)}, f32[3,32,256]{2,1,0:T(8,128)S(1)}, u32[]{:S(2)}, u32[]{:S(2)}) collective-permute-start(f32[3,32,256]{2,1,0:T(8,128)S(1)} %get-tuple-element.22.own_east), channel_id=1, source_target_pairs={{0,8},{8,16},{16,24},{1,9},{9,17},{17,25},{2,10},{10,18},{18,26},{... | collective-permute-start | bytes 294920 | tf_op jit(solution)/shard_map/ppermute | solution.py:697
  19.4 12.9 %collective-permute-start.1 = (f32[3,32,256]{2,1,0:T(8,128)S(1)}, f32[3,32,256]{2,1,0:T(8,128)S(1)}, u32[]{:S(2)}, u32[]{:S(2)}) collective-permute-start(f32[3,32,256]{2,1,0:T(8,128)S(1)} %get-tuple-element.23.own_west), channel_id=1, source_target_pairs={{8,0},{16,8},{24,16},{9,1},{17,9},{25,17},{10,2},{18,10},{26,18},{... | collective-permute-start | bytes 294920 | tf_op jit(solution)/shard_map/ppermute | solution.py:697
  21.8 14.9 %copy-start = (f32[3,32,256]{2,1,0:T(8,128)S(1)}, f32[3,32,256]{2,1,0:T(8,128)}, u32[]{:S(2)}) copy-start(f32[3,32,256]{2,1,0:T(8,128)} %inflow.3) | copy-start | bytes 294916
  47.7 26.6 %all-to-all-start = ((f32[8,2,24,1,256]{4,3,2,1,0:T(1,128)}), f32[8,2,24,1,256]{4,3,2,1,0:T(1,128)S(1)}, u32[]{:S(2)}, u32[]{:S(2)}) async-start(f32[8,2,24,1,256]{4,3,2,1,0:T(1,128)} %get-tuple-element.38), calls=%async_computation | async-start | bytes 786432 | tf_op jit(solution)/shard_map/all_to_all | solution.py:793
  53.3 27.6 %collective-permute-start.7 = (f32[480,1,256]{2,1,0:T(1,128)S(1)}, f32[480,1,256]{2,1,0:T(1,128)S(1)}, u32[]{:S(2)}, u32[]{:S(2)}) collective-permute-start(f32[480,1,256]{2,1,0:T(1,128)S(1)} %get-tuple-element.34.own_low), channel_id=1, source_target_pairs={{0,7},{1,0},{2,1},{3,2},{4,3},{5,4},{6,5},{7,6},{8,15},{9,8},{10,9... | collective-permute-start | bytes 1474568 | tf_op jit(solution)/shard_map/ppermute | solution.py:697
  57.4 23.5 %collective-permute-start.6 = (f32[480,1,256]{2,1,0:T(1,128)S(1)}, f32[480,1,256]{2,1,0:T(1,128)S(1)}, u32[]{:S(2)}, u32[]{:S(2)}) collective-permute-start(f32[480,1,256]{2,1,0:T(1,128)S(1)} %get-tuple-element.35.own_high), channel_id=1, source_target_pairs={{0,1},{1,2},{2,3},{3,4},{4,5},{5,6},{6,7},{7,0},{8,9},{9,10},{10,1... | collective-permute-start | bytes 1474568 | tf_op jit(solution)/shard_map/ppermute | solution.py:697
  57.4 16.9 %collective-permute-start.4 = (f32[3,32,256]{2,1,0:T(8,128)S(1)}, f32[3,32,256]{2,1,0:T(8,128)S(1)}, u32[]{:S(2)}, u32[]{:S(2)}) collective-permute-start(f32[3,32,256]{2,1,0:T(8,128)S(1)} %get-tuple-element.32.own_east), channel_id=1, source_target_pairs={{0,8},{8,16},{16,24},{1,9},{9,17},{17,25},{2,10},{10,18},{18,26},{... | collective-permute-start | bytes 294920 | tf_op jit(solution)/shard_map/ppermute | solution.py:697
  59.3 15.0 %collective-permute-start.5 = (f32[3,32,256]{2,1,0:T(8,128)S(1)}, f32[3,32,256]{2,1,0:T(8,128)S(1)}, u32[]{:S(2)}, u32[]{:S(2)}) collective-permute-start(f32[3,32,256]{2,1,0:T(8,128)S(1)} %get-tuple-element.33.own_west), channel_id=1, source_target_pairs={{8,0},{16,8},{24,16},{9,1},{17,9},{25,17},{10,2},{18,10},{26,18},{... | collective-permute-start | bytes 294920 | tf_op jit(solution)/shard_map/ppermute | solution.py:697
  75.2 16.9 %all-to-all-start.1 = ((f32[8,24,1,256]{3,2,1,0:T(1,128)}), f32[8,24,1,256]{3,2,1,0:T(1,128)S(1)}, u32[]{:S(2)}, u32[]{:S(2)}) async-start(f32[8,24,1,256]{3,2,1,0:T(1,128)} %share_force.1.after), calls=%async_computation.1 | async-start | bytes 393216 | tf_op jit(solution)/shard_map/all_to_all | solution.py:816
where the time goes:
time: 94 us; the launch traced here: 92.8 us
  Pallas kernels  57.6 us (61%)
  starting transfers between devices  28.4 us (30%)
  waiting for transfers between devices  4.66 us (5%)
  between operations  1.41 us (2%)
    ppermute x8, starting transfers between devices, shifted(): return lax.ppermute(x, axis, pairs)  17.4 us
    pallas_call x1, Pallas kernels, local(): pl.pallas_call(advance_second, out_shape=(stored, array((SUB, LANES), f32...  12.6 us
    pallas_call x1, Pallas kernels, local(): pl.pallas_call(load_sample, out_shape=(held, pack, pack, edge, edge, pltp...  11.6 us
    pallas_call x1, Pallas kernels, local(): pl.pallas_call(spread_next, out_shape=stored, in_specs=[ANYWHERE] + [WHOL...  11.2 us
    pallas_call x1, Pallas kernels, local(): pl.pallas_call(spread_sample, out_shape=(held, stored, pltpu.HBM(y_shape,...  11 us
    pallas_call x1, Pallas kernels, local(): pl.pallas_call(advance_first, out_shape=held, in_specs=[WHOLE], out_specs...  10.5 us
    all_to_all x1, starting transfers between devices, local(): shares = lax.all_to_all(shares, 'gy', 0, 0)  5.54 us
    all_to_all x1, starting transfers between devices, local(): all_forces = lax.all_to_all(forces, 'gy', 0, 0)  5.44 us
  transfers between devices with their start and end apart: 10, of which 3 were waited for; matrix products, arithmetic and copies ran while one was open for 0% of the time, Pallas kernels for 38%

commit v1 on v0

--- a/solution.py
+++ b/solution.py
@@ -19,7 +19,8 @@
 SUB = 8
 PACKED = 32
 BATCH = 4
-VMEM_LIMIT = 5 * 2**20
+HEAD = 1
+VMEM_LIMIT = 6 * 2**20
 
 WHOLE = pl.BlockSpec(memory_space=pltpu.VMEM)
 SCALAR = pl.BlockSpec(memory_space=pltpu.SMEM)
@@ -98,12 +99,20 @@
 
     lax.fori_loop(0, jnp.minimum(counts[0], records), place, 0)
 
+    units = (plan.shape[0] - HEAD) // 3
+
     def flatten(k, found):
         def move(j, found):
             r = bucket[k, j]
-            plan[1 + found] = r
-            plan[1 + records + found] = hubs[r, 0] - start
-            return found + 1
+
+            def add(half, found):
+                plan[HEAD + found] = r
+                plan[HEAD + units + found] = hubs[r, 0] - start
+                plan[HEAD + 2 * units + found] = half
+                return found + 1
+
+            first = (touch[r, 0] - RAD) // LANES
+            return lax.fori_loop(first, (touch[r, 1] + RAD) // LANES + 1, add, found)
 
         return lax.fori_loop(0, held[k], move, found)
 
@@ -111,29 +120,33 @@
 
 
 def pair(plan, t):
-    records = (plan.shape[0] - 1) // 2
+    units = (plan.shape[0] - HEAD) // 3
     first = 2 * t
     second = jnp.minimum(first + 1, plan[0] - 1)
-    return [(n, plan[1 + n], plan[1 + records + n]) for n in (first, second)], second > first
+    picks = []
+    for n in (first, second):
+        record, hub, half = [plan[HEAD + k * units + n] for k in range(3)]
+        picks.append((n, record, hub, pl.ds(pl.multiple_of(half * LANES, LANES), LANES)))
+    return picks, second > first
 
 
 def sampled_rows(field, weight_y, weight_z, picks):
     cells_y = field.shape[2]
     rows = 3 * cells_y
     parts = []
-    for t, r, hub in picks:
+    for t, r, hub, cols in picks:
         planes = []
         for c in range(3):
-            plane = TAP[0] * field[c, hub]
-            plane += TAP[1] * (field[c, hub - 1] + field[c, hub + 1])
-            plane += TAP[2] * (field[c, hub - 2] + field[c, hub + 2])
+            plane = TAP[0] * field[c, hub, :, cols]
+            plane += TAP[1] * (field[c, hub - 1, :, cols] + field[c, hub + 1, :, cols])
+            plane += TAP[2] * (field[c, hub - 2, :, cols] + field[c, hub + 2, :, cols])
             planes.append(plane)
-        parts.append(split(jnp.concatenate(planes, axis=0)))
+        part = split(jnp.concatenate(planes, axis=0))
+        parts.append(jnp.concatenate([part, part], axis=1))
     out = []
-    for (t, r, hub), part in zip(picks, parts):
-        picked = jnp.dot(part, weight_z[t, 0], preferred_element_type=jnp.float32)
-        rest = jnp.dot(part[:rows], weight_z[t, 1], preferred_element_type=jnp.float32)
-        picked = picked[:rows] + (picked[rows:] + rest)
+    for (t, r, hub, cols), part in zip(picks, parts):
+        picked = jnp.dot(part, weight_z[t], preferred_element_type=jnp.float32)
+        picked = picked[:rows] + picked[rows:]
         weight = weight_y[t]
         out.append(
             [
@@ -142,6 +155,14 @@
             ]
         )
     return out
+
+
+def add_rows(pack, first_row, picks, sampled, both):
+    for (t, r, hub, cols), rows, keep in zip(picks, sampled, (None, both)):
+        for c in range(3):
+            n = first_row + 3 * r + c
+            value = rows[c] if keep is None else jnp.where(keep, rows[c], 0.0)
+            pack[n] = pack[n] + value
 
 
 def pack_edges(field, edge_west, edge_east, pack_low, pack_high):
@@ -208,7 +229,6 @@
     def clear(n, carry):
         for k in range(SUB):
             pack_low[first_row + n * SUB + k] = jnp.zeros((1, points), jnp.float32)
-            pack_high[first_row + n * SUB + k] = jnp.zeros((1, points), jnp.float32)
         return carry
 
     lax.fori_loop(0, 3 * records // SUB, clear, 0)
@@ -226,17 +246,23 @@
     make_plan(hubs, tiles, touch, counts, start, plan, bucket, held)
 
     def weigh(t, carry):
-        r = plan[1 + t]
+        units = weight_z.shape[0]
+        r, half = plan[HEAD + t], plan[HEAD + 2 * units + t]
         weight_y[t] = along_y(point_y[r], base, cells_y, total_y)
         weight_z[t] = jnp.zeros(weight_z.shape[1:], weight_z.dtype)
 
         def block(k, carry):
             rows = pl.ds(pl.multiple_of(k * PACKED, PACKED), PACKED)
-            weight_z[t, 0, rows], weight_z[t, 1, rows] = along_z(point_z[r], k * PACKED)
+            rest = pl.ds(pl.multiple_of(LANES + k * PACKED, PACKED), PACKED)
+            high, low = along_z(point_z[r], half * LANES + k * PACKED)
+            weight_z[t, rows] = high
+            weight_z[t, rest] = low
             return carry
 
-        first = (touch[r, 0] - RAD) // PACKED
-        lax.fori_loop(first, (touch[r, 1] + RAD) // PACKED + 1, block, 0)
+        blocks = LANES // PACKED
+        first = (touch[r, 0] - RAD) // PACKED - half * blocks
+        last = (touch[r, 1] + RAD) // PACKED - half * blocks
+        lax.fori_loop(jnp.maximum(first, 0), jnp.minimum(last + 1, blocks), block, 0)
         return carry
 
     lax.fori_loop(0, plan[0], weigh, 0)
@@ -250,16 +276,23 @@
         return jnp.maximum(ready, wanted)
 
     def step(t, ready):
-        picks, _ = pair(plan, t)
+        picks, both = pair(plan, t)
         ready = wait_to(ready, (picks[1][2] + RAD) // SUB + 1)
-        for (_, r, _), rows in zip(picks, sampled_rows(field, weight_y, weight_z, picks)):
-            for c in range(3):
-                pack_low[first_row + 3 * r + c] = rows[c]
-                pack_high[first_row + 3 * r + c] = rows[c]
+        rows = sampled_rows(field, weight_y, weight_z, picks)
+        add_rows(pack_low, first_row, picks, rows, both)
         return ready
 
     ready = lax.fori_loop(0, (plan[0] + 1) // 2, step, jnp.int32(0))
     wait_to(ready, chunks)
+
+    def copy_rows(t, carry):
+        rows = [first_row + t * SUB + k for k in range(SUB)]
+        values = [pack_low[n] for n in rows]
+        for n, value in zip(rows, values):
+            pack_high[n] = value
+        return carry
+
+    lax.fori_loop(0, 3 * records // SUB, copy_rows, 0)
     pack_edges(field, edge_west, edge_east, pack_low, pack_high)
 
 
@@ -310,7 +343,7 @@
     count = 3 * cells_y
     across = (((1,), (1,)), ((), ()))
     spread = []
-    for (t, r, hub), scale in zip(picks, scales):
+    for (t, r, hub, cols), scale in zip(picks, scales):
         rows = [3 * cells_x + 3 * r + c for c in range(3)]
         total = [own[n] + (low[n] + high[n]) for n in rows]
         speed = jnp.sqrt(total[0] * total[0] + total[1] * total[1] + total[2] * total[2])
@@ -318,32 +351,30 @@
         weight = weight_y[t]
         spread.append(split(jnp.concatenate([weight * (pull * x) for x in total], axis=0)))
     slabs = []
-    for (t, r, hub), part in zip(picks, spread):
-        slab = lax.dot_general(part, weight_z[t, 0], across, preferred_element_type=jnp.float32)
-        rest = lax.dot_general(
-            part[:count], weight_z[t, 1], across, preferred_element_type=jnp.float32
-        )
-        slabs.append(slab[:count] + (slab[count:] + rest))
+    for (t, r, hub, cols), part in zip(picks, spread):
+        slab = lax.dot_general(part, weight_z[t], across, preferred_element_type=jnp.float32)
+        slab = slab[:count] + slab[count:]
+        slabs.append(slab[:, :LANES] + slab[:, LANES:])
     return slabs
 
 
-def add_slab(field, slab, hub):
+def add_slab(field, slab, hub, cols):
     cells_y = field.shape[2]
     for c in range(3):
         part = slab[c * cells_y : (c + 1) * cells_y]
         terms = [tap * part for tap in TAP]
         reach = range(-RAD, RAD + 1)
-        values = [field[c, hub + d] + terms[abs(d)] for d in reach]
+        values = [field[c, hub + d, :, cols] + terms[abs(d)] for d in reach]
         for d, value in zip(reach, values):
-            field[c, hub + d] = value
+            field[c, hub + d, :, cols] = value
 
 
 def spread_pair(t, scale, field, plan, points, own, low, high):
     picks, both = pair(plan, t)
     scales = [scale, jnp.where(both, scale, 0.0)]
     slabs = slabs_of(*points, own, low, high, field.shape[1:], scales, picks)
-    for (_, _, hub), slab in zip(picks, slabs):
-        add_slab(field, slab, hub)
+    for (_, _, hub, cols), slab in zip(picks, slabs):
+        add_slab(field, slab, hub, cols)
 
 
 def spread_sample(
@@ -393,28 +424,31 @@
     copy.start()
     pack_edges(section, edge_west, edge_east, pack_low, pack_high)
 
-    def clear(r, carry):
-        rows = [own_low[first_row + 3 * r + c] for c in range(3)]
-        zero = jnp.zeros_like(rows[0])
+    def clear(n, carry):
+        for k in range(SUB):
+            pack_low[first_row + n * SUB + k] = jnp.zeros_like(own_low[0])
+        return carry
+
+    lax.fori_loop(0, 3 * records // SUB, clear, 0)
+
+    def sample_step(t, carry):
+        picks, both = pair(plan, t)
+        rows = sampled_rows(section, weight_y, weight_z, picks)
+        add_rows(pack_low, first_row, picks, rows, both)
+        return carry
+
+    lax.fori_loop(0, (plan[0] + 1) // 2, sample_step, 0)
+
+    def copy_rows(r, carry):
+        old = [own_low[first_row + 3 * r + c] for c in range(3)]
+        new = [pack_low[first_row + 3 * r + c] for c in range(3)]
         for c in range(3):
-            pack_low[first_row + 3 * r + c] = zero
-            pack_high[first_row + 3 * r + c] = zero
-            share_out[r // share, 0, 3 * (r % share) + c] = rows[c]
-            share_out[r // share, 1, 3 * (r % share) + c] = zero
-        return carry
-
-    lax.fori_loop(0, records, clear, 0)
-
-    def sample_step(t, carry):
-        picks, _ = pair(plan, t)
-        for (_, r, _), rows in zip(picks, sampled_rows(section, weight_y, weight_z, picks)):
-            for c in range(3):
-                pack_low[first_row + 3 * r + c] = rows[c]
-                pack_high[first_row + 3 * r + c] = rows[c]
-                share_out[r // share, 1, 3 * (r % share) + c] = rows[c]
-        return carry
-
-    lax.fori_loop(0, (plan[0] + 1) // 2, sample_step, 0)
+            pack_high[first_row + 3 * r + c] = new[c]
+            share_out[r // share, 0, 3 * (r % share) + c] = old[c]
+            share_out[r // share, 1, 3 * (r % share) + c] = new[c]
+        return carry
+
+    lax.fori_loop(0, records, copy_rows, 0)
     lax.fori_loop(0, plan[0], wait_store, 0)
     copy.wait()
 
@@ -549,7 +583,7 @@
 
 def along_depth(i, field, shifts, slot):
     depth = shifts.shape[1]
-    x = jnp.concatenate([field[c, i + k] for k in range(2) for c in range(3)], axis=0)
+    x = jnp.concatenate([field[c, i + k] for k in range(BATCH) for c in range(3)], axis=0)
     high = x.astype(jnp.bfloat16)
     low = (x - high.astype(jnp.float32)).astype(jnp.bfloat16)
     slot[0] = jnp.dot(
@@ -612,14 +646,14 @@
             values = []
 
 
-def advance_four(i, factor, field, shifts, slots, target, finish):
-    last = field.shape[1] - 2
-    for n in range(2):
-        now, later = slots[n], slots[1 - n]
-        along_depth(jnp.minimum(i + 2, last), field, shifts, later)
-        for k in range(2):
+def advance_chunk(i, factor, field, shifts, slots, target, finish):
+    last = field.shape[1] - BATCH
+    for n in range(SUB // BATCH):
+        now, later = slots[n % 2], slots[1 - n % 2]
+        along_depth(jnp.minimum(i + BATCH, last), field, shifts, later)
+        for k in range(BATCH):
             advance(i, k, factor, field, now, target, finish)
-        i = i + 2
+        i = i + BATCH
 
 
 def advance_first(field, section, shifts, slot_a, slot_b):
@@ -627,13 +661,13 @@
     along_depth(0, field, shifts, slot_a)
 
     def step(t, carry):
-        advance_four(
-            4 * t, 1.0, field, shifts, (slot_a, slot_b), section,
+        advance_chunk(
+            SUB * t, 1.0, field, shifts, (slot_a, slot_b), section,
             lambda c, i, rows, cols, value: value,
         )
         return carry
 
-    lax.fori_loop(0, field.shape[1] // 4, step, 0)
+    lax.fori_loop(0, field.shape[1] // SUB, step, 0)
 
 
 def advance_second(
@@ -677,10 +711,7 @@
             chunk_in(k + 1).wait()
 
         chunk_old(k).wait()
-        for n in range(0, SUB, 4):
-            advance_four(
-                k * SUB + n, 0.5, section, shifts, (slot_a, slot_b), result, finish
-            )
+        advance_chunk(SUB * k, 0.5, section, shifts, (slot_a, slot_b), result, finish)
         chunk_out(k).start()
         return carry
 
@@ -722,11 +753,12 @@
     pack = array((3 * cells_x + 3 * records, 1, points), f32)
     edge = array((3, cells_y, depth), f32)
     per_record = (records, 1, points)
-    y_shape, z_shape = (records, cells_y, points), (records, 2, depth, points)
+    units = records * (depth // LANES)
+    y_shape, z_shape = (units, cells_y, points), (units, 2 * LANES, points)
     y_bytes, z_bytes = 4 * math.prod(y_shape), 2 * math.prod(z_shape)
     products = [pltpu.VMEM((3 * depth, depth), jnp.bfloat16)]
-    products += [pltpu.VMEM((2, 6 * cells_y, depth), f32)] * 2
-    record_sems = pltpu.SemaphoreType.DMA((records,))
+    products += [pltpu.VMEM((2, 3 * BATCH * cells_y, depth), f32)] * 2
+    unit_sems = pltpu.SemaphoreType.DMA((units,))
     chunk_sems = pltpu.SemaphoreType.DMA((chunks,))
 
     field, *own_a, weight_y, weight_z, strength, plan = pl.pallas_call(
@@ -735,7 +767,7 @@
             held, pack, pack, edge, edge,
             pltpu.VMEM(y_shape, f32), pltpu.VMEM(z_shape, jnp.bfloat16),
             array(per_record, f32),
-            array((1 + 2 * records,), i32),
+            array((HEAD + 3 * units,), i32),
         ),
         in_specs=[ANYWHERE] * 4 + [SCALAR],
         out_specs=(WHOLE,) * 8 + (SCALAR,),
@@ -782,7 +814,7 @@
         in_specs=[WHOLE] * 10 + [SCALAR] + [WHOLE] * 3,
         out_specs=(WHOLE,) + (ANYWHERE,) * 3 + (WHOLE,) * 5,
         input_output_aliases={0: 0},
-        scratch_shapes=[pltpu.SemaphoreType.DMA, record_sems, record_sems],
+        scratch_shapes=[pltpu.SemaphoreType.DMA, unit_sems, unit_sems],
         compiler_params=params(),
         cost_estimate=cost(2 * 10**9, 4 * size),
         name="spread_sample",
@@ -824,7 +856,7 @@
             pltpu.VMEM(whole, f32),
             pltpu.VMEM(y_shape, f32),
             pltpu.VMEM(z_shape, jnp.bfloat16),
-            chunk_sems, chunk_sems, record_sems, record_sems,
+            chunk_sems, chunk_sems, unit_sems, unit_sems,
         ],
         compiler_params=params(VMEM_LIMIT + size + y_bytes + z_bytes),
         cost_estimate=cost(2 * 10**9, 4 * size),

time: 94 us -> 93.2 us (level); the launches traced: 92.8 us -> 94.4 us
  starting transfers between devices: 28.4 us -> 43.2 us
  Pallas kernels: 57.6 us -> 49 us
  waiting for transfers between devices: 4.66 us -> 0.03 us
    ppermute x8, starting transfers between devices: 17.4 us -> 31.8 us  [shifted(): return lax.ppermute(x, axis, pairs)]
    pallas_call x1, Pallas kernels: 11.6 us -> 5.93 us  [local(): pl.pallas_call(load_sample, out_shape=(held, pack, pack, edge, edge, pltp...]
    ppermute x8, waiting for transfers between devices: 4.65 us -> 0.02 us  [shifted(): return lax.ppermute(x, axis, pairs)]
    pallas_call x1, Pallas kernels: 11 us -> 8.48 us  [local(): pl.pallas_call(spread_sample, out_shape=(held, stored, pltpu.HBM(y_shape,...]
  transfers between devices with their start and end apart: 10 -> 10, of which waited for: 3 -> 0; matrix products, arithmetic and copies ran while one was open for 0% -> 0% of each run, Pallas kernels for 38% -> 37%
where the time goes in v1:
time: 93.2 us; the launch traced here: 94.4 us
  Pallas kernels  49 us (53%)
  starting transfers between devices  43.2 us (46%)
  between operations  1.44 us (2%)
    ppermute x8, starting transfers between devices, shifted(): return lax.ppermute(x, axis, pairs)  31.8 us
    pallas_call x1, Pallas kernels, local(): pl.pallas_call(advance_second, out_shape=(stored, array((SUB, LANES), f32...  12.7 us
    pallas_call x1, Pallas kernels, local(): pl.pallas_call(spread_next, out_shape=stored, in_specs=[ANYWHERE] + [WHOL...  11.4 us
    pallas_call x1, Pallas kernels, local(): pl.pallas_call(advance_first, out_shape=held, in_specs=[WHOLE], out_specs...  9.7 us
    pallas_call x1, Pallas kernels, local(): pl.pallas_call(spread_sample, out_shape=(held, stored, pltpu.HBM(y_shape,...  8.48 us
    pallas_call x1, Pallas kernels, local(): pl.pallas_call(load_sample, out_shape=(held, pack, pack, edge, edge, pltp...  5.93 us
    all_to_all x1, starting transfers between devices, local(): shares = lax.all_to_all(shares, 'gy', 0, 0)  5.73 us
    all_to_all x1, starting transfers between devices, local(): all_forces = lax.all_to_all(forces, 'gy', 0, 0)  5.72 us
  transfers between devices with their start and end apart: 10, of which 0 were waited for; matrix products, arithmetic and copies ran while one was open for 0% of the time, Pallas kernels for 37%

profile of v1, /device:TPU:1, one launch (start us, length us, event | category | flops | bytes accessed | tf_op | source)
XLA Modules:
  0.0 94.4 jit_solution(12156573902674202930)
XLA Ops:
  1.3 5.9 %load_sample.1 = (f32[3,96,32,256]{3,2,1,0:T(8,128)S(1)}, f32[480,1,256]{2,1,0:T(1,128)S(1)}, f32[480,1,256]{2,1,0:T(1,128)S(1)}, f32[3,32,256]{2,1,0:T(8,128)S(...) custom-call(f32[3,96,32,256]{3,2,1,0:T(8,128)} %velocity.3, ...), custom_call_target="tpu_custom_call" | custom-call | flops 2000000000 | bytes 37748736 | tf_op jit(solution)/shard_map/load_sample/pallas_call | solution.py:764
  7.2 5.1 %collective-permute-start.3 = (f32[480,1,256]{2,1,0:T(1,128)S(1)}, f32[480,1,256]{2,1,0:T(1,128)S(1)}, u32[]{:S(2)}, u32[]{:S(2)}) collective-permute-start(f32[480,1,256]{2,1,0:T(1,128)S(1)} %get-tuple-element.24.own_low), channel_id=1, source_target_pairs={{0,7},{1,0},{2,1},{3,2},{4,3},{5,4},{6,5},{7,6},{8,15},{9,8},{10,9... | collective-permute-start | bytes 1474568 | tf_op jit(solution)/shard_map/ppermute | solution.py:728
  12.3 0.0 collective-permute-start.2
  12.3 10.4 %collective-permute-start = (f32[3,32,256]{2,1,0:T(8,128)S(1)}, f32[3,32,256]{2,1,0:T(8,128)S(1)}, u32[]{:S(2)}, u32[]{:S(2)}) collective-permute-start(f32[3,32,256]{2,1,0:T(8,128)S(1)} %get-tuple-element.22.own_east), channel_id=1, source_target_pairs={{0,8},{8,16},{16,24},{1,9},{9,17},{17,25},{2,10},{10,18},{18,26},{... | collective-permute-start | bytes 294920 | tf_op jit(solution)/shard_map/ppermute | solution.py:728
  22.7 1.9 %collective-permute-start.1 = (f32[3,32,256]{2,1,0:T(8,128)S(1)}, f32[3,32,256]{2,1,0:T(8,128)S(1)}, u32[]{:S(2)}, u32[]{:S(2)}) collective-permute-start(f32[3,32,256]{2,1,0:T(8,128)S(1)} %get-tuple-element.23.own_west), channel_id=1, source_target_pairs={{8,0},{16,8},{24,16},{9,1},{17,9},{25,17},{10,2},{18,10},{26,18},{... | collective-permute-start | bytes 294920 | tf_op jit(solution)/shard_map/ppermute | solution.py:728
  24.6 0.0 copy-start
  24.6 9.7 %advance_first.1.section_in = f32[3,96,32,256]{3,2,1,0:T(8,128)S(1)} custom-call(f32[3,96,32,256]{3,2,1,0:T(8,128)S(1)} %get-tuple-element.21.field), custom_call_target="tpu_custom_call" | custom-call | flops 1000000000 | bytes 37748736 | tf_op jit(solution)/shard_map/advance_first/pallas_call | solution.py:796
  34.4 0.0 collective-permute-done.ghost_low
  34.4 0.0 collective-permute-done.1.ghost_high
  34.4 0.0 collective-permute-done.3.got_high
  34.4 0.0 collective-permute-done.2.got_low
  34.4 0.0 copy-done
  34.4 8.5 %spread_sample.1 = (f32[3,96,32,256]{3,2,1,0:T(8,128)S(1)}, f32[3,96,32,256]{3,2,1,0:T(8,128)}, f32[128,32,256]{2,1,0:T(8,128)}, bf16[128,256,256]{2,1,0:T(8,128...) custom-call(f32[3,96,32,256]{3,2,1,0:T(8,128)S(1)} %advance_first.1., ...), custom_call_target="tpu_custom_call", output_to_operand_aliasing={{0}: (0, {})} | custom-call | flops 2000000000 | bytes 37748736 | tf_op jit(solution)/shard_map/spread_sample/pallas_call | solution.py:807
  42.9 5.7 %all-to-all-start = ((f32[8,2,24,1,256]{4,3,2,1,0:T(1,128)}), f32[8,2,24,1,256]{4,3,2,1,0:T(1,128)S(1)}, u32[]{:S(2)}, u32[]{:S(2)}) async-start(f32[8,2,24,1,256]{4,3,2,1,0:T(1,128)} %get-tuple-element.38), calls=%async_computation | async-start | bytes 786432 | tf_op jit(solution)/shard_map/all_to_all | solution.py:825
  48.6 4.2 %collective-permute-start.7 = (f32[480,1,256]{2,1,0:T(1,128)S(1)}, f32[480,1,256]{2,1,0:T(1,128)S(1)}, u32[]{:S(2)}, u32[]{:S(2)}) collective-permute-start(f32[480,1,256]{2,1,0:T(1,128)S(1)} %get-tuple-element.34.own_low), channel_id=1, source_target_pairs={{0,7},{1,0},{2,1},{3,2},{4,3},{5,4},{6,5},{7,6},{8,15},{9,8},{10,9... | collective-permute-start | bytes 1474568 | tf_op jit(solution)/shard_map/ppermute | solution.py:728
  52.8 0.0 collective-permute-start.6
  52.8 8.3 %collective-permute-start.4 = (f32[3,32,256]{2,1,0:T(8,128)S(1)}, f32[3,32,256]{2,1,0:T(8,128)S(1)}, u32[]{:S(2)}, u32[]{:S(2)}) collective-permute-start(f32[3,32,256]{2,1,0:T(8,128)S(1)} %get-tuple-element.32.own_east), channel_id=1, source_target_pairs={{0,8},{8,16},{16,24},{1,9},{9,17},{17,25},{2,10},{10,18},{18,26},{... | collective-permute-start | bytes 294920 | tf_op jit(solution)/shard_map/ppermute | solution.py:728
  61.1 1.9 %collective-permute-start.5 = (f32[3,32,256]{2,1,0:T(8,128)S(1)}, f32[3,32,256]{2,1,0:T(8,128)S(1)}, u32[]{:S(2)}, u32[]{:S(2)}) collective-permute-start(f32[3,32,256]{2,1,0:T(8,128)S(1)} %get-tuple-element.33.own_west), channel_id=1, source_target_pairs={{8,0},{16,8},{24,16},{9,1},{17,9},{25,17},{10,2},{18,10},{26,18},{... | collective-permute-start | bytes 294920 | tf_op jit(solution)/shard_map/ppermute | solution.py:728
  63.0 12.7 %advance_second.1 = (f32[3,96,32,256]{3,2,1,0:T(8,128)}, f32[8,128]{1,0:T(8,128)S(1)}) custom-call(f32[3,96,32,256]{3,2,1,0:T(8,128)} %get-tuple-element.30.section_hbm, f32[3,96,32,256]{3,2,1,0:T(8,128)} %velocity.3), custom_call_target="tpu_custom_call" | custom-call | flops 1000000000 | bytes 37748736 | tf_op jit(solution)/shard_map/advance_second/pallas_call | solution.py:828
  75.7 0.0 collective-permute-done.4.after_low.ghost_low
  75.7 0.0 collective-permute-done.5.after_high.ghost_high
  75.8 0.0 all-to-all-done.parts
  75.8 0.8 share_force.1.after
  76.6 5.7 %all-to-all-start.1 = ((f32[8,24,1,256]{3,2,1,0:T(1,128)}), f32[8,24,1,256]{3,2,1,0:T(1,128)S(1)}, u32[]{:S(2)}, u32[]{:S(2)}) async-start(f32[8,24,1,256]{3,2,1,0:T(1,128)} %share_force.1.after), calls=%async_computation.1 | async-start | bytes 393216 | tf_op jit(solution)/shard_map/all_to_all | solution.py:848
  82.3 0.0 collective-permute-done.7.got_high
  82.3 0.0 collective-permute-done.6.got_low
  82.3 11.4 %spread_next.1 = f32[3,96,32,256]{3,2,1,0:T(8,128)} custom-call(f32[3,96,32,256]{3,2,1,0:T(8,128)} %get-tuple-element.31.following, f32[3,32,256]{2,1,0:T(8,128)S(1)} %copy-done, f32[3,32,256]{2,1,0:T(8,128)S(1)} %collective-permute-done.4.after_low.ghost_low, f32[3,32,256]{2,1,0:T(8,128)S(1)} %collective-permute-done.5.after_high.ghost_high, ...), custom_call_target="tpu_custom_call" | custom-call | flops 2000000000 | bytes 37748736 | tf_op jit(solution)/shard_map/spread_next/pallas_call | solution.py:850
  93.7 0.0 all-to-all-done.1
  93.7 0.7 copy.9
Async XLA Ops:
  7.2 27.2 %collective-permute-start.3 = (f32[480,1,256]{2,1,0:T(1,128)S(1)}, f32[480,1,256]{2,1,0:T(1,128)S(1)}, u32[]{:S(2)}, u32[]{:S(2)}) collective-permute-start(f32[480,1,256]{2,1,0:T(1,128)S(1)} %get-tuple-element.24.own_low), channel_id=1, source_target_pairs={{0,7},{1,0},{2,1},{3,2},{4,3},{5,4},{6,5},{7,6},{8,15},{9,8},{10,9... | collective-permute-start | bytes 1474568 | tf_op jit(solution)/shard_map/ppermute | solution.py:728
  12.3 22.1 %collective-permute-start.2 = (f32[480,1,256]{2,1,0:T(1,128)S(1)}, f32[480,1,256]{2,1,0:T(1,128)S(1)}, u32[]{:S(2)}, u32[]{:S(2)}) collective-permute-start(f32[480,1,256]{2,1,0:T(1,128)S(1)} %get-tuple-element.25.own_high), channel_id=1, source_target_pairs={{0,1},{1,2},{2,3},{3,4},{4,5},{5,6},{6,7},{7,0},{8,9},{9,10},{10,1... | collective-permute-start | bytes 1474568 | tf_op jit(solution)/shard_map/ppermute | solution.py:728
  12.3 22.0 %collective-permute-start = (f32[3,32,256]{2,1,0:T(8,128)S(1)}, f32[3,32,256]{2,1,0:T(8,128)S(1)}, u32[]{:S(2)}, u32[]{:S(2)}) collective-permute-start(f32[3,32,256]{2,1,0:T(8,128)S(1)} %get-tuple-element.22.own_east), channel_id=1, source_target_pairs={{0,8},{8,16},{16,24},{1,9},{9,17},{17,25},{2,10},{10,18},{18,26},{... | collective-permute-start | bytes 294920 | tf_op jit(solution)/shard_map/ppermute | solution.py:728
  22.7 11.7 %collective-permute-start.1 = (f32[3,32,256]{2,1,0:T(8,128)S(1)}, f32[3,32,256]{2,1,0:T(8,128)S(1)}, u32[]{:S(2)}, u32[]{:S(2)}) collective-permute-start(f32[3,32,256]{2,1,0:T(8,128)S(1)} %get-tuple-element.23.own_west), channel_id=1, source_target_pairs={{8,0},{16,8},{24,16},{9,1},{17,9},{25,17},{10,2},{18,10},{26,18},{... | collective-permute-start | bytes 294920 | tf_op jit(solution)/shard_map/ppermute | solution.py:728
  24.6 9.8 %copy-start = (f32[3,32,256]{2,1,0:T(8,128)S(1)}, f32[3,32,256]{2,1,0:T(8,128)}, u32[]{:S(2)}) copy-start(f32[3,32,256]{2,1,0:T(8,128)} %inflow.3) | copy-start | bytes 294916
  42.9 32.9 %all-to-all-start = ((f32[8,2,24,1,256]{4,3,2,1,0:T(1,128)}), f32[8,2,24,1,256]{4,3,2,1,0:T(1,128)S(1)}, u32[]{:S(2)}, u32[]{:S(2)}) async-start(f32[8,2,24,1,256]{4,3,2,1,0:T(1,128)} %get-tuple-element.38), calls=%async_computation | async-start | bytes 786432 | tf_op jit(solution)/shard_map/all_to_all | solution.py:825
  48.6 33.7 %collective-permute-start.7 = (f32[480,1,256]{2,1,0:T(1,128)S(1)}, f32[480,1,256]{2,1,0:T(1,128)S(1)}, u32[]{:S(2)}, u32[]{:S(2)}) collective-permute-start(f32[480,1,256]{2,1,0:T(1,128)S(1)} %get-tuple-element.34.own_low), channel_id=1, source_target_pairs={{0,7},{1,0},{2,1},{3,2},{4,3},{5,4},{6,5},{7,6},{8,15},{9,8},{10,9... | collective-permute-start | bytes 1474568 | tf_op jit(solution)/shard_map/ppermute | solution.py:728
  52.8 29.5 %collective-permute-start.6 = (f32[480,1,256]{2,1,0:T(1,128)S(1)}, f32[480,1,256]{2,1,0:T(1,128)S(1)}, u32[]{:S(2)}, u32[]{:S(2)}) collective-permute-start(f32[480,1,256]{2,1,0:T(1,128)S(1)} %get-tuple-element.35.own_high), channel_id=1, source_target_pairs={{0,1},{1,2},{2,3},{3,4},{4,5},{5,6},{6,7},{7,0},{8,9},{9,10},{10,1... | collective-permute-start | bytes 1474568 | tf_op jit(solution)/shard_map/ppermute | solution.py:728
  52.8 22.9 %collective-permute-start.4 = (f32[3,32,256]{2,1,0:T(8,128)S(1)}, f32[3,32,256]{2,1,0:T(8,128)S(1)}, u32[]{:S(2)}, u32[]{:S(2)}) collective-permute-start(f32[3,32,256]{2,1,0:T(8,128)S(1)} %get-tuple-element.32.own_east), channel_id=1, source_target_pairs={{0,8},{8,16},{16,24},{1,9},{9,17},{17,25},{2,10},{10,18},{18,26},{... | collective-permute-start | bytes 294920 | tf_op jit(solution)/shard_map/ppermute | solution.py:728
  61.1 14.7 %collective-permute-start.5 = (f32[3,32,256]{2,1,0:T(8,128)S(1)}, f32[3,32,256]{2,1,0:T(8,128)S(1)}, u32[]{:S(2)}, u32[]{:S(2)}) collective-permute-start(f32[3,32,256]{2,1,0:T(8,128)S(1)} %get-tuple-element.33.own_west), channel_id=1, source_target_pairs={{8,0},{16,8},{24,16},{9,1},{17,9},{25,17},{10,2},{18,10},{26,18},{... | collective-permute-start | bytes 294920 | tf_op jit(solution)/shard_map/ppermute | solution.py:728
  76.6 17.1 %all-to-all-start.1 = ((f32[8,24,1,256]{3,2,1,0:T(1,128)}), f32[8,24,1,256]{3,2,1,0:T(1,128)S(1)}, u32[]{:S(2)}, u32[]{:S(2)}) async-start(f32[8,24,1,256]{3,2,1,0:T(1,128)} %share_force.1.after), calls=%async_computation.1 | async-start | bytes 393216 | tf_op jit(solution)/shard_map/all_to_all | solution.py:848

commit v2 on v1

--- a/solution.py
+++ b/solution.py
@@ -17,7 +17,7 @@
 LOW = [float(jnp.bfloat16(tap - high)) for tap, high in zip(TAP, HIGH)]
 LANES = 128
 SUB = 8
-PACKED = 32
+GROUP = 4
 BATCH = 4
 HEAD = 1
 VMEM_LIMIT = 6 * 2**20
@@ -51,9 +51,9 @@
 
 def along_z(point_z, start):
     points = point_z.shape[-1]
-    row = lax.broadcasted_iota(jnp.int32, (PACKED, points), 0).astype(jnp.bfloat16)
+    row = lax.broadcasted_iota(jnp.int32, (LANES, points), 0).astype(jnp.bfloat16)
     place = (point_z - start).astype(jnp.float32)
-    place = jnp.broadcast_to(place, (PACKED, points)).astype(jnp.bfloat16)
+    place = jnp.broadcast_to(place, (LANES, points)).astype(jnp.bfloat16)
     dist = jnp.abs(row - place)
     near = [dist == float(d) for d in range(RAD + 1)]
     out = []
@@ -119,15 +119,20 @@
     plan[0] = lax.fori_loop(0, chunks, flatten, jnp.int32(0))
 
 
-def pair(plan, t):
+def group(plan, t):
     units = (plan.shape[0] - HEAD) // 3
-    first = 2 * t
-    second = jnp.minimum(first + 1, plan[0] - 1)
-    picks = []
-    for n in (first, second):
+    picks, keeps = [], []
+    for k in range(GROUP):
+        wanted = GROUP * t + k
+        n = jnp.minimum(wanted, plan[0] - 1)
         record, hub, half = [plan[HEAD + k * units + n] for k in range(3)]
         picks.append((n, record, hub, pl.ds(pl.multiple_of(half * LANES, LANES), LANES)))
-    return picks, second > first
+        keeps.append(wanted == n)
+    return picks, keeps
+
+
+def groups_of(plan):
+    return (plan[0] + GROUP - 1) // GROUP
 
 
 def sampled_rows(field, weight_y, weight_z, picks):
@@ -157,12 +162,11 @@
     return out
 
 
-def add_rows(pack, first_row, picks, sampled, both):
-    for (t, r, hub, cols), rows, keep in zip(picks, sampled, (None, both)):
+def add_rows(pack, first_row, picks, sampled, keeps):
+    for (t, r, hub, cols), rows, keep in zip(picks, sampled, keeps):
         for c in range(3):
             n = first_row + 3 * r + c
-            value = rows[c] if keep is None else jnp.where(keep, rows[c], 0.0)
-            pack[n] = pack[n] + value
+            pack[n] = pack[n] + jnp.where(keep, rows[c], 0.0)
 
 
 def pack_edges(field, edge_west, edge_east, pack_low, pack_high):
@@ -186,8 +190,8 @@
 
 def load_sample(
     velocity, positions, tiles_hbm, coefs_hbm, counts,
-    field, pack_low, pack_high, edge_west, edge_east, weight_y, weight_z, strength, plan,
-    point_y, point_z, hubs, tiles, places, coefs, flags, touch, bucket, held, small_sems, touch_sem, sems,
+    field, pack_low, pack_high, edge_west, edge_east, weight_y, weight_z, strength, point_y, plan,
+    point_z, hubs, tiles, places, coefs, flags, touch, bucket, held, small_sems, touch_sem, sems,
 ):
     cells_x, cells_y, depth = field.shape[1:]
     records, points = coefs.shape
@@ -247,25 +251,19 @@
 
     def weigh(t, carry):
         units = weight_z.shape[0]
-        r, half = plan[HEAD + t], plan[HEAD + 2 * units + t]
-        weight_y[t] = along_y(point_y[r], base, cells_y, total_y)
-        weight_z[t] = jnp.zeros(weight_z.shape[1:], weight_z.dtype)
-
-        def block(k, carry):
-            rows = pl.ds(pl.multiple_of(k * PACKED, PACKED), PACKED)
-            rest = pl.ds(pl.multiple_of(LANES + k * PACKED, PACKED), PACKED)
-            high, low = along_z(point_z[r], half * LANES + k * PACKED)
-            weight_z[t, rows] = high
-            weight_z[t, rest] = low
-            return carry
-
-        blocks = LANES // PACKED
-        first = (touch[r, 0] - RAD) // PACKED - half * blocks
-        last = (touch[r, 1] + RAD) // PACKED - half * blocks
-        lax.fori_loop(jnp.maximum(first, 0), jnp.minimum(last + 1, blocks), block, 0)
-        return carry
-
-    lax.fori_loop(0, plan[0], weigh, 0)
+        made = []
+        for k in range(2):
+            n = jnp.minimum(2 * t + k, plan[0] - 1)
+            r, half = plan[HEAD + n], plan[HEAD + 2 * units + n]
+            high, low = along_z(point_z[r], half * LANES)
+            made.append((n, along_y(point_y[r], base, cells_y, total_y), high, low))
+        for n, across, high, low in made:
+            weight_y[n] = across
+            weight_z[n, 0:LANES] = high
+            weight_z[n, LANES:] = low
+        return carry
+
+    lax.fori_loop(0, (plan[0] + 1) // 2, weigh, 0)
 
     def wait_to(ready, wanted):
         def step(k, carry):
@@ -276,13 +274,13 @@
         return jnp.maximum(ready, wanted)
 
     def step(t, ready):
-        picks, both = pair(plan, t)
-        ready = wait_to(ready, (picks[1][2] + RAD) // SUB + 1)
+        picks, keeps = group(plan, t)
+        ready = wait_to(ready, (picks[-1][2] + RAD) // SUB + 1)
         rows = sampled_rows(field, weight_y, weight_z, picks)
-        add_rows(pack_low, first_row, picks, rows, both)
+        add_rows(pack_low, first_row, picks, rows, keeps)
         return ready
 
-    ready = lax.fori_loop(0, (plan[0] + 1) // 2, step, jnp.int32(0))
+    ready = lax.fori_loop(0, groups_of(plan), step, jnp.int32(0))
     wait_to(ready, chunks)
 
     def copy_rows(t, carry):
@@ -338,7 +336,7 @@
             target[c, i, rows, :] = value
 
 
-def slabs_of(weight_y, weight_z, strength, own, low, high, cells, scales, picks):
+def slabs_of(weight_of, weight_z, strength, own, low, high, cells, scales, picks):
     cells_x, cells_y, depth = cells
     count = 3 * cells_y
     across = (((1,), (1,)), ((), ()))
@@ -348,7 +346,7 @@
         total = [own[n] + (low[n] + high[n]) for n in rows]
         speed = jnp.sqrt(total[0] * total[0] + total[1] * total[1] + total[2] * total[2])
         pull = strength[r] * (-scale) * speed
-        weight = weight_y[t]
+        weight = weight_of(t, r)
         spread.append(split(jnp.concatenate([weight * (pull * x) for x in total], axis=0)))
     slabs = []
     for (t, r, hub, cols), part in zip(picks, spread):
@@ -369,9 +367,9 @@
             field[c, hub + d, :, cols] = value
 
 
-def spread_pair(t, scale, field, plan, points, own, low, high):
-    picks, both = pair(plan, t)
-    scales = [scale, jnp.where(both, scale, 0.0)]
+def spread_group(t, scale, field, plan, points, own, low, high):
+    picks, keeps = group(plan, t)
+    scales = [jnp.where(keep, scale, 0.0) for keep in keeps]
     slabs = slabs_of(*points, own, low, high, field.shape[1:], scales, picks)
     for (_, _, hub, cols), slab in zip(picks, slabs):
         add_slab(field, slab, hub, cols)
@@ -380,28 +378,23 @@
 def spread_sample(
     section_in, inflow, ghost_low, ghost_high, own_low, own_high, own_west, own_east, got_low, got_high,
     plan, weight_y, weight_z, strength,
-    section, section_out, stored_y, stored_z, pack_low, pack_high, edge_west, edge_east,
-    share_out, sem, sem_y, sem_z,
+    section, section_out, stored_z, pack_low, pack_high, edge_west, edge_east,
+    share_out, sem, sem_z,
 ):
     cells_x = section.shape[1]
     records = strength.shape[0]
     share = share_out.shape[2] // 3
     first_row = 3 * cells_x
 
-    def copies(t):
-        return (
-            pltpu.make_async_copy(weight_y.at[t], stored_y.at[t], sem_y.at[t]),
-            pltpu.make_async_copy(weight_z.at[t], stored_z.at[t], sem_z.at[t]),
-        )
+    def store(t):
+        return pltpu.make_async_copy(weight_z.at[t], stored_z.at[t], sem_z.at[t])
 
     def start_store(t, carry):
-        for copy in copies(t):
-            copy.start()
+        store(t).start()
         return carry
 
     def wait_store(t, carry):
-        for copy in copies(t):
-            copy.wait()
+        store(t).wait()
         return carry
 
     lax.fori_loop(0, plan[0], start_store, 0)
@@ -415,11 +408,11 @@
     lax.fori_loop(0, cells_x // SUB, fix_step, 0)
 
     def spread_step(t, carry):
-        points = (weight_y, weight_z, strength)
-        spread_pair(t, TIME_STEP, section, plan, points, own_low, got_low, got_high)
-        return carry
-
-    lax.fori_loop(0, (plan[0] + 1) // 2, spread_step, 0)
+        points = (lambda n, r: weight_y[n], weight_z, strength)
+        spread_group(t, TIME_STEP, section, plan, points, own_low, got_low, got_high)
+        return carry
+
+    lax.fori_loop(0, groups_of(plan), spread_step, 0)
     copy = pltpu.make_async_copy(section, section_out, sem)
     copy.start()
     pack_edges(section, edge_west, edge_east, pack_low, pack_high)
@@ -432,12 +425,12 @@
     lax.fori_loop(0, 3 * records // SUB, clear, 0)
 
     def sample_step(t, carry):
-        picks, both = pair(plan, t)
+        picks, keeps = group(plan, t)
         rows = sampled_rows(section, weight_y, weight_z, picks)
-        add_rows(pack_low, first_row, picks, rows, both)
-        return carry
-
-    lax.fori_loop(0, (plan[0] + 1) // 2, sample_step, 0)
+        add_rows(pack_low, first_row, picks, rows, keeps)
+        return carry
+
+    lax.fori_loop(0, groups_of(plan), sample_step, 0)
 
     def copy_rows(r, carry):
         old = [own_low[first_row + 3 * r + c] for c in range(3)]
@@ -482,8 +475,8 @@
 
 def spread_next(
     following, inflow, ghost_low, ghost_high, own_low, own_high, own_west, own_east, got_low, got_high,
-    plan, stored_y, stored_z, strength, after,
-    result, field, weight_y, weight_z, in_sems, out_sems, sem_y, sem_z,
+    plan, point_y, stored_z, strength, after,
+    result, field, weight_z, in_sems, out_sems, sem_z,
 ):
     chunks = field.shape[1] // SUB
     factor = 0.5
@@ -523,15 +516,16 @@
         return jnp.maximum(sent, done)
 
     def weights(t):
-        return (
-            pltpu.make_async_copy(stored_y.at[t], weight_y.at[t], sem_y.at[t]),
-            pltpu.make_async_copy(stored_z.at[t], weight_z.at[t], sem_z.at[t]),
-        )
+        return pltpu.make_async_copy(stored_z.at[t], weight_z.at[t], sem_z.at[t])
 
     def start_weights(t, carry):
-        for copy in weights(t):
-            copy.start()
-        return carry
+        weights(t).start()
+        return carry
+
+    def weight_of(t, r):
+        cells_y = field.shape[2]
+        base = lax.axis_index("gy") * cells_y
+        return along_y(point_y[r], base, cells_y, cells_y * lax.axis_size("gy"))
 
     found = plan[0]
     for k in range(chunks):
@@ -540,23 +534,21 @@
 
     def step(t, carry):
         ready, sent = carry
-        picks, both = pair(plan, t)
-        for copy in weights(picks[0][0]):
-            copy.wait()
-
-        @pl.when(both)
-        def _():
-            for copy in weights(picks[1][0]):
-                copy.wait()
-
-        ready = wait_to(ready, (picks[1][2] + RAD) // SUB + 1)
+        picks, keeps = group(plan, t)
+        for (n, _, _, _), keep in zip(picks, keeps):
+
+            @pl.when(keep)
+            def _(n=n):
+                weights(n).wait()
+
+        ready = wait_to(ready, (picks[-1][2] + RAD) // SUB + 1)
         sent = send_to(sent, (picks[0][2] + RAD) // SUB - 1)
-        points = (weight_y, weight_z, strength)
-        spread_pair(t, factor * TIME_STEP, field, plan, points, own_low, got_low, got_high)
+        points = (weight_of, weight_z, strength)
+        spread_group(t, factor * TIME_STEP, field, plan, points, own_low, got_low, got_high)
         return ready, sent
 
     zero = jnp.int32(0)
-    ready, sent = lax.fori_loop(0, (plan[0] + 1) // 2, step, (zero, zero))
+    ready, sent = lax.fori_loop(0, groups_of(plan), step, (zero, zero))
     sent = send_to(sent, ready)
 
     def finish(k, carry):
@@ -646,14 +638,11 @@
             values = []
 
 
-def advance_chunk(i, factor, field, shifts, slots, target, finish):
-    last = field.shape[1] - BATCH
-    for n in range(SUB // BATCH):
-        now, later = slots[n % 2], slots[1 - n % 2]
-        along_depth(jnp.minimum(i + BATCH, last), field, shifts, later)
-        for k in range(BATCH):
-            advance(i, k, factor, field, now, target, finish)
-        i = i + BATCH
+def advance_batch(i, n, factor, field, shifts, slots, target, finish):
+    now, later = slots[n % 2], slots[1 - n % 2]
+    along_depth(jnp.minimum(i + BATCH, field.shape[1] - BATCH), field, shifts, later)
+    for k in range(BATCH):
+        advance(i, k, factor, field, now, target, finish)
 
 
 def advance_first(field, section, shifts, slot_a, slot_b):
@@ -661,10 +650,11 @@
     along_depth(0, field, shifts, slot_a)
 
     def step(t, carry):
-        advance_chunk(
-            SUB * t, 1.0, field, shifts, (slot_a, slot_b), section,
-            lambda c, i, rows, cols, value: value,
-        )
+        for n in range(SUB // BATCH):
+            advance_batch(
+                SUB * t + BATCH * n, n, 1.0, field, shifts, (slot_a, slot_b), section,
+                lambda c, i, rows, cols, value: value,
+            )
         return carry
 
     lax.fori_loop(0, field.shape[1] // SUB, step, 0)
@@ -674,10 +664,10 @@
     section_hbm, velocity, following, token,
     section, field, result, shifts, slot_a, slot_b, in_sems, old_sems, out_sems,
 ):
-    chunks = section.shape[1] // SUB
+    chunks = section.shape[1] // BATCH
 
     def planes(k):
-        return pl.ds(k * SUB, SUB)
+        return pl.ds(k * BATCH, BATCH)
 
     def chunk_in(k):
         return pltpu.make_async_copy(
@@ -705,17 +695,21 @@
     chunk_in(0).wait()
     along_depth(0, section, shifts, slot_a)
 
-    def step(k, carry):
-        @pl.when(k + 1 < chunks)
-        def _():
-            chunk_in(k + 1).wait()
-
-        chunk_old(k).wait()
-        advance_chunk(SUB * k, 0.5, section, shifts, (slot_a, slot_b), result, finish)
-        chunk_out(k).start()
-        return carry
-
-    lax.fori_loop(0, chunks, step, 0)
+    def step(t, carry):
+        slots = (slot_a, slot_b)
+        for n in range(SUB // BATCH):
+            k = t * (SUB // BATCH) + n
+
+            @pl.when(k + 1 < chunks)
+            def _(k=k):
+                chunk_in(k + 1).wait()
+
+            chunk_old(k).wait()
+            advance_batch(k * BATCH, n, 0.5, section, shifts, slots, result, finish)
+            chunk_out(k).start()
+        return carry
+
+    lax.fori_loop(0, section.shape[1] // SUB, step, 0)
     for k in range(chunks):
         chunk_out(k).wait()
 
@@ -755,24 +749,23 @@
     per_record = (records, 1, points)
     units = records * (depth // LANES)
     y_shape, z_shape = (units, cells_y, points), (units, 2 * LANES, points)
-    y_bytes, z_bytes = 4 * math.prod(y_shape), 2 * math.prod(z_shape)
+    z_bytes = 2 * math.prod(z_shape)
     products = [pltpu.VMEM((3 * depth, depth), jnp.bfloat16)]
     products += [pltpu.VMEM((2, 3 * BATCH * cells_y, depth), f32)] * 2
     unit_sems = pltpu.SemaphoreType.DMA((units,))
     chunk_sems = pltpu.SemaphoreType.DMA((chunks,))
 
-    field, *own_a, weight_y, weight_z, strength, plan = pl.pallas_call(
+    field, *own_a, weight_y, weight_z, strength, point_y, plan = pl.pallas_call(
         load_sample,
         out_shape=(
             held, pack, pack, edge, edge,
             pltpu.VMEM(y_shape, f32), pltpu.VMEM(z_shape, jnp.bfloat16),
-            array(per_record, f32),
+            array(per_record, f32), array(per_record, i32),
             array((HEAD + 3 * units,), i32),
         ),
         in_specs=[ANYWHERE] * 4 + [SCALAR],
-        out_specs=(WHOLE,) * 8 + (SCALAR,),
+        out_specs=(WHOLE,) * 9 + (SCALAR,),
         scratch_shapes=[
-            pltpu.VMEM(per_record, i32),
             pltpu.VMEM(per_record, i32),
             pltpu.SMEM((records, LANES), i32),
             pltpu.SMEM((2, records), i32),
@@ -804,17 +797,17 @@
         name="advance_first",
     )(resident(field))
 
-    _, section, stored_y, stored_z, *own_b, shares = pl.pallas_call(
+    _, section, stored_z, *own_b, shares = pl.pallas_call(
         spread_sample,
         out_shape=(
-            held, stored, pltpu.HBM(y_shape, f32), pltpu.HBM(z_shape, jnp.bfloat16),
+            held, stored, pltpu.HBM(z_shape, jnp.bfloat16),
             pack, pack, edge, edge,
             array((groups_y, 2, 3 * share, 1, points), f32),
         ),
         in_specs=[WHOLE] * 10 + [SCALAR] + [WHOLE] * 3,
-        out_specs=(WHOLE,) + (ANYWHERE,) * 3 + (WHOLE,) * 5,
+        out_specs=(WHOLE,) + (ANYWHERE,) * 2 + (WHOLE,) * 5,
         input_output_aliases={0: 0},
-        scratch_shapes=[pltpu.SemaphoreType.DMA, unit_sems, unit_sems],
+        scratch_shapes=[pltpu.SemaphoreType.DMA, unit_sems],
         compiler_params=params(),
         cost_estimate=cost(2 * 10**9, 4 * size),
         name="spread_sample",
@@ -830,7 +823,9 @@
         out_shape=(stored, array((SUB, LANES), f32)),
         in_specs=[ANYWHERE] * 2,
         out_specs=(ANYWHERE, WHOLE),
-        scratch_shapes=[pltpu.VMEM(whole, f32)] * 3 + products + [chunk_sems] * 3,
+        scratch_shapes=[pltpu.VMEM(whole, f32)] * 3
+        + products
+        + [pltpu.SemaphoreType.DMA((cells_x // BATCH,))] * 3,
         compiler_params=params(VMEM_LIMIT + 3 * size),
         cost_estimate=cost(10**9, 4 * size),
         name="advance_second",
@@ -850,20 +845,19 @@
     velocity_next = pl.pallas_call(
         spread_next,
         out_shape=stored,
-        in_specs=[ANYWHERE] + [WHOLE] * 9 + [SCALAR, ANYWHERE, ANYWHERE, WHOLE, ANYWHERE],
+        in_specs=[ANYWHERE] + [WHOLE] * 9 + [SCALAR, WHOLE, ANYWHERE, WHOLE, ANYWHERE],
         out_specs=ANYWHERE,
         scratch_shapes=[
             pltpu.VMEM(whole, f32),
-            pltpu.VMEM(y_shape, f32),
             pltpu.VMEM(z_shape, jnp.bfloat16),
-            chunk_sems, chunk_sems, unit_sems, unit_sems,
+            chunk_sems, chunk_sems, unit_sems,
         ],
-        compiler_params=params(VMEM_LIMIT + size + y_bytes + z_bytes),
+        compiler_params=params(VMEM_LIMIT + size + z_bytes),
         cost_estimate=cost(2 * 10**9, 4 * size),
         name="spread_next",
     )(
         streamed(following), inflow, *ghosts_b[:2], *own_b, *ghosts_b[2:],
-        plan, streamed(stored_y), streamed(stored_z), strength, forces,
+        plan, point_y, streamed(stored_z), strength, forces,
     )
     return (velocity_next, all_forces.reshape(1, records, 3, points))
 

time: 93.2 us -> 93.7 us (level); the launches traced: 94.4 us -> 93.3 us
  starting transfers between devices: 43.2 us -> 37.7 us
  Pallas kernels: 49 us -> 52.5 us
    ppermute x8, starting transfers between devices: 31.8 us -> 22.9 us  [shifted(): return lax.ppermute(x, axis, pairs)]
    all_to_all x1, starting transfers between devices: 5.73 us -> 9.11 us  [local(): shares = lax.all_to_all(shares, 'gy', 0, 0)]
    pallas_call x1, Pallas kernels: 12.7 us -> 15.4 us  [local(): pl.pallas_call(advance_second, out_shape=(stored, array((SUB, LANES), f32...]
    pallas_call x1, Pallas kernels: 5.93 us -> 8.49 us  [local(): pl.pallas_call(load_sample, out_shape=(held, pack, pack, edge, edge, pltp...]
    pallas_call x1, Pallas kernels: 11.4 us -> 10.3 us  [local(): pl.pallas_call(spread_next, out_shape=stored, in_specs=[ANYWHERE] + [WHOL...]
  transfers between devices with their start and end apart: 10 -> 10, of which waited for: 0 -> 1; matrix products, arithmetic and copies ran while one was open for 0% -> 0% of each run, Pallas kernels for 37% -> 39%
where the time goes in v2:
time: 93.7 us; the launch traced here: 93.3 us
  Pallas kernels  52.5 us (56%)
  starting transfers between devices  37.7 us (40%)
  between operations  1.43 us (2%)
    ppermute x8, starting transfers between devices, shifted(): return lax.ppermute(x, axis, pairs)  22.9 us
    pallas_call x1, Pallas kernels, local(): pl.pallas_call(advance_second, out_shape=(stored, array((SUB, LANES), f32...  15.4 us
    pallas_call x1, Pallas kernels, local(): pl.pallas_call(spread_next, out_shape=stored, in_specs=[ANYWHERE] + [WHOL...  10.3 us
    pallas_call x1, Pallas kernels, local(): pl.pallas_call(advance_first, out_shape=held, in_specs=[WHOLE], out_specs...  9.7 us
    all_to_all x1, starting transfers between devices, local(): shares = lax.all_to_all(shares, 'gy', 0, 0)  9.11 us
    pallas_call x1, Pallas kernels, local(): pl.pallas_call(load_sample, out_shape=(held, pack, pack, edge, edge, pltp...  8.49 us
    pallas_call x1, Pallas kernels, local(): pl.pallas_call(spread_sample, out_shape=(held, stored, pltpu.HBM(z_shape,...  7.84 us
    all_to_all x1, starting transfers between devices, local(): all_forces = lax.all_to_all(forces, 'gy', 0, 0)  5.72 us
  transfers between devices with their start and end apart: 10, of which 1 were waited for; matrix products, arithmetic and copies ran while one was open for 0% of the time, Pallas kernels for 39%

profile of v2, /device:TPU:1, one launch (start us, length us, event | category | flops | bytes accessed | tf_op | source)
XLA Modules:
  0.0 93.3 jit_solution(2955895218088223669)
XLA Ops:
  1.3 8.5 %load_sample.1 = (f32[3,96,32,256]{3,2,1,0:T(8,128)S(1)}, f32[480,1,256]{2,1,0:T(1,128)S(1)}, f32[480,1,256]{2,1,0:T(1,128)S(1)}, f32[3,32,256]{2,1,0:T(8,128)S(...) custom-call(f32[3,96,32,256]{3,2,1,0:T(8,128)} %velocity.3, ...), custom_call_target="tpu_custom_call" | custom-call | flops 2000000000 | bytes 37748736 | tf_op jit(solution)/shard_map/load_sample/pallas_call | solution.py:758
  9.8 5.1 %collective-permute-start.3 = (f32[480,1,256]{2,1,0:T(1,128)S(1)}, f32[480,1,256]{2,1,0:T(1,128)S(1)}, u32[]{:S(2)}, u32[]{:S(2)}) collective-permute-start(f32[480,1,256]{2,1,0:T(1,128)S(1)} %get-tuple-element.24.own_low), channel_id=1, source_target_pairs={{0,7},{1,0},{2,1},{3,2},{4,3},{5,4},{6,5},{7,6},{8,15},{9,8},{10,9... | collective-permute-start | bytes 1474568 | tf_op jit(solution)/shard_map/ppermute | solution.py:722
  14.8 0.0 collective-permute-start.2
  14.8 6.8 %collective-permute-start = (f32[3,32,256]{2,1,0:T(8,128)S(1)}, f32[3,32,256]{2,1,0:T(8,128)S(1)}, u32[]{:S(2)}, u32[]{:S(2)}) collective-permute-start(f32[3,32,256]{2,1,0:T(8,128)S(1)} %get-tuple-element.22.own_east), channel_id=1, source_target_pairs={{0,8},{8,16},{16,24},{1,9},{9,17},{17,25},{2,10},{10,18},{18,26},{... | collective-permute-start | bytes 294920 | tf_op jit(solution)/shard_map/ppermute | solution.py:722
  21.7 1.9 %collective-permute-start.1 = (f32[3,32,256]{2,1,0:T(8,128)S(1)}, f32[3,32,256]{2,1,0:T(8,128)S(1)}, u32[]{:S(2)}, u32[]{:S(2)}) collective-permute-start(f32[3,32,256]{2,1,0:T(8,128)S(1)} %get-tuple-element.23.own_west), channel_id=1, source_target_pairs={{8,0},{16,8},{24,16},{9,1},{17,9},{25,17},{10,2},{18,10},{26,18},{... | collective-permute-start | bytes 294920 | tf_op jit(solution)/shard_map/ppermute | solution.py:722
  23.6 0.0 copy-start
  23.6 9.7 %advance_first.1.section_in = f32[3,96,32,256]{3,2,1,0:T(8,128)S(1)} custom-call(f32[3,96,32,256]{3,2,1,0:T(8,128)S(1)} %get-tuple-element.21.field), custom_call_target="tpu_custom_call" | custom-call | flops 1000000000 | bytes 37748736 | tf_op jit(solution)/shard_map/advance_first/pallas_call | solution.py:789
  33.3 0.0 collective-permute-done.ghost_low
  33.3 0.0 collective-permute-done.1.ghost_high
  33.3 0.0 collective-permute-done.3.got_high
  33.3 0.9 collective-permute-done.2.got_low
  34.2 0.0 copy-done
  34.2 7.8 %spread_sample.1 = (f32[3,96,32,256]{3,2,1,0:T(8,128)S(1)}, f32[3,96,32,256]{3,2,1,0:T(8,128)}, bf16[128,256,256]{2,1,0:T(8,128)(2,1)}, f32[480,1,256]{2,1,0:T(1...) custom-call(f32[3,96,32,256]{3,2,1,0:T(8,128)S(1)} %advance_first.1., ...), custom_call_target="tpu_custom_call", output_to_operand_aliasing={{0}: (0, {})} | custom-call | flops 2000000000 | bytes 37748736 | tf_op jit(solution)/shard_map/spread_sample/pallas_call | solution.py:800
  42.1 9.1 %all-to-all-start = ((f32[8,2,24,1,256]{4,3,2,1,0:T(1,128)}), f32[8,2,24,1,256]{4,3,2,1,0:T(1,128)S(1)}, u32[]{:S(2)}, u32[]{:S(2)}) async-start(f32[8,2,24,1,256]{4,3,2,1,0:T(1,128)} %get-tuple-element.38), calls=%async_computation | async-start | bytes 786432 | tf_op jit(solution)/shard_map/all_to_all | solution.py:818
  51.2 4.2 %collective-permute-start.7 = (f32[480,1,256]{2,1,0:T(1,128)S(1)}, f32[480,1,256]{2,1,0:T(1,128)S(1)}, u32[]{:S(2)}, u32[]{:S(2)}) collective-permute-start(f32[480,1,256]{2,1,0:T(1,128)S(1)} %get-tuple-element.34.own_low), channel_id=1, source_target_pairs={{0,7},{1,0},{2,1},{3,2},{4,3},{5,4},{6,5},{7,6},{8,15},{9,8},{10,9... | collective-permute-start | bytes 1474568 | tf_op jit(solution)/shard_map/ppermute | solution.py:722
  55.4 0.0 collective-permute-start.6
  55.4 1.9 %collective-permute-start.4 = (f32[3,32,256]{2,1,0:T(8,128)S(1)}, f32[3,32,256]{2,1,0:T(8,128)S(1)}, u32[]{:S(2)}, u32[]{:S(2)}) collective-permute-start(f32[3,32,256]{2,1,0:T(8,128)S(1)} %get-tuple-element.32.own_east), channel_id=1, source_target_pairs={{0,8},{8,16},{16,24},{1,9},{9,17},{17,25},{2,10},{10,18},{18,26},{... | collective-permute-start | bytes 294920 | tf_op jit(solution)/shard_map/ppermute | solution.py:722
  57.3 3.1 %collective-permute-start.5 = (f32[3,32,256]{2,1,0:T(8,128)S(1)}, f32[3,32,256]{2,1,0:T(8,128)S(1)}, u32[]{:S(2)}, u32[]{:S(2)}) collective-permute-start(f32[3,32,256]{2,1,0:T(8,128)S(1)} %get-tuple-element.33.own_west), channel_id=1, source_target_pairs={{8,0},{16,8},{24,16},{9,1},{17,9},{25,17},{10,2},{18,10},{26,18},{... | collective-permute-start | bytes 294920 | tf_op jit(solution)/shard_map/ppermute | solution.py:722
  60.3 15.4 %advance_second.1 = (f32[3,96,32,256]{3,2,1,0:T(8,128)}, f32[8,128]{1,0:T(8,128)S(1)}) custom-call(f32[3,96,32,256]{3,2,1,0:T(8,128)} %get-tuple-element.30.section_hbm, f32[3,96,32,256]{3,2,1,0:T(8,128)} %velocity.3), custom_call_target="tpu_custom_call" | custom-call | flops 1000000000 | bytes 37748736 | tf_op jit(solution)/shard_map/advance_second/pallas_call | solution.py:821
  75.7 0.0 collective-permute-done.4.after_low.ghost_low
  75.7 0.0 collective-permute-done.5.after_high.ghost_high
  75.7 0.0 all-to-all-done.parts
  75.7 0.8 share_force.1.after
  76.5 5.7 %all-to-all-start.1 = ((f32[8,24,1,256]{3,2,1,0:T(1,128)}), f32[8,24,1,256]{3,2,1,0:T(1,128)S(1)}, u32[]{:S(2)}, u32[]{:S(2)}) async-start(f32[8,24,1,256]{3,2,1,0:T(1,128)} %share_force.1.after), calls=%async_computation.1 | async-start | bytes 393216 | tf_op jit(solution)/shard_map/all_to_all | solution.py:843
  82.3 0.0 collective-permute-done.7.got_high
  82.3 0.0 collective-permute-done.6.got_low
  82.3 10.3 %spread_next.1 = f32[3,96,32,256]{3,2,1,0:T(8,128)} custom-call(f32[3,96,32,256]{3,2,1,0:T(8,128)} %get-tuple-element.31.following, f32[3,32,256]{2,1,0:T(8,128)S(1)} %copy-done, f32[3,32,256]{2,1,0:T(8,128)S(1)} %collective-permute-done.4.after_low.ghost_low, f32[3,32,256]{2,1,0:T(8,128)S(1)} %collective-permute-done.5.after_high.ghost_high, ...), custom_call_target="tpu_custom_call" | custom-call | flops 2000000000 | bytes 37748736 | tf_op jit(solution)/shard_map/spread_next/pallas_call | solution.py:845
  92.6 0.0 all-to-all-done.1
  92.6 0.7 copy.9
Async XLA Ops:
  9.8 23.5 %collective-permute-start.3 = (f32[480,1,256]{2,1,0:T(1,128)S(1)}, f32[480,1,256]{2,1,0:T(1,128)S(1)}, u32[]{:S(2)}, u32[]{:S(2)}) collective-permute-start(f32[480,1,256]{2,1,0:T(1,128)S(1)} %get-tuple-element.24.own_low), channel_id=1, source_target_pairs={{0,7},{1,0},{2,1},{3,2},{4,3},{5,4},{6,5},{7,6},{8,15},{9,8},{10,9... | collective-permute-start | bytes 1474568 | tf_op jit(solution)/shard_map/ppermute | solution.py:722
  14.8 19.4 %collective-permute-start.2 = (f32[480,1,256]{2,1,0:T(1,128)S(1)}, f32[480,1,256]{2,1,0:T(1,128)S(1)}, u32[]{:S(2)}, u32[]{:S(2)}) collective-permute-start(f32[480,1,256]{2,1,0:T(1,128)S(1)} %get-tuple-element.25.own_high), channel_id=1, source_target_pairs={{0,1},{1,2},{2,3},{3,4},{4,5},{5,6},{6,7},{7,0},{8,9},{9,10},{10,1... | collective-permute-start | bytes 1474568 | tf_op jit(solution)/shard_map/ppermute | solution.py:722
  14.8 18.5 %collective-permute-start = (f32[3,32,256]{2,1,0:T(8,128)S(1)}, f32[3,32,256]{2,1,0:T(8,128)S(1)}, u32[]{:S(2)}, u32[]{:S(2)}) collective-permute-start(f32[3,32,256]{2,1,0:T(8,128)S(1)} %get-tuple-element.22.own_east), channel_id=1, source_target_pairs={{0,8},{8,16},{16,24},{1,9},{9,17},{17,25},{2,10},{10,18},{18,26},{... | collective-permute-start | bytes 294920 | tf_op jit(solution)/shard_map/ppermute | solution.py:722
  21.7 11.7 %collective-permute-start.1 = (f32[3,32,256]{2,1,0:T(8,128)S(1)}, f32[3,32,256]{2,1,0:T(8,128)S(1)}, u32[]{:S(2)}, u32[]{:S(2)}) collective-permute-start(f32[3,32,256]{2,1,0:T(8,128)S(1)} %get-tuple-element.23.own_west), channel_id=1, source_target_pairs={{8,0},{16,8},{24,16},{9,1},{17,9},{25,17},{10,2},{18,10},{26,18},{... | collective-permute-start | bytes 294920 | tf_op jit(solution)/shard_map/ppermute | solution.py:722
  23.6 10.7 %copy-start = (f32[3,32,256]{2,1,0:T(8,128)S(1)}, f32[3,32,256]{2,1,0:T(8,128)}, u32[]{:S(2)}) copy-start(f32[3,32,256]{2,1,0:T(8,128)} %inflow.3) | copy-start | bytes 294916
  42.1 33.6 %all-to-all-start = ((f32[8,2,24,1,256]{4,3,2,1,0:T(1,128)}), f32[8,2,24,1,256]{4,3,2,1,0:T(1,128)S(1)}, u32[]{:S(2)}, u32[]{:S(2)}) async-start(f32[8,2,24,1,256]{4,3,2,1,0:T(1,128)} %get-tuple-element.38), calls=%async_computation | async-start | bytes 786432 | tf_op jit(solution)/shard_map/all_to_all | solution.py:818
  51.2 31.1 %collective-permute-start.7 = (f32[480,1,256]{2,1,0:T(1,128)S(1)}, f32[480,1,256]{2,1,0:T(1,128)S(1)}, u32[]{:S(2)}, u32[]{:S(2)}) collective-permute-start(f32[480,1,256]{2,1,0:T(1,128)S(1)} %get-tuple-element.34.own_low), channel_id=1, source_target_pairs={{0,7},{1,0},{2,1},{3,2},{4,3},{5,4},{6,5},{7,6},{8,15},{9,8},{10,9... | collective-permute-start | bytes 1474568 | tf_op jit(solution)/shard_map/ppermute | solution.py:722
  55.4 26.9 %collective-permute-start.6 = (f32[480,1,256]{2,1,0:T(1,128)S(1)}, f32[480,1,256]{2,1,0:T(1,128)S(1)}, u32[]{:S(2)}, u32[]{:S(2)}) collective-permute-start(f32[480,1,256]{2,1,0:T(1,128)S(1)} %get-tuple-element.35.own_high), channel_id=1, source_target_pairs={{0,1},{1,2},{2,3},{3,4},{4,5},{5,6},{6,7},{7,0},{8,9},{9,10},{10,1... | collective-permute-start | bytes 1474568 | tf_op jit(solution)/shard_map/ppermute | solution.py:722
  55.4 20.3 %collective-permute-start.4 = (f32[3,32,256]{2,1,0:T(8,128)S(1)}, f32[3,32,256]{2,1,0:T(8,128)S(1)}, u32[]{:S(2)}, u32[]{:S(2)}) collective-permute-start(f32[3,32,256]{2,1,0:T(8,128)S(1)} %get-tuple-element.32.own_east), channel_id=1, source_target_pairs={{0,8},{8,16},{16,24},{1,9},{9,17},{17,25},{2,10},{10,18},{18,26},{... | collective-permute-start | bytes 294920 | tf_op jit(solution)/shard_map/ppermute | solution.py:722
  57.3 18.4 %collective-permute-start.5 = (f32[3,32,256]{2,1,0:T(8,128)S(1)}, f32[3,32,256]{2,1,0:T(8,128)S(1)}, u32[]{:S(2)}, u32[]{:S(2)}) collective-permute-start(f32[3,32,256]{2,1,0:T(8,128)S(1)} %get-tuple-element.33.own_west), channel_id=1, source_target_pairs={{8,0},{16,8},{24,16},{9,1},{17,9},{25,17},{10,2},{18,10},{26,18},{... | collective-permute-start | bytes 294920 | tf_op jit(solution)/shard_map/ppermute | solution.py:722
  76.5 16.0 %all-to-all-start.1 = ((f32[8,24,1,256]{3,2,1,0:T(1,128)}), f32[8,24,1,256]{3,2,1,0:T(1,128)S(1)}, u32[]{:S(2)}, u32[]{:S(2)}) async-start(f32[8,24,1,256]{3,2,1,0:T(1,128)} %share_force.1.after), calls=%async_computation.1 | async-start | bytes 393216 | tf_op jit(solution)/shard_map/all_to_all | solution.py:843

commit v3 on v2

--- a/solution.py
+++ b/solution.py
@@ -19,8 +19,10 @@
 SUB = 8
 GROUP = 4
 BATCH = 4
+PLANES = 8
+BLOCK = 2 * PLANES
 HEAD = 1
-VMEM_LIMIT = 6 * 2**20
+VMEM_LIMIT = 8 * 2**20
 
 WHOLE = pl.BlockSpec(memory_space=pltpu.VMEM)
 SCALAR = pl.BlockSpec(memory_space=pltpu.SMEM)
@@ -50,18 +52,15 @@
 
 
 def along_z(point_z, start):
-    points = point_z.shape[-1]
-    row = lax.broadcasted_iota(jnp.int32, (LANES, points), 0).astype(jnp.bfloat16)
-    place = (point_z - start).astype(jnp.float32)
-    place = jnp.broadcast_to(place, (LANES, points)).astype(jnp.bfloat16)
-    dist = jnp.abs(row - place)
-    near = [dist == float(d) for d in range(RAD + 1)]
+    shape = (LANES, point_z.shape[-1])
+    dist = jnp.abs(lax.broadcasted_iota(jnp.int32, shape, 0) - (point_z - start))
+    near = [dist == d for d in range(RAD + 1)]
     out = []
     for taps in (HIGH, LOW):
-        value = jnp.zeros_like(row)
+        value = 0.0
         for d in range(RAD, -1, -1):
-            value = jnp.where(near[d], jnp.full_like(row, taps[d]), value)
-        out.append(value)
+            value = jnp.where(near[d], taps[d], value)
+        out.append(value.astype(jnp.bfloat16))
     return out
 
 
@@ -575,7 +574,7 @@
 
 def along_depth(i, field, shifts, slot):
     depth = shifts.shape[1]
-    x = jnp.concatenate([field[c, i + k] for k in range(BATCH) for c in range(3)], axis=0)
+    x = jnp.concatenate([field[c, i + k] for k in range(PLANES) for c in range(3)], axis=0)
     high = x.astype(jnp.bfloat16)
     low = (x - high.astype(jnp.float32)).astype(jnp.bfloat16)
     slot[0] = jnp.dot(
@@ -640,8 +639,8 @@
 
 def advance_batch(i, n, factor, field, shifts, slots, target, finish):
     now, later = slots[n % 2], slots[1 - n % 2]
-    along_depth(jnp.minimum(i + BATCH, field.shape[1] - BATCH), field, shifts, later)
-    for k in range(BATCH):
+    along_depth(jnp.minimum(i + PLANES, field.shape[1] - PLANES), field, shifts, later)
+    for k in range(PLANES):
         advance(i, k, factor, field, now, target, finish)
 
 
@@ -650,24 +649,24 @@
     along_depth(0, field, shifts, slot_a)
 
     def step(t, carry):
-        for n in range(SUB // BATCH):
+        for n in range(BLOCK // PLANES):
             advance_batch(
-                SUB * t + BATCH * n, n, 1.0, field, shifts, (slot_a, slot_b), section,
+                BLOCK * t + PLANES * n, n, 1.0, field, shifts, (slot_a, slot_b), section,
                 lambda c, i, rows, cols, value: value,
             )
         return carry
 
-    lax.fori_loop(0, field.shape[1] // SUB, step, 0)
+    lax.fori_loop(0, field.shape[1] // BLOCK, step, 0)
 
 
 def advance_second(
     section_hbm, velocity, following, token,
     section, field, result, shifts, slot_a, slot_b, in_sems, old_sems, out_sems,
 ):
-    chunks = section.shape[1] // BATCH
+    chunks = section.shape[1] // PLANES
 
     def planes(k):
-        return pl.ds(k * BATCH, BATCH)
+        return pl.ds(k * PLANES, PLANES)
 
     def chunk_in(k):
         return pltpu.make_async_copy(
@@ -697,19 +696,24 @@
 
     def step(t, carry):
         slots = (slot_a, slot_b)
-        for n in range(SUB // BATCH):
-            k = t * (SUB // BATCH) + n
+        per = BLOCK // PLANES
+        for n in range(per):
+            k = t * per + n
 
             @pl.when(k + 1 < chunks)
             def _(k=k):
                 chunk_in(k + 1).wait()
 
             chunk_old(k).wait()
-            advance_batch(k * BATCH, n, 0.5, section, shifts, slots, result, finish)
-            chunk_out(k).start()
-        return carry
-
-    lax.fori_loop(0, section.shape[1] // SUB, step, 0)
+        for n in range(per):
+            advance_batch(
+                t * BLOCK + n * PLANES, n, 0.5, section, shifts, slots, result, finish
+            )
+        for n in range(per):
+            chunk_out(t * per + n).start()
+        return carry
+
+    lax.fori_loop(0, chunks * PLANES // BLOCK, step, 0)
     for k in range(chunks):
         chunk_out(k).wait()
 
@@ -751,7 +755,7 @@
     y_shape, z_shape = (units, cells_y, points), (units, 2 * LANES, points)
     z_bytes = 2 * math.prod(z_shape)
     products = [pltpu.VMEM((3 * depth, depth), jnp.bfloat16)]
-    products += [pltpu.VMEM((2, 3 * BATCH * cells_y, depth), f32)] * 2
+    products += [pltpu.VMEM((2, 3 * PLANES * cells_y, depth), f32)] * 2
     unit_sems = pltpu.SemaphoreType.DMA((units,))
     chunk_sems = pltpu.SemaphoreType.DMA((chunks,))
 
@@ -825,7 +829,7 @@
         out_specs=(ANYWHERE, WHOLE),
         scratch_shapes=[pltpu.VMEM(whole, f32)] * 3
         + products
-        + [pltpu.SemaphoreType.DMA((cells_x // BATCH,))] * 3,
+        + [pltpu.SemaphoreType.DMA((cells_x // PLANES,))] * 3,
         compiler_params=params(VMEM_LIMIT + 3 * size),
         cost_estimate=cost(10**9, 4 * size),
         name="advance_second",

time: 93.7 us -> 90 us (0.961)
  starting transfers between devices: 37.7 us -> 27.5 us
  waiting for transfers between devices: 0.92 us -> 6.94 us
    ppermute x8, waiting for transfers between devices: 0.92 us -> 6.93 us  [shifted(): return lax.ppermute(x, axis, pairs)]
    ppermute x8, starting transfers between devices: 22.9 us -> 17.2 us  [shifted(): return lax.ppermute(x, axis, pairs)]
    all_to_all x1, starting transfers between devices: 9.11 us -> 4.83 us  [local(): shares = lax.all_to_all(shares, 'gy', 0, 0)]
    pallas_call x1, Pallas kernels: 8.49 us -> 11.1 us  [local(): pl.pallas_call(load_sample, out_shape=(held, pack, pack, edge, edge, pltp...]
    pallas_call x1, Pallas kernels: 15.4 us -> 13 us  [local(): pl.pallas_call(advance_second, out_shape=(stored, array((SUB, LANES), f32...]
    pallas_call x1, Pallas kernels: 7.84 us -> 9.01 us  [local(): pl.pallas_call(spread_sample, out_shape=(held, stored, pltpu.HBM(z_shape,...]
  transfers between devices with their start and end apart: 10 -> 10, of which waited for: 1 -> 3; matrix products, arithmetic and copies ran while one was open for 0% -> 0% of each run, Pallas kernels for 39% -> 37%
where the time goes in v3:
time: 90 us; the launch traced here: 89.3 us
  Pallas kernels  52.8 us (59%)
  starting transfers between devices  27.5 us (31%)
  waiting for transfers between devices  6.94 us (8%)
  between operations  1.41 us (2%)
    ppermute x8, starting transfers between devices, shifted(): return lax.ppermute(x, axis, pairs)  17.2 us
    pallas_call x1, Pallas kernels, local(): pl.pallas_call(advance_second, out_shape=(stored, array((SUB, LANES), f32...  13 us
    pallas_call x1, Pallas kernels, local(): pl.pallas_call(load_sample, out_shape=(held, pack, pack, edge, edge, pltp...  11.1 us
    pallas_call x1, Pallas kernels, local(): pl.pallas_call(spread_next, out_shape=stored, in_specs=[ANYWHERE] + [WHOL...  9.67 us
    pallas_call x1, Pallas kernels, local(): pl.pallas_call(advance_first, out_shape=held, in_specs=[WHOLE], out_specs...  9.25 us
    pallas_call x1, Pallas kernels, local(): pl.pallas_call(spread_sample, out_shape=(held, stored, pltpu.HBM(z_shape,...  9.01 us
    ppermute x8, waiting for transfers between devices, shifted(): return lax.ppermute(x, axis, pairs)  6.93 us
    all_to_all x1, starting transfers between devices, local(): all_forces = lax.all_to_all(forces, 'gy', 0, 0)  5.43 us
  transfers between devices with their start and end apart: 10, of which 3 were waited for; matrix products, arithmetic and copies ran while one was open for 0% of the time, Pallas kernels for 37%

profile of v3, /device:TPU:1, one launch (start us, length us, event | category | flops | bytes accessed | tf_op | source)
XLA Modules:
  0.0 89.3 jit_solution(14901269536260263641)
XLA Ops:
  1.3 11.1 %load_sample.1 = (f32[3,96,32,256]{3,2,1,0:T(8,128)S(1)}, f32[480,1,256]{2,1,0:T(1,128)S(1)}, f32[480,1,256]{2,1,0:T(1,128)S(1)}, f32[3,32,256]{2,1,0:T(8,128)S(...) custom-call(f32[3,96,32,256]{3,2,1,0:T(8,128)} %velocity.3, ...), custom_call_target="tpu_custom_call" | custom-call | flops 2000000000 | bytes 37748736 | tf_op jit(solution)/shard_map/load_sample/pallas_call | solution.py:762
  12.4 3.6 %collective-permute-start.3 = (f32[480,1,256]{2,1,0:T(1,128)S(1)}, f32[480,1,256]{2,1,0:T(1,128)S(1)}, u32[]{:S(2)}, u32[]{:S(2)}) collective-permute-start(f32[480,1,256]{2,1,0:T(1,128)S(1)} %get-tuple-element.24.own_low), channel_id=1, source_target_pairs={{0,7},{1,0},{2,1},{3,2},{4,3},{5,4},{6,5},{7,6},{8,15},{9,8},{10,9... | collective-permute-start | bytes 1474568 | tf_op jit(solution)/shard_map/ppermute | solution.py:726
  16.0 0.8 collective-permute-start.2
  16.8 1.9 %collective-permute-start = (f32[3,32,256]{2,1,0:T(8,128)S(1)}, f32[3,32,256]{2,1,0:T(8,128)S(1)}, u32[]{:S(2)}, u32[]{:S(2)}) collective-permute-start(f32[3,32,256]{2,1,0:T(8,128)S(1)} %get-tuple-element.22.own_east), channel_id=1, source_target_pairs={{0,8},{8,16},{16,24},{1,9},{9,17},{17,25},{2,10},{10,18},{18,26},{... | collective-permute-start | bytes 294920 | tf_op jit(solution)/shard_map/ppermute | solution.py:726
  18.7 2.4 %collective-permute-start.1 = (f32[3,32,256]{2,1,0:T(8,128)S(1)}, f32[3,32,256]{2,1,0:T(8,128)S(1)}, u32[]{:S(2)}, u32[]{:S(2)}) collective-permute-start(f32[3,32,256]{2,1,0:T(8,128)S(1)} %get-tuple-element.23.own_west), channel_id=1, source_target_pairs={{8,0},{16,8},{24,16},{9,1},{17,9},{25,17},{10,2},{18,10},{26,18},{... | collective-permute-start | bytes 294920 | tf_op jit(solution)/shard_map/ppermute | solution.py:726
  21.1 0.0 copy-start
  21.2 9.2 %advance_first.1.section_in = f32[3,96,32,256]{3,2,1,0:T(8,128)S(1)} custom-call(f32[3,96,32,256]{3,2,1,0:T(8,128)S(1)} %get-tuple-element.21.field), custom_call_target="tpu_custom_call" | custom-call | flops 1000000000 | bytes 37748736 | tf_op jit(solution)/shard_map/advance_first/pallas_call | solution.py:793
  30.4 0.0 collective-permute-done.ghost_low
  30.4 0.0 collective-permute-done.1.ghost_high
  30.4 5.3 %collective-permute-done.3.got_high = f32[480,1,256]{2,1,0:T(1,128)S(1)} collective-permute-done((f32[480,1,256]{2,1,0:T(1,128)S(1)}, f32[480,1,256]{2,1,0:T(1,128)S(1)}, u32[]{:S(2)}, u32[]{:S(2)}) %collective-permute-start.3) | collective-permute-done | bytes 491552 | tf_op jit(solution)/shard_map/ppermute | solution.py:726
  35.8 0.7 collective-permute-done.2.got_low
  36.5 0.0 copy-done
  36.5 9.0 %spread_sample.1 = (f32[3,96,32,256]{3,2,1,0:T(8,128)S(1)}, f32[3,96,32,256]{3,2,1,0:T(8,128)}, bf16[128,256,256]{2,1,0:T(8,128)(2,1)}, f32[480,1,256]{2,1,0:T(1...) custom-call(f32[3,96,32,256]{3,2,1,0:T(8,128)S(1)} %advance_first.1., ...), custom_call_target="tpu_custom_call", output_to_operand_aliasing={{0}: (0, {})} | custom-call | flops 2000000000 | bytes 37748736 | tf_op jit(solution)/shard_map/spread_sample/pallas_call | solution.py:804
  45.5 4.8 %all-to-all-start = ((f32[8,2,24,1,256]{4,3,2,1,0:T(1,128)}), f32[8,2,24,1,256]{4,3,2,1,0:T(1,128)S(1)}, u32[]{:S(2)}, u32[]{:S(2)}) async-start(f32[8,2,24,1,256]{4,3,2,1,0:T(1,128)} %get-tuple-element.38), calls=%async_computation | async-start | bytes 786432 | tf_op jit(solution)/shard_map/all_to_all | solution.py:822
  50.3 4.2 %collective-permute-start.7 = (f32[480,1,256]{2,1,0:T(1,128)S(1)}, f32[480,1,256]{2,1,0:T(1,128)S(1)}, u32[]{:S(2)}, u32[]{:S(2)}) collective-permute-start(f32[480,1,256]{2,1,0:T(1,128)S(1)} %get-tuple-element.34.own_low), channel_id=1, source_target_pairs={{0,7},{1,0},{2,1},{3,2},{4,3},{5,4},{6,5},{7,6},{8,15},{9,8},{10,9... | collective-permute-start | bytes 1474568 | tf_op jit(solution)/shard_map/ppermute | solution.py:726
  54.5 0.0 collective-permute-start.6
  54.5 1.9 %collective-permute-start.4 = (f32[3,32,256]{2,1,0:T(8,128)S(1)}, f32[3,32,256]{2,1,0:T(8,128)S(1)}, u32[]{:S(2)}, u32[]{:S(2)}) collective-permute-start(f32[3,32,256]{2,1,0:T(8,128)S(1)} %get-tuple-element.32.own_east), channel_id=1, source_target_pairs={{0,8},{8,16},{16,24},{1,9},{9,17},{17,25},{2,10},{10,18},{18,26},{... | collective-permute-start | bytes 294920 | tf_op jit(solution)/shard_map/ppermute | solution.py:726
  56.4 2.4 %collective-permute-start.5 = (f32[3,32,256]{2,1,0:T(8,128)S(1)}, f32[3,32,256]{2,1,0:T(8,128)S(1)}, u32[]{:S(2)}, u32[]{:S(2)}) collective-permute-start(f32[3,32,256]{2,1,0:T(8,128)S(1)} %get-tuple-element.33.own_west), channel_id=1, source_target_pairs={{8,0},{16,8},{24,16},{9,1},{17,9},{25,17},{10,2},{18,10},{26,18},{... | collective-permute-start | bytes 294920 | tf_op jit(solution)/shard_map/ppermute | solution.py:726
  58.8 13.0 %advance_second.1 = (f32[3,96,32,256]{3,2,1,0:T(8,128)}, f32[8,128]{1,0:T(8,128)S(1)}) custom-call(f32[3,96,32,256]{3,2,1,0:T(8,128)} %get-tuple-element.30.section_hbm, f32[3,96,32,256]{3,2,1,0:T(8,128)} %velocity.3), custom_call_target="tpu_custom_call" | custom-call | flops 1000000000 | bytes 37748736 | tf_op jit(solution)/shard_map/advance_second/pallas_call | solution.py:825
  71.8 0.0 collective-permute-done.4.after_low.ghost_low
  71.8 0.0 collective-permute-done.5.after_high.ghost_high
  71.8 0.0 all-to-all-done.parts
  71.8 0.8 share_force.1.after
  72.6 5.4 %all-to-all-start.1 = ((f32[8,24,1,256]{3,2,1,0:T(1,128)}), f32[8,24,1,256]{3,2,1,0:T(1,128)S(1)}, u32[]{:S(2)}, u32[]{:S(2)}) async-start(f32[8,24,1,256]{3,2,1,0:T(1,128)} %share_force.1.after), calls=%async_computation.1 | async-start | bytes 393216 | tf_op jit(solution)/shard_map/all_to_all | solution.py:847
  78.1 0.9 collective-permute-done.7.got_high
  79.0 0.0 collective-permute-done.6.got_low
  79.0 9.7 %spread_next.1 = f32[3,96,32,256]{3,2,1,0:T(8,128)} custom-call(f32[3,96,32,256]{3,2,1,0:T(8,128)} %get-tuple-element.31.following, f32[3,32,256]{2,1,0:T(8,128)S(1)} %copy-done, f32[3,32,256]{2,1,0:T(8,128)S(1)} %collective-permute-done.4.after_low.ghost_low, f32[3,32,256]{2,1,0:T(8,128)S(1)} %collective-permute-done.5.after_high.ghost_high, ...), custom_call_target="tpu_custom_call" | custom-call | flops 2000000000 | bytes 37748736 | tf_op jit(solution)/shard_map/spread_next/pallas_call | solution.py:849
  88.6 0.0 all-to-all-done.1
  88.7 0.7 copy.9
Async XLA Ops:
  12.4 23.4 %collective-permute-start.3 = (f32[480,1,256]{2,1,0:T(1,128)S(1)}, f32[480,1,256]{2,1,0:T(1,128)S(1)}, u32[]{:S(2)}, u32[]{:S(2)}) collective-permute-start(f32[480,1,256]{2,1,0:T(1,128)S(1)} %get-tuple-element.24.own_low), channel_id=1, source_target_pairs={{0,7},{1,0},{2,1},{3,2},{4,3},{5,4},{6,5},{7,6},{8,15},{9,8},{10,9... | collective-permute-start | bytes 1474568 | tf_op jit(solution)/shard_map/ppermute | solution.py:726
  16.0 20.5 %collective-permute-start.2 = (f32[480,1,256]{2,1,0:T(1,128)S(1)}, f32[480,1,256]{2,1,0:T(1,128)S(1)}, u32[]{:S(2)}, u32[]{:S(2)}) collective-permute-start(f32[480,1,256]{2,1,0:T(1,128)S(1)} %get-tuple-element.25.own_high), channel_id=1, source_target_pairs={{0,1},{1,2},{2,3},{3,4},{4,5},{5,6},{6,7},{7,0},{8,9},{9,10},{10,1... | collective-permute-start | bytes 1474568 | tf_op jit(solution)/shard_map/ppermute | solution.py:726
  16.8 13.6 %collective-permute-start = (f32[3,32,256]{2,1,0:T(8,128)S(1)}, f32[3,32,256]{2,1,0:T(8,128)S(1)}, u32[]{:S(2)}, u32[]{:S(2)}) collective-permute-start(f32[3,32,256]{2,1,0:T(8,128)S(1)} %get-tuple-element.22.own_east), channel_id=1, source_target_pairs={{0,8},{8,16},{16,24},{1,9},{9,17},{17,25},{2,10},{10,18},{18,26},{... | collective-permute-start | bytes 294920 | tf_op jit(solution)/shard_map/ppermute | solution.py:726
  18.7 11.7 %collective-permute-start.1 = (f32[3,32,256]{2,1,0:T(8,128)S(1)}, f32[3,32,256]{2,1,0:T(8,128)S(1)}, u32[]{:S(2)}, u32[]{:S(2)}) collective-permute-start(f32[3,32,256]{2,1,0:T(8,128)S(1)} %get-tuple-element.23.own_west), channel_id=1, source_target_pairs={{8,0},{16,8},{24,16},{9,1},{17,9},{25,17},{10,2},{18,10},{26,18},{... | collective-permute-start | bytes 294920 | tf_op jit(solution)/shard_map/ppermute | solution.py:726
  21.1 15.3 %copy-start = (f32[3,32,256]{2,1,0:T(8,128)S(1)}, f32[3,32,256]{2,1,0:T(8,128)}, u32[]{:S(2)}) copy-start(f32[3,32,256]{2,1,0:T(8,128)} %inflow.3) | copy-start | bytes 294916
  45.5 26.3 %all-to-all-start = ((f32[8,2,24,1,256]{4,3,2,1,0:T(1,128)}), f32[8,2,24,1,256]{4,3,2,1,0:T(1,128)S(1)}, u32[]{:S(2)}, u32[]{:S(2)}) async-start(f32[8,2,24,1,256]{4,3,2,1,0:T(1,128)} %get-tuple-element.38), calls=%async_computation | async-start | bytes 786432 | tf_op jit(solution)/shard_map/all_to_all | solution.py:822
  50.3 28.7 %collective-permute-start.7 = (f32[480,1,256]{2,1,0:T(1,128)S(1)}, f32[480,1,256]{2,1,0:T(1,128)S(1)}, u32[]{:S(2)}, u32[]{:S(2)}) collective-permute-start(f32[480,1,256]{2,1,0:T(1,128)S(1)} %get-tuple-element.34.own_low), channel_id=1, source_target_pairs={{0,7},{1,0},{2,1},{3,2},{4,3},{5,4},{6,5},{7,6},{8,15},{9,8},{10,9... | collective-permute-start | bytes 1474568 | tf_op jit(solution)/shard_map/ppermute | solution.py:726
  54.5 24.5 %collective-permute-start.6 = (f32[480,1,256]{2,1,0:T(1,128)S(1)}, f32[480,1,256]{2,1,0:T(1,128)S(1)}, u32[]{:S(2)}, u32[]{:S(2)}) collective-permute-start(f32[480,1,256]{2,1,0:T(1,128)S(1)} %get-tuple-element.35.own_high), channel_id=1, source_target_pairs={{0,1},{1,2},{2,3},{3,4},{4,5},{5,6},{6,7},{7,0},{8,9},{9,10},{10,1... | collective-permute-start | bytes 1474568 | tf_op jit(solution)/shard_map/ppermute | solution.py:726
  54.5 17.3 %collective-permute-start.4 = (f32[3,32,256]{2,1,0:T(8,128)S(1)}, f32[3,32,256]{2,1,0:T(8,128)S(1)}, u32[]{:S(2)}, u32[]{:S(2)}) collective-permute-start(f32[3,32,256]{2,1,0:T(8,128)S(1)} %get-tuple-element.32.own_east), channel_id=1, source_target_pairs={{0,8},{8,16},{16,24},{1,9},{9,17},{17,25},{2,10},{10,18},{18,26},{... | collective-permute-start | bytes 294920 | tf_op jit(solution)/shard_map/ppermute | solution.py:726
  56.4 15.4 %collective-permute-start.5 = (f32[3,32,256]{2,1,0:T(8,128)S(1)}, f32[3,32,256]{2,1,0:T(8,128)S(1)}, u32[]{:S(2)}, u32[]{:S(2)}) collective-permute-start(f32[3,32,256]{2,1,0:T(8,128)S(1)} %get-tuple-element.33.own_west), channel_id=1, source_target_pairs={{8,0},{16,8},{24,16},{9,1},{17,9},{25,17},{10,2},{18,10},{26,18},{... | collective-permute-start | bytes 294920 | tf_op jit(solution)/shard_map/ppermute | solution.py:726
  72.6 16.0 %all-to-all-start.1 = ((f32[8,24,1,256]{3,2,1,0:T(1,128)}), f32[8,24,1,256]{3,2,1,0:T(1,128)S(1)}, u32[]{:S(2)}, u32[]{:S(2)}) async-start(f32[8,24,1,256]{3,2,1,0:T(1,128)} %share_force.1.after), calls=%async_computation.1 | async-start | bytes 393216 | tf_op jit(solution)/shard_map/all_to_all | solution.py:847

commit v4 on v3

--- a/solution.py
+++ b/solution.py
@@ -21,7 +21,8 @@
 BATCH = 4
 PLANES = 8
 BLOCK = 2 * PLANES
-HEAD = 1
+CHUNK = 16
+TILES = 8
 VMEM_LIMIT = 8 * 2**20
 
 WHOLE = pl.BlockSpec(memory_space=pltpu.VMEM)
@@ -52,15 +53,18 @@
 
 
 def along_z(point_z, start):
-    shape = (LANES, point_z.shape[-1])
-    dist = jnp.abs(lax.broadcasted_iota(jnp.int32, shape, 0) - (point_z - start))
-    near = [dist == d for d in range(RAD + 1)]
+    points = point_z.shape[-1]
+    row = lax.broadcasted_iota(jnp.int32, (LANES, points), 0).astype(jnp.bfloat16)
+    place = (point_z - start).astype(jnp.float32)
+    place = jnp.broadcast_to(place, (LANES, points)).astype(jnp.bfloat16)
+    dist = jnp.abs(row - place)
+    near = [dist == float(d) for d in range(RAD + 1)]
     out = []
     for taps in (HIGH, LOW):
-        value = 0.0
+        value = jnp.zeros_like(row)
         for d in range(RAD, -1, -1):
-            value = jnp.where(near[d], taps[d], value)
-        out.append(value.astype(jnp.bfloat16))
+            value = jnp.where(near[d], jnp.full_like(row, taps[d]), value)
+        out.append(value)
     return out
 
 
@@ -78,60 +82,60 @@
     )
 
 
-def make_plan(hubs, tiles, touch, counts, start, plan, bucket, held):
-    tile_y, groups_y = lax.axis_index("gy"), lax.axis_size("gy")
-    records, chunks = tiles.shape[1], held.shape[0]
-    for k in range(chunks):
-        held[k] = 0
-
-    def place(r, carry):
-        offset = tile_y - tiles[0, r]
-        offset = jnp.where(offset < 0, offset + groups_y, offset)
-
-        @pl.when(jnp.logical_and(offset < tiles[1, r], touch[r, 1] >= 0))
-        def _():
-            k = (hubs[r, 0] - start + RAD) // SUB
-            bucket[k, held[k]] = r
-            held[k] = held[k] + 1
-
-        return carry
-
-    lax.fori_loop(0, jnp.minimum(counts[0], records), place, 0)
-
-    units = (plan.shape[0] - HEAD) // 3
-
-    def flatten(k, found):
-        def move(j, found):
-            r = bucket[k, j]
-
-            def add(half, found):
-                plan[HEAD + found] = r
-                plan[HEAD + units + found] = hubs[r, 0] - start
-                plan[HEAD + 2 * units + found] = half
-                return found + 1
-
-            first = (touch[r, 0] - RAD) // LANES
-            return lax.fori_loop(first, (touch[r, 1] + RAD) // LANES + 1, add, found)
-
-        return lax.fori_loop(0, held[k], move, found)
-
-    plan[0] = lax.fori_loop(0, chunks, flatten, jnp.int32(0))
+def make_plan(hub, lowest, highest, tiles, live, table):
+    f32, i32 = jnp.float32, jnp.int32
+    tile_y = lax.axis_index("gy").astype(f32)
+    groups_y = float(lax.axis_size("gy"))
+    records, units = hub.shape[0], table.shape[1]
+    square = (records, records)
+    diagonal = lax.broadcasted_iota(i32, square, 0) == lax.broadcasted_iota(i32, square, 1)
+
+    def turned(x, axis):
+        kept = jnp.where(diagonal, jnp.broadcast_to(x, square), 0.0)
+        return jnp.sum(kept, axis=axis, keepdims=True)
+
+    first, count = turned(tiles[0:1].astype(f32), 1), turned(tiles[1:2].astype(f32), 1)
+    offset = tile_y - first
+    offset = jnp.where(offset < 0.0, offset + groups_y, offset)
+    order = lax.broadcasted_iota(i32, (records, 1), 0).astype(f32)
+    valid = jnp.logical_and(offset < count, order < live)
+    valid = jnp.logical_and(valid, highest >= 0.0)
+    low = jnp.right_shift(lowest.astype(i32) - RAD, 7)
+    high = jnp.right_shift(highest.astype(i32) + RAD, 7)
+    number = jnp.where(valid, (high - low + 1).astype(f32), 0.0)
+    key = hub * float(records) + order
+    before = turned(key, 0) < key
+    place = jnp.sum(jnp.where(before, turned(number, 0), 0.0), axis=1, keepdims=True)
+    lane = lax.broadcasted_iota(i32, (records, units), 1).astype(f32)
+    mine = jnp.logical_and(lane >= place, lane < place + number)
+
+    def pick(value):
+        return jnp.sum(jnp.where(mine, value, 0.0), axis=0, keepdims=True).astype(i32)
+
+    table[0:1] = pick(order)
+    table[1:2] = pick(hub)
+    table[2:3] = pick(low.astype(f32) + lane - place)
+    total = jnp.sum(number, axis=0, keepdims=True).astype(i32)
+    table[3:4] = jnp.broadcast_to(total, (1, units))
+
+
+def found(plan):
+    return plan[3, 0]
 
 
 def group(plan, t):
-    units = (plan.shape[0] - HEAD) // 3
     picks, keeps = [], []
     for k in range(GROUP):
         wanted = GROUP * t + k
-        n = jnp.minimum(wanted, plan[0] - 1)
-        record, hub, half = [plan[HEAD + k * units + n] for k in range(3)]
-        picks.append((n, record, hub, pl.ds(pl.multiple_of(half * LANES, LANES), LANES)))
+        n = jnp.minimum(wanted, found(plan) - 1)
+        cols = pl.ds(pl.multiple_of(plan[2, n] * LANES, LANES), LANES)
+        picks.append((n, plan[0, n], plan[1, n], cols))
         keeps.append(wanted == n)
     return picks, keeps
 
 
 def groups_of(plan):
-    return (plan[0] + GROUP - 1) // GROUP
+    return (found(plan) + GROUP - 1) // GROUP
 
 
 def sampled_rows(field, weight_y, weight_z, picks):
@@ -190,16 +194,16 @@
 def load_sample(
     velocity, positions, tiles_hbm, coefs_hbm, counts,
     field, pack_low, pack_high, edge_west, edge_east, weight_y, weight_z, strength, point_y, plan,
-    point_z, hubs, tiles, places, coefs, flags, touch, bucket, held, small_sems, touch_sem, sems,
+    point_z, hubs, tiles, places, coefs, table, small_sems, plan_sem, sems,
 ):
     cells_x, cells_y, depth = field.shape[1:]
     records, points = coefs.shape
-    chunks = cells_x // SUB
+    chunks = cells_x // CHUNK
     first_row = 3 * cells_x
     start = lax.axis_index("gx") * cells_x
 
     def chunk(k):
-        planes = pl.ds(k * SUB, SUB)
+        planes = pl.ds(k * CHUNK, CHUNK)
         return pltpu.make_async_copy(velocity.at[:, planes], field.at[:, planes], sems.at[k])
 
     small = [
@@ -218,16 +222,17 @@
         copy.start()
     for k in range(chunks):
         chunk(k).start()
-    small[0].wait()
+    for copy in small[:3]:
+        copy.wait()
     near = wrapped(places[0], base, total_y)
     inside = jnp.logical_and(near >= -RAD, near < cells_y + RAD)
     height = places[1].astype(jnp.float32)
     lowest = jnp.min(jnp.where(inside, height, float(depth)), axis=1, keepdims=True)
     highest = jnp.max(jnp.where(inside, height, -1.0), axis=1, keepdims=True)
-    column = lax.broadcasted_iota(jnp.int32, flags.shape, 1)
-    flags[...] = jnp.where(column == 0, lowest, highest).astype(jnp.int32)
-    touch_copy = pltpu.make_async_copy(flags, touch, touch_sem)
-    touch_copy.start()
+    hub = (hubs[:, 0:1] - start).astype(jnp.float32)
+    make_plan(hub, lowest, highest, tiles, counts[0].astype(jnp.float32), table)
+    plan_copy = pltpu.make_async_copy(table, plan, plan_sem)
+    plan_copy.start()
 
     def clear(n, carry):
         for k in range(SUB):
@@ -235,8 +240,7 @@
         return carry
 
     lax.fori_loop(0, 3 * records // SUB, clear, 0)
-    for copy in small[1:]:
-        copy.wait()
+    small[3].wait()
     for first in range(0, records, SUB):
         here = range(first, first + SUB)
         rows = [
@@ -245,15 +249,13 @@
         ]
         for r, (y, z, coef) in zip(here, rows):
             point_y[r], point_z[r], strength[r] = y, z, coef
-    touch_copy.wait()
-    make_plan(hubs, tiles, touch, counts, start, plan, bucket, held)
+    plan_copy.wait()
 
     def weigh(t, carry):
-        units = weight_z.shape[0]
         made = []
         for k in range(2):
-            n = jnp.minimum(2 * t + k, plan[0] - 1)
-            r, half = plan[HEAD + n], plan[HEAD + 2 * units + n]
+            n = jnp.minimum(2 * t + k, found(plan) - 1)
+            r, half = plan[0, n], plan[2, n]
             high, low = along_z(point_z[r], half * LANES)
             made.append((n, along_y(point_y[r], base, cells_y, total_y), high, low))
         for n, across, high, low in made:
@@ -262,7 +264,7 @@
             weight_z[n, LANES:] = low
         return carry
 
-    lax.fori_loop(0, (plan[0] + 1) // 2, weigh, 0)
+    lax.fori_loop(0, (found(plan) + 1) // 2, weigh, 0)
 
     def wait_to(ready, wanted):
         def step(k, carry):
@@ -274,7 +276,7 @@
 
     def step(t, ready):
         picks, keeps = group(plan, t)
-        ready = wait_to(ready, (picks[-1][2] + RAD) // SUB + 1)
+        ready = wait_to(ready, (picks[-1][2] + RAD) // CHUNK + 1)
         rows = sampled_rows(field, weight_y, weight_z, picks)
         add_rows(pack_low, first_row, picks, rows, keeps)
         return ready
@@ -386,7 +388,8 @@
     first_row = 3 * cells_x
 
     def store(t):
-        return pltpu.make_async_copy(weight_z.at[t], stored_z.at[t], sem_z.at[t])
+        some = pl.ds(t * TILES, TILES)
+        return pltpu.make_async_copy(weight_z.at[some], stored_z.at[some], sem_z.at[t])
 
     def start_store(t, carry):
         store(t).start()
@@ -396,7 +399,8 @@
         store(t).wait()
         return carry
 
-    lax.fori_loop(0, plan[0], start_store, 0)
+    stores = (found(plan) + TILES - 1) // TILES
+    lax.fori_loop(0, stores, start_store, 0)
 
     def fix_step(t, carry):
         fix_rows(1.0, section, own_low, own_high, got_low, got_high, t)
@@ -441,7 +445,7 @@
         return carry
 
     lax.fori_loop(0, records, copy_rows, 0)
-    lax.fori_loop(0, plan[0], wait_store, 0)
+    lax.fori_loop(0, stores, wait_store, 0)
     copy.wait()
 
 
@@ -477,21 +481,23 @@
     plan, point_y, stored_z, strength, after,
     result, field, weight_z, in_sems, out_sems, sem_z,
 ):
-    chunks = field.shape[1] // SUB
+    chunks = field.shape[1] // CHUNK
     factor = 0.5
 
     def chunk_in(k):
-        planes = pl.ds(k * SUB, SUB)
+        planes = pl.ds(k * CHUNK, CHUNK)
         return pltpu.make_async_copy(following.at[:, planes], field.at[:, planes], in_sems.at[k])
 
     def chunk_out(k):
-        planes = pl.ds(k * SUB, SUB)
+        planes = pl.ds(k * CHUNK, CHUNK)
         return pltpu.make_async_copy(field.at[:, planes], result.at[:, planes], out_sems.at[k])
 
     def wait_to(ready, wanted):
         def step(k, carry):
             chunk_in(k).wait()
-            fix_rows(factor, field, own_low, own_high, got_low, got_high, k)
+            for n in range(CHUNK // SUB):
+                t = k * (CHUNK // SUB) + n
+                fix_rows(factor, field, own_low, own_high, got_low, got_high, t)
 
             @pl.when(k == 0)
             def _():
@@ -515,7 +521,8 @@
         return jnp.maximum(sent, done)
 
     def weights(t):
-        return pltpu.make_async_copy(stored_z.at[t], weight_z.at[t], sem_z.at[t])
+        some = pl.ds(t * TILES, TILES)
+        return pltpu.make_async_copy(stored_z.at[some], weight_z.at[some], sem_z.at[t])
 
     def start_weights(t, carry):
         weights(t).start()
@@ -526,22 +533,20 @@
         base = lax.axis_index("gy") * cells_y
         return along_y(point_y[r], base, cells_y, cells_y * lax.axis_size("gy"))
 
-    found = plan[0]
+    loads = (found(plan) + TILES - 1) // TILES
     for k in range(chunks):
         chunk_in(k).start()
-        lax.fori_loop(k * found // chunks, (k + 1) * found // chunks, start_weights, 0)
+        lax.fori_loop(k * loads // chunks, (k + 1) * loads // chunks, start_weights, 0)
 
     def step(t, carry):
         ready, sent = carry
         picks, keeps = group(plan, t)
-        for (n, _, _, _), keep in zip(picks, keeps):
-
-            @pl.when(keep)
-            def _(n=n):
-                weights(n).wait()
-
-        ready = wait_to(ready, (picks[-1][2] + RAD) // SUB + 1)
-        sent = send_to(sent, (picks[0][2] + RAD) // SUB - 1)
+        @pl.when(t * GROUP % TILES == 0)
+        def _():
+            weights(t * GROUP // TILES).wait()
+
+        ready = wait_to(ready, (picks[-1][2] + RAD) // CHUNK + 1)
+        sent = send_to(sent, (picks[0][2] - RAD) // CHUNK)
         points = (weight_of, weight_z, strength)
         spread_group(t, factor * TIME_STEP, field, plan, points, own_low, got_low, got_high)
         return ready, sent
@@ -663,22 +668,25 @@
     section_hbm, velocity, following, token,
     section, field, result, shifts, slot_a, slot_b, in_sems, old_sems, out_sems,
 ):
-    chunks = section.shape[1] // PLANES
+    cells_x = section.shape[1]
+    blocks = cells_x // BLOCK
 
     def planes(k):
-        return pl.ds(k * PLANES, PLANES)
-
-    def chunk_in(k):
-        return pltpu.make_async_copy(
-            section_hbm.at[:, planes(k)], section.at[:, planes(k)], in_sems.at[k]
-        )
-
-    def chunk_old(k):
+        return pl.ds(k * BLOCK, BLOCK)
+
+    def section_in(k):
+        if isinstance(k, int) and k in (0, blocks):
+            some = pl.ds(0 if k == 0 else cells_x - PLANES, PLANES)
+        else:
+            some = pl.ds(k * BLOCK - PLANES, BLOCK)
+        return pltpu.make_async_copy(section_hbm.at[:, some], section.at[:, some], in_sems.at[k])
+
+    def old_in(k):
         return pltpu.make_async_copy(
             velocity.at[:, planes(k)], field.at[:, planes(k)], old_sems.at[k]
         )
 
-    def chunk_out(k):
+    def block_out(k):
         return pltpu.make_async_copy(
             result.at[:, planes(k)], following.at[:, planes(k)], out_sems.at[k]
         )
@@ -686,36 +694,35 @@
     def finish(c, i, rows, cols, value):
         return value + 0.5 * field[c, i, rows, cols]
 
-    for k in range(chunks):
-        chunk_in(k).start()
-        chunk_old(k).start()
+    for k in range(blocks + 1):
+        section_in(k).start()
+        if k > 0:
+            old_in(k - 1).start()
     token[...] = jnp.zeros_like(token)
     fill_shifts(shifts)
-    chunk_in(0).wait()
+    section_in(0).wait()
     along_depth(0, section, shifts, slot_a)
 
     def step(t, carry):
-        slots = (slot_a, slot_b)
-        per = BLOCK // PLANES
-        for n in range(per):
-            k = t * per + n
-
-            @pl.when(k + 1 < chunks)
-            def _(k=k):
-                chunk_in(k + 1).wait()
-
-            chunk_old(k).wait()
-        for n in range(per):
+        @pl.when(t + 1 < blocks)
+        def _():
+            section_in(t + 1).wait()
+
+        @pl.when(t + 1 == blocks)
+        def _():
+            section_in(blocks).wait()
+
+        old_in(t).wait()
+        for n in range(BLOCK // PLANES):
             advance_batch(
-                t * BLOCK + n * PLANES, n, 0.5, section, shifts, slots, result, finish
+                t * BLOCK + n * PLANES, n, 0.5, section, shifts, (slot_a, slot_b), result, finish
             )
-        for n in range(per):
-            chunk_out(t * per + n).start()
-        return carry
-
-    lax.fori_loop(0, chunks * PLANES // BLOCK, step, 0)
-    for k in range(chunks):
-        chunk_out(k).wait()
+        block_out(t).start()
+        return carry
+
+    lax.fori_loop(0, blocks, step, 0)
+    for k in range(blocks):
+        block_out(k).wait()
 
 
 def shifted(x, axis, step, periodic):
@@ -743,7 +750,7 @@
     tiles, coefs = tiles[0].T, coefs[0]
     records, points = coefs.shape
     share = records // groups_y
-    chunks = cells_x // SUB
+    chunks = cells_x // CHUNK
     size = 4 * math.prod(whole)
     held = pltpu.VMEM(whole, f32)
     stored = pltpu.HBM(whole, f32)
@@ -756,7 +763,7 @@
     z_bytes = 2 * math.prod(z_shape)
     products = [pltpu.VMEM((3 * depth, depth), jnp.bfloat16)]
     products += [pltpu.VMEM((2, 3 * PLANES * cells_y, depth), f32)] * 2
-    unit_sems = pltpu.SemaphoreType.DMA((units,))
+    unit_sems = pltpu.SemaphoreType.DMA((units // TILES,))
     chunk_sems = pltpu.SemaphoreType.DMA((chunks,))
 
     field, *own_a, weight_y, weight_z, strength, point_y, plan = pl.pallas_call(
@@ -765,20 +772,17 @@
             held, pack, pack, edge, edge,
             pltpu.VMEM(y_shape, f32), pltpu.VMEM(z_shape, jnp.bfloat16),
             array(per_record, f32), array(per_record, i32),
-            array((HEAD + 3 * units,), i32),
+            array((SUB, units), i32),
         ),
         in_specs=[ANYWHERE] * 4 + [SCALAR],
         out_specs=(WHOLE,) * 9 + (SCALAR,),
         scratch_shapes=[
             pltpu.VMEM(per_record, i32),
-            pltpu.SMEM((records, LANES), i32),
-            pltpu.SMEM((2, records), i32),
+            pltpu.VMEM((records, LANES), i32),
+            pltpu.VMEM((2, records), i32),
             pltpu.VMEM((2, records, points), i32),
             pltpu.VMEM((records, points), f32),
-            pltpu.VMEM((records, LANES), i32),
-            pltpu.SMEM((records, LANES), i32),
-            pltpu.SMEM((chunks, records), i32),
-            pltpu.SMEM((chunks,), i32),
+            pltpu.VMEM((SUB, units), i32),
             pltpu.SemaphoreType.DMA((4,)),
             pltpu.SemaphoreType.DMA,
             chunk_sems,
@@ -829,7 +833,7 @@
         out_specs=(ANYWHERE, WHOLE),
         scratch_shapes=[pltpu.VMEM(whole, f32)] * 3
         + products
-        + [pltpu.SemaphoreType.DMA((cells_x // PLANES,))] * 3,
+        + [pltpu.SemaphoreType.DMA((cells_x // BLOCK + 1,))] * 3,
         compiler_params=params(VMEM_LIMIT + 3 * size),
         cost_estimate=cost(10**9, 4 * size),
         name="advance_second",

time: 90 us -> 86.9 us (0.966); the launches traced: 89.3 us -> 85.2 us
  Pallas kernels: 52.8 us -> 44.1 us
  starting transfers between devices: 27.5 us -> 35.2 us
  waiting for transfers between devices: 6.94 us -> 3.76 us
    ppermute x8, starting transfers between devices: 17.2 us -> 25 us  [shifted(): return lax.ppermute(x, axis, pairs)]
    pallas_call x1, Pallas kernels: 11.1 us -> 5.42 us  [local(): pl.pallas_call(load_sample, out_shape=(held, pack, pack, edge, edge, pltp...]
    ppermute x8, waiting for transfers between devices: 6.93 us -> 3.75 us  [shifted(): return lax.ppermute(x, axis, pairs)]
    pallas_call x1, Pallas kernels: 9.01 us -> 6.45 us  [local(): pl.pallas_call(spread_sample, out_shape=(held, stored, pltpu.HBM(z_shape,...]
  transfers between devices with their start and end apart: 10 -> 10, of which waited for: 3 -> 2; matrix products, arithmetic and copies ran while one was open for 0% -> 0% of each run, Pallas kernels for 37% -> 38%
where the time goes in v4:
time: 86.9 us; the launch traced here: 85.2 us
  Pallas kernels  44.1 us (51%)
  starting transfers between devices  35.2 us (41%)
  waiting for transfers between devices  3.76 us (4%)
  between operations  1.42 us (2%)
    ppermute x8, starting transfers between devices, shifted(): return lax.ppermute(x, axis, pairs)  25 us
    pallas_call x1, Pallas kernels, local(): pl.pallas_call(advance_second, out_shape=(stored, array((SUB, LANES), f32...  12.9 us
    pallas_call x1, Pallas kernels, local(): pl.pallas_call(spread_next, out_shape=stored, in_specs=[ANYWHERE] + [WHOL...  9.33 us
    pallas_call x1, Pallas kernels, local(): pl.pallas_call(advance_first, out_shape=held, in_specs=[WHOLE], out_specs...  9.25 us
    pallas_call x1, Pallas kernels, local(): pl.pallas_call(spread_sample, out_shape=(held, stored, pltpu.HBM(z_shape,...  6.45 us
    all_to_all x1, starting transfers between devices, local(): all_forces = lax.all_to_all(forces, 'gy', 0, 0)  5.7 us
    pallas_call x1, Pallas kernels, local(): pl.pallas_call(load_sample, out_shape=(held, pack, pack, edge, edge, pltp...  5.42 us
    all_to_all x1, starting transfers between devices, local(): shares = lax.all_to_all(shares, 'gy', 0, 0)  4.45 us
  transfers between devices with their start and end apart: 10, of which 2 were waited for; matrix products, arithmetic and copies ran while one was open for 0% of the time, Pallas kernels for 38%

profile of v4, /device:TPU:1, one launch (start us, length us, event | category | flops | bytes accessed | tf_op | source)
XLA Modules:
  0.0 85.2 jit_solution(11472915163769059703)
XLA Ops:
  1.3 5.4 %load_sample.1 = (f32[3,96,32,256]{3,2,1,0:T(8,128)S(1)}, f32[480,1,256]{2,1,0:T(1,128)S(1)}, f32[480,1,256]{2,1,0:T(1,128)S(1)}, f32[3,32,256]{2,1,0:T(8,128)S(...) custom-call(f32[3,96,32,256]{3,2,1,0:T(8,128)} %velocity.3, ...), custom_call_target="tpu_custom_call" | custom-call | flops 2000000000 | bytes 37748736 | tf_op jit(solution)/shard_map/load_sample/pallas_call | solution.py:769
  6.7 5.1 %collective-permute-start.3 = (f32[480,1,256]{2,1,0:T(1,128)S(1)}, f32[480,1,256]{2,1,0:T(1,128)S(1)}, u32[]{:S(2)}, u32[]{:S(2)}) collective-permute-start(f32[480,1,256]{2,1,0:T(1,128)S(1)} %get-tuple-element.24.own_low), channel_id=1, source_target_pairs={{0,7},{1,0},{2,1},{3,2},{4,3},{5,4},{6,5},{7,6},{8,15},{9,8},{10,9... | collective-permute-start | bytes 1474568 | tf_op jit(solution)/shard_map/ppermute | solution.py:733
  11.8 0.0 collective-permute-start.2
  11.8 4.4 %collective-permute-start = (f32[3,32,256]{2,1,0:T(8,128)S(1)}, f32[3,32,256]{2,1,0:T(8,128)S(1)}, u32[]{:S(2)}, u32[]{:S(2)}) collective-permute-start(f32[3,32,256]{2,1,0:T(8,128)S(1)} %get-tuple-element.22.own_east), channel_id=1, source_target_pairs={{0,8},{8,16},{16,24},{1,9},{9,17},{17,25},{2,10},{10,18},{18,26},{... | collective-permute-start | bytes 294920 | tf_op jit(solution)/shard_map/ppermute | solution.py:733
  16.2 1.9 %collective-permute-start.1 = (f32[3,32,256]{2,1,0:T(8,128)S(1)}, f32[3,32,256]{2,1,0:T(8,128)S(1)}, u32[]{:S(2)}, u32[]{:S(2)}) collective-permute-start(f32[3,32,256]{2,1,0:T(8,128)S(1)} %get-tuple-element.23.own_west), channel_id=1, source_target_pairs={{8,0},{16,8},{24,16},{9,1},{17,9},{25,17},{10,2},{18,10},{26,18},{... | collective-permute-start | bytes 294920 | tf_op jit(solution)/shard_map/ppermute | solution.py:733
  18.1 0.0 copy-start
  18.1 9.2 %advance_first.1.section_in = f32[3,96,32,256]{3,2,1,0:T(8,128)S(1)} custom-call(f32[3,96,32,256]{3,2,1,0:T(8,128)S(1)} %get-tuple-element.21.field), custom_call_target="tpu_custom_call" | custom-call | flops 1000000000 | bytes 37748736 | tf_op jit(solution)/shard_map/advance_first/pallas_call | solution.py:797
  27.4 0.0 collective-permute-done.ghost_low
  27.4 0.0 collective-permute-done.1.ghost_high
  27.4 2.8 %collective-permute-done.3.got_high = f32[480,1,256]{2,1,0:T(1,128)S(1)} collective-permute-done((f32[480,1,256]{2,1,0:T(1,128)S(1)}, f32[480,1,256]{2,1,0:T(1,128)S(1)}, u32[]{:S(2)}, u32[]{:S(2)}) %collective-permute-start.3) | collective-permute-done | bytes 491552 | tf_op jit(solution)/shard_map/ppermute | solution.py:733
  30.3 0.9 %collective-permute-done.2.got_low = f32[480,1,256]{2,1,0:T(1,128)S(1)} collective-permute-done((f32[480,1,256]{2,1,0:T(1,128)S(1)}, f32[480,1,256]{2,1,0:T(1,128)S(1)}, u32[]{:S(2)}, u32[]{:S(2)}) %collective-permute-start.2) | collective-permute-done | bytes 491552 | tf_op jit(solution)/shard_map/ppermute | solution.py:733
  31.2 0.0 copy-done
  31.2 6.5 %spread_sample.1 = (f32[3,96,32,256]{3,2,1,0:T(8,128)S(1)}, f32[3,96,32,256]{3,2,1,0:T(8,128)}, bf16[128,256,256]{2,1,0:T(8,128)(2,1)}, f32[480,1,256]{2,1,0:T(1...) custom-call(f32[3,96,32,256]{3,2,1,0:T(8,128)S(1)} %advance_first.1., ...), custom_call_target="tpu_custom_call", output_to_operand_aliasing={{0}: (0, {})} | custom-call | flops 2000000000 | bytes 37748736 | tf_op jit(solution)/shard_map/spread_sample/pallas_call | solution.py:808
  37.6 4.5 %all-to-all-start = ((f32[8,2,24,1,256]{4,3,2,1,0:T(1,128)}), f32[8,2,24,1,256]{4,3,2,1,0:T(1,128)S(1)}, u32[]{:S(2)}, u32[]{:S(2)}) async-start(f32[8,2,24,1,256]{4,3,2,1,0:T(1,128)} %get-tuple-element.38), calls=%async_computation | async-start | bytes 786432 | tf_op jit(solution)/shard_map/all_to_all | solution.py:826
  42.1 4.2 %collective-permute-start.7 = (f32[480,1,256]{2,1,0:T(1,128)S(1)}, f32[480,1,256]{2,1,0:T(1,128)S(1)}, u32[]{:S(2)}, u32[]{:S(2)}) collective-permute-start(f32[480,1,256]{2,1,0:T(1,128)S(1)} %get-tuple-element.34.own_low), channel_id=1, source_target_pairs={{0,7},{1,0},{2,1},{3,2},{4,3},{5,4},{6,5},{7,6},{8,15},{9,8},{10,9... | collective-permute-start | bytes 1474568 | tf_op jit(solution)/shard_map/ppermute | solution.py:733
  46.2 0.0 collective-permute-start.6
  46.2 7.5 %collective-permute-start.4 = (f32[3,32,256]{2,1,0:T(8,128)S(1)}, f32[3,32,256]{2,1,0:T(8,128)S(1)}, u32[]{:S(2)}, u32[]{:S(2)}) collective-permute-start(f32[3,32,256]{2,1,0:T(8,128)S(1)} %get-tuple-element.32.own_east), channel_id=1, source_target_pairs={{0,8},{8,16},{16,24},{1,9},{9,17},{17,25},{2,10},{10,18},{18,26},{... | collective-permute-start | bytes 294920 | tf_op jit(solution)/shard_map/ppermute | solution.py:733
  53.8 1.9 %collective-permute-start.5 = (f32[3,32,256]{2,1,0:T(8,128)S(1)}, f32[3,32,256]{2,1,0:T(8,128)S(1)}, u32[]{:S(2)}, u32[]{:S(2)}) collective-permute-start(f32[3,32,256]{2,1,0:T(8,128)S(1)} %get-tuple-element.33.own_west), channel_id=1, source_target_pairs={{8,0},{16,8},{24,16},{9,1},{17,9},{25,17},{10,2},{18,10},{26,18},{... | collective-permute-start | bytes 294920 | tf_op jit(solution)/shard_map/ppermute | solution.py:733
  55.7 12.9 %advance_second.1 = (f32[3,96,32,256]{3,2,1,0:T(8,128)}, f32[8,128]{1,0:T(8,128)S(1)}) custom-call(f32[3,96,32,256]{3,2,1,0:T(8,128)} %get-tuple-element.30.section_hbm, f32[3,96,32,256]{3,2,1,0:T(8,128)} %velocity.3), custom_call_target="tpu_custom_call" | custom-call | flops 1000000000 | bytes 37748736 | tf_op jit(solution)/shard_map/advance_second/pallas_call | solution.py:829
  68.6 0.0 collective-permute-done.4.after_low.ghost_low
  68.6 0.0 collective-permute-done.5.after_high.ghost_high
  68.6 0.0 all-to-all-done.parts
  68.6 0.8 share_force.1.after
  69.4 5.7 %all-to-all-start.1 = ((f32[8,24,1,256]{3,2,1,0:T(1,128)}), f32[8,24,1,256]{3,2,1,0:T(1,128)S(1)}, u32[]{:S(2)}, u32[]{:S(2)}) async-start(f32[8,24,1,256]{3,2,1,0:T(1,128)} %share_force.1.after), calls=%async_computation.1 | async-start | bytes 393216 | tf_op jit(solution)/shard_map/all_to_all | solution.py:851
  75.1 0.0 collective-permute-done.7.got_high
  75.1 0.0 collective-permute-done.6.got_low
  75.1 9.3 %spread_next.1 = f32[3,96,32,256]{3,2,1,0:T(8,128)} custom-call(f32[3,96,32,256]{3,2,1,0:T(8,128)} %get-tuple-element.31.following, f32[3,32,256]{2,1,0:T(8,128)S(1)} %copy-done, f32[3,32,256]{2,1,0:T(8,128)S(1)} %collective-permute-done.4.after_low.ghost_low, f32[3,32,256]{2,1,0:T(8,128)S(1)} %collective-permute-done.5.after_high.ghost_high, ...), custom_call_target="tpu_custom_call" | custom-call | flops 2000000000 | bytes 37748736 | tf_op jit(solution)/shard_map/spread_next/pallas_call | solution.py:853
  84.5 0.0 all-to-all-done.1
  84.5 0.7 copy.9
Async XLA Ops:
  6.7 23.6 %collective-permute-start.3 = (f32[480,1,256]{2,1,0:T(1,128)S(1)}, f32[480,1,256]{2,1,0:T(1,128)S(1)}, u32[]{:S(2)}, u32[]{:S(2)}) collective-permute-start(f32[480,1,256]{2,1,0:T(1,128)S(1)} %get-tuple-element.24.own_low), channel_id=1, source_target_pairs={{0,7},{1,0},{2,1},{3,2},{4,3},{5,4},{6,5},{7,6},{8,15},{9,8},{10,9... | collective-permute-start | bytes 1474568 | tf_op jit(solution)/shard_map/ppermute | solution.py:733
  11.8 19.3 %collective-permute-start.2 = (f32[480,1,256]{2,1,0:T(1,128)S(1)}, f32[480,1,256]{2,1,0:T(1,128)S(1)}, u32[]{:S(2)}, u32[]{:S(2)}) collective-permute-start(f32[480,1,256]{2,1,0:T(1,128)S(1)} %get-tuple-element.25.own_high), channel_id=1, source_target_pairs={{0,1},{1,2},{2,3},{3,4},{4,5},{5,6},{6,7},{7,0},{8,9},{9,10},{10,1... | collective-permute-start | bytes 1474568 | tf_op jit(solution)/shard_map/ppermute | solution.py:733
  11.8 15.6 %collective-permute-start = (f32[3,32,256]{2,1,0:T(8,128)S(1)}, f32[3,32,256]{2,1,0:T(8,128)S(1)}, u32[]{:S(2)}, u32[]{:S(2)}) collective-permute-start(f32[3,32,256]{2,1,0:T(8,128)S(1)} %get-tuple-element.22.own_east), channel_id=1, source_target_pairs={{0,8},{8,16},{16,24},{1,9},{9,17},{17,25},{2,10},{10,18},{18,26},{... | collective-permute-start | bytes 294920 | tf_op jit(solution)/shard_map/ppermute | solution.py:733
  16.2 11.2 %collective-permute-start.1 = (f32[3,32,256]{2,1,0:T(8,128)S(1)}, f32[3,32,256]{2,1,0:T(8,128)S(1)}, u32[]{:S(2)}, u32[]{:S(2)}) collective-permute-start(f32[3,32,256]{2,1,0:T(8,128)S(1)} %get-tuple-element.23.own_west), channel_id=1, source_target_pairs={{8,0},{16,8},{24,16},{9,1},{17,9},{25,17},{10,2},{18,10},{26,18},{... | collective-permute-start | bytes 294920 | tf_op jit(solution)/shard_map/ppermute | solution.py:733
  18.1 13.0 %copy-start = (f32[3,32,256]{2,1,0:T(8,128)S(1)}, f32[3,32,256]{2,1,0:T(8,128)}, u32[]{:S(2)}) copy-start(f32[3,32,256]{2,1,0:T(8,128)} %inflow.3) | copy-start | bytes 294916
  37.6 31.0 %all-to-all-start = ((f32[8,2,24,1,256]{4,3,2,1,0:T(1,128)}), f32[8,2,24,1,256]{4,3,2,1,0:T(1,128)S(1)}, u32[]{:S(2)}, u32[]{:S(2)}) async-start(f32[8,2,24,1,256]{4,3,2,1,0:T(1,128)} %get-tuple-element.38), calls=%async_computation | async-start | bytes 786432 | tf_op jit(solution)/shard_map/all_to_all | solution.py:826
  42.1 33.0 %collective-permute-start.7 = (f32[480,1,256]{2,1,0:T(1,128)S(1)}, f32[480,1,256]{2,1,0:T(1,128)S(1)}, u32[]{:S(2)}, u32[]{:S(2)}) collective-permute-start(f32[480,1,256]{2,1,0:T(1,128)S(1)} %get-tuple-element.34.own_low), channel_id=1, source_target_pairs={{0,7},{1,0},{2,1},{3,2},{4,3},{5,4},{6,5},{7,6},{8,15},{9,8},{10,9... | collective-permute-start | bytes 1474568 | tf_op jit(solution)/shard_map/ppermute | solution.py:733
  46.2 28.9 %collective-permute-start.6 = (f32[480,1,256]{2,1,0:T(1,128)S(1)}, f32[480,1,256]{2,1,0:T(1,128)S(1)}, u32[]{:S(2)}, u32[]{:S(2)}) collective-permute-start(f32[480,1,256]{2,1,0:T(1,128)S(1)} %get-tuple-element.35.own_high), channel_id=1, source_target_pairs={{0,1},{1,2},{2,3},{3,4},{4,5},{5,6},{6,7},{7,0},{8,9},{9,10},{10,1... | collective-permute-start | bytes 1474568 | tf_op jit(solution)/shard_map/ppermute | solution.py:733
  46.2 22.3 %collective-permute-start.4 = (f32[3,32,256]{2,1,0:T(8,128)S(1)}, f32[3,32,256]{2,1,0:T(8,128)S(1)}, u32[]{:S(2)}, u32[]{:S(2)}) collective-permute-start(f32[3,32,256]{2,1,0:T(8,128)S(1)} %get-tuple-element.32.own_east), channel_id=1, source_target_pairs={{0,8},{8,16},{16,24},{1,9},{9,17},{17,25},{2,10},{10,18},{18,26},{... | collective-permute-start | bytes 294920 | tf_op jit(solution)/shard_map/ppermute | solution.py:733
  53.8 14.8 %collective-permute-start.5 = (f32[3,32,256]{2,1,0:T(8,128)S(1)}, f32[3,32,256]{2,1,0:T(8,128)S(1)}, u32[]{:S(2)}, u32[]{:S(2)}) collective-permute-start(f32[3,32,256]{2,1,0:T(8,128)S(1)} %get-tuple-element.33.own_west), channel_id=1, source_target_pairs={{8,0},{16,8},{24,16},{9,1},{17,9},{25,17},{10,2},{18,10},{26,18},{... | collective-permute-start | bytes 294920 | tf_op jit(solution)/shard_map/ppermute | solution.py:733
  69.4 15.1 %all-to-all-start.1 = ((f32[8,24,1,256]{3,2,1,0:T(1,128)}), f32[8,24,1,256]{3,2,1,0:T(1,128)S(1)}, u32[]{:S(2)}, u32[]{:S(2)}) async-start(f32[8,24,1,256]{3,2,1,0:T(1,128)} %share_force.1.after), calls=%async_computation.1 | async-start | bytes 393216 | tf_op jit(solution)/shard_map/all_to_all | solution.py:851

commit v5 on v4

--- a/solution.py
+++ b/solution.py
@@ -172,11 +172,14 @@
             pack[n] = pack[n] + jnp.where(keep, rows[c], 0.0)
 
 
-def pack_edges(field, edge_west, edge_east, pack_low, pack_high):
-    cells_x, cells_y, depth = field.shape[1:]
+def pack_sides(field, edge_west, edge_east):
     for c in range(3):
         edge_west[c] = field[c, 0]
-        edge_east[c] = field[c, cells_x - 1]
+        edge_east[c] = field[c, field.shape[1] - 1]
+
+
+def pack_rows(field, low_out, high_out, first, last):
+    cells_x, cells_y = field.shape[1:3]
 
     def step(t, carry):
         cells = [(c, t * BATCH + k) for k in range(BATCH) for c in range(3)]
@@ -184,22 +187,21 @@
             (field[c, i, pl.ds(0, 1), :], field[c, i, pl.ds(cells_y - 1, 1), :]) for c, i in cells
         ]
         for (c, i), (low, high) in zip(cells, rows):
-            pack_low[c * cells_x + i] = low
-            pack_high[c * cells_x + i] = high
-        return carry
-
-    lax.fori_loop(0, cells_x // BATCH, step, 0)
-
-
-def load_sample(
+            low_out[c * cells_x + i] = low
+            high_out[c * cells_x + i] = high
+        return carry
+
+    lax.fori_loop(first // BATCH, last // BATCH, step, 0)
+
+
+def load_field(
     velocity, positions, tiles_hbm, coefs_hbm, counts,
-    field, pack_low, pack_high, edge_west, edge_east, weight_y, weight_z, strength, point_y, plan,
-    point_z, hubs, tiles, places, coefs, table, small_sems, plan_sem, sems,
+    field, edge_low, edge_high, edge_west, edge_east, strength, point_y, point_z, plan,
+    hubs, tiles, places, coefs, table, small_sems, plan_sem, sems,
 ):
     cells_x, cells_y, depth = field.shape[1:]
     records, points = coefs.shape
     chunks = cells_x // CHUNK
-    first_row = 3 * cells_x
     start = lax.axis_index("gx") * cells_x
 
     def chunk(k):
@@ -234,12 +236,6 @@
     plan_copy = pltpu.make_async_copy(table, plan, plan_sem)
     plan_copy.start()
 
-    def clear(n, carry):
-        for k in range(SUB):
-            pack_low[first_row + n * SUB + k] = jnp.zeros((1, points), jnp.float32)
-        return carry
-
-    lax.fori_loop(0, 3 * records // SUB, clear, 0)
     small[3].wait()
     for first in range(0, records, SUB):
         here = range(first, first + SUB)
@@ -249,7 +245,31 @@
         ]
         for r, (y, z, coef) in zip(here, rows):
             point_y[r], point_z[r], strength[r] = y, z, coef
+
+    def arrived(k, carry):
+        chunk(k).wait()
+        pack_rows(field, edge_low, edge_high, k * CHUNK, (k + 1) * CHUNK)
+        return carry
+
+    lax.fori_loop(0, chunks, arrived, 0)
+    pack_sides(field, edge_west, edge_east)
     plan_copy.wait()
+
+
+def clear_rows(pack, first, last):
+    def clear(n, carry):
+        for k in range(SUB):
+            pack[first + n * SUB + k] = jnp.zeros(pack.shape[1:], jnp.float32)
+        return carry
+
+    lax.fori_loop(0, (last - first) // SUB, clear, 0)
+
+
+def sample_first(field, plan, point_y, point_z, weight_y, weight_z, partial):
+    cells_y = field.shape[2]
+    total_y = cells_y * lax.axis_size("gy")
+    base = lax.axis_index("gy") * cells_y
+    clear_rows(partial, 0, partial.shape[0])
 
     def weigh(t, carry):
         made = []
@@ -266,33 +286,13 @@
 
     lax.fori_loop(0, (found(plan) + 1) // 2, weigh, 0)
 
-    def wait_to(ready, wanted):
-        def step(k, carry):
-            chunk(k).wait()
-            return carry
-
-        lax.fori_loop(ready, wanted, step, 0)
-        return jnp.maximum(ready, wanted)
-
-    def step(t, ready):
+    def step(t, carry):
         picks, keeps = group(plan, t)
-        ready = wait_to(ready, (picks[-1][2] + RAD) // CHUNK + 1)
         rows = sampled_rows(field, weight_y, weight_z, picks)
-        add_rows(pack_low, first_row, picks, rows, keeps)
-        return ready
-
-    ready = lax.fori_loop(0, groups_of(plan), step, jnp.int32(0))
-    wait_to(ready, chunks)
-
-    def copy_rows(t, carry):
-        rows = [first_row + t * SUB + k for k in range(SUB)]
-        values = [pack_low[n] for n in rows]
-        for n, value in zip(rows, values):
-            pack_high[n] = value
-        return carry
-
-    lax.fori_loop(0, 3 * records // SUB, copy_rows, 0)
-    pack_edges(field, edge_west, edge_east, pack_low, pack_high)
+        add_rows(partial, 0, picks, rows, keeps)
+        return carry
+
+    lax.fori_loop(0, groups_of(plan), step, 0)
 
 
 def fix_west(factor, target, own, inflow, ghost):
@@ -337,13 +337,12 @@
             target[c, i, rows, :] = value
 
 
-def slabs_of(weight_of, weight_z, strength, own, low, high, cells, scales, picks):
-    cells_x, cells_y, depth = cells
+def slabs_of(weight_of, weight_z, strength, first_row, own, low, high, cells_y, scales, picks):
     count = 3 * cells_y
     across = (((1,), (1,)), ((), ()))
     spread = []
     for (t, r, hub, cols), scale in zip(picks, scales):
-        rows = [3 * cells_x + 3 * r + c for c in range(3)]
+        rows = [first_row + 3 * r + c for c in range(3)]
         total = [own[n] + (low[n] + high[n]) for n in rows]
         speed = jnp.sqrt(total[0] * total[0] + total[1] * total[1] + total[2] * total[2])
         pull = strength[r] * (-scale) * speed
@@ -368,17 +367,17 @@
             field[c, hub + d, :, cols] = value
 
 
-def spread_group(t, scale, field, plan, points, own, low, high):
+def spread_group(t, scale, field, plan, points, first_row, own, low, high):
     picks, keeps = group(plan, t)
     scales = [jnp.where(keep, scale, 0.0) for keep in keeps]
-    slabs = slabs_of(*points, own, low, high, field.shape[1:], scales, picks)
+    slabs = slabs_of(*points, first_row, own, low, high, field.shape[2], scales, picks)
     for (_, _, hub, cols), slab in zip(picks, slabs):
         add_slab(field, slab, hub, cols)
 
 
 def spread_sample(
     section_in, inflow, ghost_low, ghost_high, own_low, own_high, own_west, own_east, got_low, got_high,
-    plan, weight_y, weight_z, strength,
+    own, part_low, part_high, plan, weight_y, weight_z, strength,
     section, section_out, stored_z, pack_low, pack_high, edge_west, edge_east,
     share_out, sem, sem_z,
 ):
@@ -412,20 +411,15 @@
 
     def spread_step(t, carry):
         points = (lambda n, r: weight_y[n], weight_z, strength)
-        spread_group(t, TIME_STEP, section, plan, points, own_low, got_low, got_high)
+        spread_group(t, TIME_STEP, section, plan, points, 0, own, part_low, part_high)
         return carry
 
     lax.fori_loop(0, groups_of(plan), spread_step, 0)
     copy = pltpu.make_async_copy(section, section_out, sem)
     copy.start()
-    pack_edges(section, edge_west, edge_east, pack_low, pack_high)
-
-    def clear(n, carry):
-        for k in range(SUB):
-            pack_low[first_row + n * SUB + k] = jnp.zeros_like(own_low[0])
-        return carry
-
-    lax.fori_loop(0, 3 * records // SUB, clear, 0)
+    pack_sides(section, edge_west, edge_east)
+    pack_rows(section, pack_low, pack_high, 0, cells_x)
+    clear_rows(pack_low, first_row, first_row + 3 * records)
 
     def sample_step(t, carry):
         picks, keeps = group(plan, t)
@@ -436,7 +430,7 @@
     lax.fori_loop(0, groups_of(plan), sample_step, 0)
 
     def copy_rows(r, carry):
-        old = [own_low[first_row + 3 * r + c] for c in range(3)]
+        old = [own[3 * r + c] for c in range(3)]
         new = [pack_low[first_row + 3 * r + c] for c in range(3)]
         for c in range(3):
             pack_high[first_row + 3 * r + c] = new[c]
@@ -548,7 +542,9 @@
         ready = wait_to(ready, (picks[-1][2] + RAD) // CHUNK + 1)
         sent = send_to(sent, (picks[0][2] - RAD) // CHUNK)
         points = (weight_of, weight_z, strength)
-        spread_group(t, factor * TIME_STEP, field, plan, points, own_low, got_low, got_high)
+        first_row = 3 * field.shape[1]
+        packs = (own_low, got_low, got_high)
+        spread_group(t, factor * TIME_STEP, field, plan, points, first_row, *packs)
         return ready, sent
 
     zero = jnp.int32(0)
@@ -649,7 +645,7 @@
         advance(i, k, factor, field, now, target, finish)
 
 
-def advance_first(field, section, shifts, slot_a, slot_b):
+def advance_first(field, after, section, shifts, slot_a, slot_b):
     fill_shifts(shifts)
     along_depth(0, field, shifts, slot_a)
 
@@ -733,11 +729,11 @@
     return lax.ppermute(x, axis, pairs)
 
 
-def exchange(pack_low, pack_high, edge_west, edge_east):
-    got_low = shifted(pack_high, "gy", 1, True)
-    got_high = shifted(pack_low, "gy", -1, True)
-    ghost_low = shifted(edge_east, "gx", 1, False)
-    ghost_high = shifted(edge_west, "gx", -1, False)
+def exchange(low, high, west, east):
+    got_low = shifted(high, "gy", 1, True)
+    got_high = shifted(low, "gy", -1, True)
+    ghost_low = shifted(east, "gx", 1, False)
+    ghost_high = shifted(west, "gx", -1, False)
     return ghost_low, ghost_high, got_low, got_high
 
 
@@ -766,18 +762,17 @@
     unit_sems = pltpu.SemaphoreType.DMA((units // TILES,))
     chunk_sems = pltpu.SemaphoreType.DMA((chunks,))
 
-    field, *own_a, weight_y, weight_z, strength, point_y, plan = pl.pallas_call(
-        load_sample,
+    halo = array((3 * cells_x, 1, points), f32)
+    field, *own_a, strength, point_y, point_z, plan = pl.pallas_call(
+        load_field,
         out_shape=(
-            held, pack, pack, edge, edge,
-            pltpu.VMEM(y_shape, f32), pltpu.VMEM(z_shape, jnp.bfloat16),
-            array(per_record, f32), array(per_record, i32),
+            held, halo, halo, edge, edge,
+            array(per_record, f32), array(per_record, i32), array(per_record, i32),
             array((SUB, units), i32),
         ),
         in_specs=[ANYWHERE] * 4 + [SCALAR],
-        out_specs=(WHOLE,) * 9 + (SCALAR,),
+        out_specs=(WHOLE,) * 8 + (SCALAR,),
         scratch_shapes=[
-            pltpu.VMEM(per_record, i32),
             pltpu.VMEM((records, LANES), i32),
             pltpu.VMEM((2, records), i32),
             pltpu.VMEM((2, records, points), i32),
@@ -788,22 +783,37 @@
             chunk_sems,
         ],
         compiler_params=params(),
-        cost_estimate=cost(2 * 10**9, 4 * size),
-        name="load_sample",
+        cost_estimate=cost(10**9, size),
+        name="load_field",
     )(streamed(velocity), streamed(positions), streamed(tiles), streamed(coefs), counts)
+    field = resident(field)
+    ghosts_a = exchange(*own_a)
+
+    weight_y, weight_z, partial = pl.pallas_call(
+        sample_first,
+        out_shape=(
+            pltpu.VMEM(y_shape, f32), pltpu.VMEM(z_shape, jnp.bfloat16),
+            array((3 * records, 1, points), f32),
+        ),
+        in_specs=[WHOLE, SCALAR, WHOLE, WHOLE],
+        out_specs=(WHOLE,) * 3,
+        compiler_params=params(),
+        cost_estimate=cost(2 * 10**9, size),
+        name="sample_first",
+    )(field, plan, point_y, point_z)
     weight_y, weight_z = resident(weight_y), resident(weight_z)
-    ghosts_a = exchange(*own_a)
+    parts_a = (partial, shifted(partial, "gy", 1, True), shifted(partial, "gy", -1, True))
 
     section = pl.pallas_call(
         advance_first,
         out_shape=held,
-        in_specs=[WHOLE],
+        in_specs=[WHOLE, ANYWHERE],
         out_specs=WHOLE,
         scratch_shapes=products,
         compiler_params=params(),
         cost_estimate=cost(10**9, 4 * size),
         name="advance_first",
-    )(resident(field))
+    )(field, partial)
 
     _, section, stored_z, *own_b, shares = pl.pallas_call(
         spread_sample,
@@ -812,7 +822,7 @@
             pack, pack, edge, edge,
             array((groups_y, 2, 3 * share, 1, points), f32),
         ),
-        in_specs=[WHOLE] * 10 + [SCALAR] + [WHOLE] * 3,
+        in_specs=[WHOLE] * 13 + [SCALAR] + [WHOLE] * 3,
         out_specs=(WHOLE,) + (ANYWHERE,) * 2 + (WHOLE,) * 5,
         input_output_aliases={0: 0},
         scratch_shapes=[pltpu.SemaphoreType.DMA, unit_sems],
@@ -821,7 +831,7 @@
         name="spread_sample",
     )(
         resident(section), inflow, *ghosts_a[:2], *own_a, *ghosts_a[2:],
-        plan, weight_y, weight_z, strength,
+        *parts_a, plan, weight_y, weight_z, strength,
     )
     shares = lax.all_to_all(shares, "gy", 0, 0)
     ghosts_b = exchange(*own_b)

time: 86.9 us -> 86.7 us (level); the launches traced: 85.2 us -> 86.6 us
  waiting for transfers between devices: 3.76 us -> 0.83 us
  starting transfers between devices: 35.2 us -> 37.2 us
  Pallas kernels: 44.1 us -> 45.6 us
    ppermute x8 -> x10, waiting for transfers between devices: 3.75 us -> 0.82 us  [shifted(): return lax.ppermute(x, axis, pairs)]
    pallas_call x2 -> x3, Pallas kernels: 14.7 us -> 16.1 us  [the longest x1 10.3 us: local(): pl.pallas_call(advance_first, out_shape=held, in_specs=[WHOLE, ANYWHERE],...]
    ppermute x8 -> x10, starting transfers between devices: 25 us -> 26 us  [shifted(): return lax.ppermute(x, axis, pairs)]
    all_to_all x1, starting transfers between devices: 4.45 us -> 5.41 us  [local(): shares = lax.all_to_all(shares, 'gy', 0, 0)]
  transfers between devices with their start and end apart: 10 -> 12, of which waited for: 2 -> 1; matrix products, arithmetic and copies ran while one was open for 0% -> 0% of each run, Pallas kernels for 38% -> 40%
where the time goes in v5:
time: 86.7 us; the launch traced here: 86.6 us
  Pallas kernels  45.6 us (53%)
  starting transfers between devices  37.2 us (43%)
  local copies, waits for them, and re-layouts  1.49 us (2%)
  between operations  1.45 us (2%)
    ppermute x10, starting transfers between devices, shifted(): return lax.ppermute(x, axis, pairs)  26 us
    pallas_call x1, Pallas kernels, local(): pl.pallas_call(advance_second, out_shape=(stored, array((SUB, LANES), f32...  12.9 us
    pallas_call x1, Pallas kernels, local(): pl.pallas_call(advance_first, out_shape=held, in_specs=[WHOLE, ANYWHERE],...  10.3 us
    pallas_call x1, Pallas kernels, local(): pl.pallas_call(spread_next, out_shape=stored, in_specs=[ANYWHERE] + [WHOL...  9.34 us
    pallas_call x1, Pallas kernels, local(): pl.pallas_call(spread_sample, out_shape=(held, stored, pltpu.HBM(z_shape,...  6.54 us
    all_to_all x1, starting transfers between devices, local(): all_forces = lax.all_to_all(forces, 'gy', 0, 0)  5.7 us
    all_to_all x1, starting transfers between devices, local(): shares = lax.all_to_all(shares, 'gy', 0, 0)  5.41 us
    pallas_call x1, Pallas kernels, local(): pl.pallas_call(load_field, out_shape=(held, halo, halo, edge, edge, array...  4.66 us
  transfers between devices with their start and end apart: 12, of which 1 were waited for; matrix products, arithmetic and copies ran while one was open for 0% of the time, Pallas kernels for 40%

profile of v5, /device:TPU:1, one launch (start us, length us, event | category | flops | bytes accessed | tf_op | source)
XLA Modules:
  0.0 86.6 jit_solution(9089554048878392839)
XLA Ops:
  1.3 4.7 %load_field.1 = (f32[3,96,32,256]{3,2,1,0:T(8,128)S(1)}, f32[288,1,256]{2,1,0:T(1,128)S(1)}, f32[288,1,256]{2,1,0:T(1,128)S(1)}, f32[3,32,256]{2,1,0:T(8,128)S(1...) custom-call(f32[3,96,32,256]{3,2,1,0:T(8,128)} %velocity.3, ...), custom_call_target="tpu_custom_call" | custom-call | flops 1000000000 | bytes 9437184 | tf_op jit(solution)/shard_map/load_field/pallas_call | solution.py:766
  5.9 4.5 %collective-permute-start = (f32[3,32,256]{2,1,0:T(8,128)S(1)}, f32[3,32,256]{2,1,0:T(8,128)S(1)}, u32[]{:S(2)}, u32[]{:S(2)}) collective-permute-start(f32[3,32,256]{2,1,0:T(8,128)S(1)} %get-tuple-element.28.own_east), channel_id=1, source_target_pairs={{0,8},{8,16},{16,24},{1,9},{9,17},{17,25},{2,10},{10,18},{18,26},{... | collective-permute-start | bytes 294920 | tf_op jit(solution)/shard_map/ppermute | solution.py:729
  10.5 4.3 %collective-permute-start.3 = (f32[288,1,256]{2,1,0:T(1,128)S(1)}, f32[288,1,256]{2,1,0:T(1,128)S(1)}, u32[]{:S(2)}, u32[]{:S(2)}) collective-permute-start(f32[288,1,256]{2,1,0:T(1,128)S(1)} %get-tuple-element.30.own_low), channel_id=1, source_target_pairs={{0,7},{1,0},{2,1},{3,2},{4,3},{5,4},{6,5},{7,6},{8,15},{9,8},{10,9... | collective-permute-start | bytes 884744 | tf_op jit(solution)/shard_map/ppermute | solution.py:729
  14.8 0.0 collective-permute-start.2
  14.8 1.2 %sample_first.1 = (f32[128,32,256]{2,1,0:T(8,128)S(1)}, bf16[128,256,256]{2,1,0:T(8,128)(2,1)S(1)}, f32[192,1,256]{2,1,0:T(1,128)S(1)}) custom-call(f32[3,96,32,256]{3,2,1,0:T(8,128)S(1)} %get-tuple-element.23.field, s32[8,128]{1,0:T(8,128)S(1)} %get-tuple-element.24.plan, s32[64,1,256]{2,1,0:T(1,128)S(1)} %get-tuple-element.25.point_y, ...), custom_call_target="tpu_custom_call" | custom-call | flops 2000000000 | bytes 9437184 | tf_op jit(solution)/shard_map/sample_first/pallas_call | solution.py:792
  16.0 3.8 %collective-permute-start.5 = (f32[192,1,256]{2,1,0:T(1,128)S(1)}, f32[192,1,256]{2,1,0:T(1,128)S(1)}, u32[]{:S(2)}, u32[]{:S(2)}) collective-permute-start(f32[192,1,256]{2,1,0:T(1,128)S(1)} %get-tuple-element.27.after.own), channel_id=1, source_target_pairs={{0,7},{1,0},{2,1},{3,2},{4,3},{5,4},{6,5},{7,6},{8,15},{9,8},{10,9... | collective-permute-start | bytes 589832 | tf_op jit(solution)/shard_map/ppermute | solution.py:729
  19.8 0.0 collective-permute-start.4
  19.8 0.0 collective-permute-done.ghost_low
  19.8 0.0 copy-start.2
  19.8 2.6 %collective-permute-start.1 = (f32[3,32,256]{2,1,0:T(8,128)S(1)}, f32[3,32,256]{2,1,0:T(8,128)S(1)}, u32[]{:S(2)}, u32[]{:S(2)}) collective-permute-start(f32[3,32,256]{2,1,0:T(8,128)S(1)} %get-tuple-element.29.own_west), channel_id=1, source_target_pairs={{8,0},{16,8},{24,16},{9,1},{17,9},{25,17},{10,2},{18,10},{26,18},{... | collective-permute-start | bytes 294920 | tf_op jit(solution)/shard_map/ppermute | solution.py:729
  22.4 10.3 %advance_first.1.section_in = f32[3,96,32,256]{3,2,1,0:T(8,128)S(1)} custom-call(f32[3,96,32,256]{3,2,1,0:T(8,128)S(1)} %get-tuple-element.23.field, f32[192,1,256]{2,1,0:T(1,128)S(1)} %get-tuple-element.27.after.own), custom_call_target="tpu_custom_call" | custom-call | flops 1000000000 | bytes 37748736 | tf_op jit(solution)/shard_map/advance_first/pallas_call | solution.py:807
  32.7 0.0 collective-permute-done.1.ghost_high
  32.7 0.0 collective-permute-done.5.part_high
  32.7 0.8 collective-permute-done.4.part_low
  33.5 0.0 collective-permute-done.3.got_high
  33.5 0.0 collective-permute-done.2.got_low
  33.5 0.0 copy-done.2
  33.5 6.5 %spread_sample.1 = (f32[3,96,32,256]{3,2,1,0:T(8,128)S(1)}, f32[3,96,32,256]{3,2,1,0:T(8,128)}, bf16[128,256,256]{2,1,0:T(8,128)(2,1)}, f32[480,1,256]{2,1,0:T(1...) custom-call(f32[3,96,32,256]{3,2,1,0:T(8,128)S(1)} %advance_first.1., ...), custom_call_target="tpu_custom_call", output_to_operand_aliasing={{0}: (0, {})} | custom-call | flops 2000000000 | bytes 37748736 | tf_op jit(solution)/shard_map/spread_sample/pallas_call | solution.py:818
  40.0 0.0 copy-start
  40.0 0.8 copy-done
  40.8 5.4 %all-to-all-start = ((f32[8,2,24,1,256]{4,3,2,1,0:T(1,128)}), f32[8,2,24,1,256]{4,3,2,1,0:T(1,128)S(1)}, u32[]{:S(2)}, u32[]{:S(2)}) async-start(f32[8,2,24,1,256]{4,3,2,1,0:T(1,128)} %get-tuple-element.42), calls=%async_computation | async-start | bytes 786432 | tf_op jit(solution)/shard_map/all_to_all | solution.py:836
  46.2 4.2 %collective-permute-start.9 = (f32[480,1,256]{2,1,0:T(1,128)S(1)}, f32[480,1,256]{2,1,0:T(1,128)S(1)}, u32[]{:S(2)}, u32[]{:S(2)}) collective-permute-start(f32[480,1,256]{2,1,0:T(1,128)S(1)} %get-tuple-element.39.own_low), channel_id=1, source_target_pairs={{0,7},{1,0},{2,1},{3,2},{4,3},{5,4},{6,5},{7,6},{8,15},{9,8},{10,9... | collective-permute-start | bytes 1474568 | tf_op jit(solution)/shard_map/ppermute | solution.py:729
  50.4 0.0 collective-permute-start.8
  50.4 4.7 %collective-permute-start.6 = (f32[3,32,256]{2,1,0:T(8,128)S(1)}, f32[3,32,256]{2,1,0:T(8,128)S(1)}, u32[]{:S(2)}, u32[]{:S(2)}) collective-permute-start(f32[3,32,256]{2,1,0:T(8,128)S(1)} %get-tuple-element.37.own_east), channel_id=1, source_target_pairs={{0,8},{8,16},{16,24},{1,9},{9,17},{17,25},{2,10},{10,18},{18,26},{... | collective-permute-start | bytes 294920 | tf_op jit(solution)/shard_map/ppermute | solution.py:729
  55.1 1.9 %collective-permute-start.7 = (f32[3,32,256]{2,1,0:T(8,128)S(1)}, f32[3,32,256]{2,1,0:T(8,128)S(1)}, u32[]{:S(2)}, u32[]{:S(2)}) collective-permute-start(f32[3,32,256]{2,1,0:T(8,128)S(1)} %get-tuple-element.38.own_west), channel_id=1, source_target_pairs={{8,0},{16,8},{24,16},{9,1},{17,9},{25,17},{10,2},{18,10},{26,18},{... | collective-permute-start | bytes 294920 | tf_op jit(solution)/shard_map/ppermute | solution.py:729
  57.0 0.0 copy-start.1
  57.1 12.9 %advance_second.1 = (f32[3,96,32,256]{3,2,1,0:T(8,128)}, f32[8,128]{1,0:T(8,128)S(1)}) custom-call(f32[3,96,32,256]{3,2,1,0:T(8,128)} %get-tuple-element.35.section_hbm, f32[3,96,32,256]{3,2,1,0:T(8,128)} %velocity.3), custom_call_target="tpu_custom_call" | custom-call | flops 1000000000 | bytes 37748736 | tf_op jit(solution)/shard_map/advance_second/pallas_call | solution.py:839
  69.9 0.0 collective-permute-done.6.after_low.ghost_low
  69.9 0.0 collective-permute-done.7.after_high.ghost_high
  70.0 0.0 all-to-all-done.parts
  70.0 0.8 share_force.1.after
  70.8 5.7 %all-to-all-start.1 = ((f32[8,24,1,256]{3,2,1,0:T(1,128)}), f32[8,24,1,256]{3,2,1,0:T(1,128)S(1)}, u32[]{:S(2)}, u32[]{:S(2)}) async-start(f32[8,24,1,256]{3,2,1,0:T(1,128)} %share_force.1.after), calls=%async_computation.1 | async-start | bytes 393216 | tf_op jit(solution)/shard_map/all_to_all | solution.py:861
  76.5 0.0 collective-permute-done.9.got_high
  76.5 0.0 collective-permute-done.8.got_low
  76.5 0.0 copy-done.1
  76.5 9.3 %spread_next.1 = f32[3,96,32,256]{3,2,1,0:T(8,128)} custom-call(f32[3,96,32,256]{3,2,1,0:T(8,128)} %get-tuple-element.36.following, f32[3,32,256]{2,1,0:T(8,128)S(1)} %copy-done.2, f32[3,32,256]{2,1,0:T(8,128)S(1)} %collective-permute-done.6.after_low.ghost_low, f32[3,32,256]{2,1,0:T(8,128)S(1)} %collective-permute-done.7.after_high.ghost_high, ...), custom_call_target="tpu_custom_call" | custom-call | flops 2000000000 | bytes 37748736 | tf_op jit(solution)/shard_map/spread_next/pallas_call | solution.py:863
  85.8 0.0 all-to-all-done.1
  85.9 0.7 copy.9
Async XLA Ops:
  5.9 13.8 %collective-permute-start = (f32[3,32,256]{2,1,0:T(8,128)S(1)}, f32[3,32,256]{2,1,0:T(8,128)S(1)}, u32[]{:S(2)}, u32[]{:S(2)}) collective-permute-start(f32[3,32,256]{2,1,0:T(8,128)S(1)} %get-tuple-element.28.own_east), channel_id=1, source_target_pairs={{0,8},{8,16},{16,24},{1,9},{9,17},{17,25},{2,10},{10,18},{18,26},{... | collective-permute-start | bytes 294920 | tf_op jit(solution)/shard_map/ppermute | solution.py:729
  10.5 23.0 %collective-permute-start.3 = (f32[288,1,256]{2,1,0:T(1,128)S(1)}, f32[288,1,256]{2,1,0:T(1,128)S(1)}, u32[]{:S(2)}, u32[]{:S(2)}) collective-permute-start(f32[288,1,256]{2,1,0:T(1,128)S(1)} %get-tuple-element.30.own_low), channel_id=1, source_target_pairs={{0,7},{1,0},{2,1},{3,2},{4,3},{5,4},{6,5},{7,6},{8,15},{9,8},{10,9... | collective-permute-start | bytes 884744 | tf_op jit(solution)/shard_map/ppermute | solution.py:729
  14.8 18.7 %collective-permute-start.2 = (f32[288,1,256]{2,1,0:T(1,128)S(1)}, f32[288,1,256]{2,1,0:T(1,128)S(1)}, u32[]{:S(2)}, u32[]{:S(2)}) collective-permute-start(f32[288,1,256]{2,1,0:T(1,128)S(1)} %get-tuple-element.31.own_high), channel_id=1, source_target_pairs={{0,1},{1,2},{2,3},{3,4},{4,5},{5,6},{6,7},{7,0},{8,9},{9,10},{10,1... | collective-permute-start | bytes 884744 | tf_op jit(solution)/shard_map/ppermute | solution.py:729
  16.0 16.7 %collective-permute-start.5 = (f32[192,1,256]{2,1,0:T(1,128)S(1)}, f32[192,1,256]{2,1,0:T(1,128)S(1)}, u32[]{:S(2)}, u32[]{:S(2)}) collective-permute-start(f32[192,1,256]{2,1,0:T(1,128)S(1)} %get-tuple-element.27.after.own), channel_id=1, source_target_pairs={{0,7},{1,0},{2,1},{3,2},{4,3},{5,4},{6,5},{7,6},{8,15},{9,8},{10,9... | collective-permute-start | bytes 589832 | tf_op jit(solution)/shard_map/ppermute | solution.py:729
  19.8 13.7 %collective-permute-start.4 = (f32[192,1,256]{2,1,0:T(1,128)S(1)}, f32[192,1,256]{2,1,0:T(1,128)S(1)}, u32[]{:S(2)}, u32[]{:S(2)}) collective-permute-start(f32[192,1,256]{2,1,0:T(1,128)S(1)} %get-tuple-element.27.after.own), channel_id=1, source_target_pairs={{0,1},{1,2},{2,3},{3,4},{4,5},{5,6},{6,7},{7,0},{8,9},{9,10},{10,1... | collective-permute-start | bytes 589832 | tf_op jit(solution)/shard_map/ppermute | solution.py:729
  19.8 13.7 %copy-start.2 = (f32[3,32,256]{2,1,0:T(8,128)S(1)}, f32[3,32,256]{2,1,0:T(8,128)}, u32[]{:S(2)}) copy-start(f32[3,32,256]{2,1,0:T(8,128)} %inflow.3) | copy-start | bytes 294916
  19.8 12.9 %collective-permute-start.1 = (f32[3,32,256]{2,1,0:T(8,128)S(1)}, f32[3,32,256]{2,1,0:T(8,128)S(1)}, u32[]{:S(2)}, u32[]{:S(2)}) collective-permute-start(f32[3,32,256]{2,1,0:T(8,128)S(1)} %get-tuple-element.29.own_west), channel_id=1, source_target_pairs={{8,0},{16,8},{24,16},{9,1},{17,9},{25,17},{10,2},{18,10},{26,18},{... | collective-permute-start | bytes 294920 | tf_op jit(solution)/shard_map/ppermute | solution.py:729
  40.0 0.8 copy-start
  40.8 29.1 %all-to-all-start = ((f32[8,2,24,1,256]{4,3,2,1,0:T(1,128)}), f32[8,2,24,1,256]{4,3,2,1,0:T(1,128)S(1)}, u32[]{:S(2)}, u32[]{:S(2)}) async-start(f32[8,2,24,1,256]{4,3,2,1,0:T(1,128)} %get-tuple-element.42), calls=%async_computation | async-start | bytes 786432 | tf_op jit(solution)/shard_map/all_to_all | solution.py:836
  46.2 30.2 %collective-permute-start.9 = (f32[480,1,256]{2,1,0:T(1,128)S(1)}, f32[480,1,256]{2,1,0:T(1,128)S(1)}, u32[]{:S(2)}, u32[]{:S(2)}) collective-permute-start(f32[480,1,256]{2,1,0:T(1,128)S(1)} %get-tuple-element.39.own_low), channel_id=1, source_target_pairs={{0,7},{1,0},{2,1},{3,2},{4,3},{5,4},{6,5},{7,6},{8,15},{9,8},{10,9... | collective-permute-start | bytes 1474568 | tf_op jit(solution)/shard_map/ppermute | solution.py:729
  50.4 26.1 %collective-permute-start.8 = (f32[480,1,256]{2,1,0:T(1,128)}, f32[480,1,256]{2,1,0:T(1,128)S(1)}, u32[]{:S(2)}, u32[]{:S(2)}) collective-permute-start(f32[480,1,256]{2,1,0:T(1,128)} %copy-done), channel_id=1, source_target_pairs={{0,1},{1,2},{2,3},{3,4},{4,5},{5,6},{6,7},{7,0},{8,9},{9,10},{10,1... | collective-permute-start | bytes 1474568 | tf_op jit(solution)/shard_map/ppermute | solution.py:729
  50.4 19.5 %collective-permute-start.6 = (f32[3,32,256]{2,1,0:T(8,128)S(1)}, f32[3,32,256]{2,1,0:T(8,128)S(1)}, u32[]{:S(2)}, u32[]{:S(2)}) collective-permute-start(f32[3,32,256]{2,1,0:T(8,128)S(1)} %get-tuple-element.37.own_east), channel_id=1, source_target_pairs={{0,8},{8,16},{16,24},{1,9},{9,17},{17,25},{2,10},{10,18},{18,26},{... | collective-permute-start | bytes 294920 | tf_op jit(solution)/shard_map/ppermute | solution.py:729
  55.1 14.8 %collective-permute-start.7 = (f32[3,32,256]{2,1,0:T(8,128)S(1)}, f32[3,32,256]{2,1,0:T(8,128)S(1)}, u32[]{:S(2)}, u32[]{:S(2)}) collective-permute-start(f32[3,32,256]{2,1,0:T(8,128)S(1)} %get-tuple-element.38.own_west), channel_id=1, source_target_pairs={{8,0},{16,8},{24,16},{9,1},{17,9},{25,17},{10,2},{18,10},{26,18},{... | collective-permute-start | bytes 294920 | tf_op jit(solution)/shard_map/ppermute | solution.py:729
  57.0 19.4 %copy-start.1 = (f32[480,1,256]{2,1,0:T(1,128)S(1)}, f32[480,1,256]{2,1,0:T(1,128)}, u32[]{:S(2)}) copy-start(f32[480,1,256]{2,1,0:T(1,128)} %copy-done) | copy-start | bytes 1474564
  70.8 15.1 %all-to-all-start.1 = ((f32[8,24,1,256]{3,2,1,0:T(1,128)}), f32[8,24,1,256]{3,2,1,0:T(1,128)S(1)}, u32[]{:S(2)}, u32[]{:S(2)}) async-start(f32[8,24,1,256]{3,2,1,0:T(1,128)} %share_force.1.after), calls=%async_computation.1 | async-start | bytes 393216 | tf_op jit(solution)/shard_map/all_to_all | solution.py:861

commit v6 on v4

--- a/solution.py
+++ b/solution.py
@@ -574,21 +574,14 @@
     difference = (upper - lower).astype(shifts.dtype)
     shifts[0:depth] = difference
     shifts[depth : 2 * depth] = difference
-    shifts[2 * depth : 3 * depth] = (upper + lower).astype(shifts.dtype)
 
 
 def along_depth(i, field, shifts, slot):
-    depth = shifts.shape[1]
     x = jnp.concatenate([field[c, i + k] for k in range(PLANES) for c in range(3)], axis=0)
     high = x.astype(jnp.bfloat16)
     low = (x - high.astype(jnp.float32)).astype(jnp.bfloat16)
-    slot[0] = jnp.dot(
-        jnp.concatenate([high, low], axis=1),
-        shifts[0 : 2 * depth],
-        preferred_element_type=jnp.float32,
-    )
-    slot[1] = jnp.dot(
-        high, shifts[2 * depth : 3 * depth], preferred_element_type=jnp.float32
+    slot[...] = jnp.dot(
+        jnp.concatenate([high, low], axis=1), shifts[...], preferred_element_type=jnp.float32
     )
 
 
@@ -596,7 +589,8 @@
     cells_x, cells_y, depth = field.shape[1:]
     groups, halves = cells_y // SUB, depth // LANES
     row = lax.broadcasted_iota(jnp.int32, (SUB, LANES), 0)
-    first_row, last_row = row == 0, row == SUB - 1
+    lane = lax.broadcasted_iota(jnp.int32, (SUB, LANES), 1)
+    first_row, last_row, first_lane = row == 0, row == SUB - 1, lane == 0
     spread = factor * TIME_STEP * VISCOSITY
     centre = factor * (1.0 - 6.0 * TIME_STEP * VISCOSITY)
     zero = jnp.zeros((SUB, LANES), jnp.float32)
@@ -611,11 +605,12 @@
 
     values = []
     for g in range(groups):
+        turned = {}
         for h in range(halves):
             rows, cols = pl.ds(g * SUB, SUB), pl.ds(h * LANES, LANES)
             q = [at(c, g, h) for c in range(3)]
             speeds = [(0.5 * factor * TIME_STEP) * x for x in q]
-            less = [spread - s for s in speeds[:2]]
+            less = [spread - s for s in speeds]
             more = [spread + s for s in speeds[:2]]
             if g == 0:
                 more[1] = jnp.where(first_row, zero, more[1])
@@ -634,7 +629,10 @@
                 total += field[c, east, rows, cols] * less[0]
                 total += field[c, west, rows, cols] * more[0]
                 total += above * less[1] + below * more[1]
-                total += spread * slot[1, place, cols] - speeds[2] * slot[0, place, cols]
+                lower = pltpu.roll(x, 1, 1)
+                turned[c, h] = lower
+                lower = jnp.where(first_lane, zero if h == 0 else turned[c, h - 1], lower)
+                total += slot[place, cols] * less[2] + (2.0 * spread) * lower
                 values.append((c, rows, cols, finish(c, here, rows, cols, total)))
         if g % 2 == 1 or g + 1 == groups:
             for c, rows, cols, value in values:
@@ -761,8 +759,8 @@
     units = records * (depth // LANES)
     y_shape, z_shape = (units, cells_y, points), (units, 2 * LANES, points)
     z_bytes = 2 * math.prod(z_shape)
-    products = [pltpu.VMEM((3 * depth, depth), jnp.bfloat16)]
-    products += [pltpu.VMEM((2, 3 * PLANES * cells_y, depth), f32)] * 2
+    products = [pltpu.VMEM((2 * depth, depth), jnp.bfloat16)]
+    products += [pltpu.VMEM((3 * PLANES * cells_y, depth), f32)] * 2
     unit_sems = pltpu.SemaphoreType.DMA((units // TILES,))
     chunk_sems = pltpu.SemaphoreType.DMA((chunks,))
 

time: 86.9 us -> 85.4 us (0.983); the launches traced: 85.2 us -> 85.1 us
  starting transfers between devices: 35.2 us -> 36.8 us
  Pallas kernels: 44.1 us -> 43.1 us
    ppermute x8, starting transfers between devices: 25 us -> 27.6 us  [shifted(): return lax.ppermute(x, axis, pairs)]
    all_to_all x1, starting transfers between devices: 4.45 us -> 3.49 us  [local(): shares = lax.all_to_all(shares, 'gy', 0, 0)]
  transfers between devices with their start and end apart: 10 -> 10, of which waited for: 2 -> 1; matrix products, arithmetic and copies ran while one was open for 0% -> 0% of each run, Pallas kernels for 38% -> 37%
where the time goes in v6:
time: 85.4 us; the launch traced here: 85.1 us
  Pallas kernels  43.1 us (50%)
  starting transfers between devices  36.8 us (43%)
  waiting for transfers between devices  3.1 us (4%)
  between operations  1.43 us (2%)
    ppermute x8, starting transfers between devices, shifted(): return lax.ppermute(x, axis, pairs)  27.6 us
    pallas_call x1, Pallas kernels, local(): pl.pallas_call(advance_second, out_shape=(stored, array((SUB, LANES), f32...  12.2 us
    pallas_call x1, Pallas kernels, local(): pl.pallas_call(spread_next, out_shape=stored, in_specs=[ANYWHERE] + [WHOL...  9.33 us
    pallas_call x1, Pallas kernels, local(): pl.pallas_call(advance_first, out_shape=held, in_specs=[WHOLE], out_specs...  8.87 us
    pallas_call x1, Pallas kernels, local(): pl.pallas_call(spread_sample, out_shape=(held, stored, pltpu.HBM(z_shape,...  6.45 us
    all_to_all x1, starting transfers between devices, local(): all_forces = lax.all_to_all(forces, 'gy', 0, 0)  5.72 us
    pallas_call x1, Pallas kernels, local(): pl.pallas_call(load_sample, out_shape=(held, pack, pack, edge, edge, pltp...  5.42 us
    all_to_all x1, starting transfers between devices, local(): shares = lax.all_to_all(shares, 'gy', 0, 0)  3.49 us
  transfers between devices with their start and end apart: 10, of which 1 were waited for; matrix products, arithmetic and copies ran while one was open for 0% of the time, Pallas kernels for 37%

profile of v6, /device:TPU:1, one launch (start us, length us, event | category | flops | bytes accessed | tf_op | source)
XLA Modules:
  0.0 85.1 jit_solution(8816036251942492162)
XLA Ops:
  1.3 5.4 %load_sample.1 = (f32[3,96,32,256]{3,2,1,0:T(8,128)S(1)}, f32[480,1,256]{2,1,0:T(1,128)S(1)}, f32[480,1,256]{2,1,0:T(1,128)S(1)}, f32[3,32,256]{2,1,0:T(8,128)S(...) custom-call(f32[3,96,32,256]{3,2,1,0:T(8,128)} %velocity.3, ...), custom_call_target="tpu_custom_call" | custom-call | flops 2000000000 | bytes 37748736 | tf_op jit(solution)/shard_map/load_sample/pallas_call | solution.py:767
  6.7 4.8 %collective-permute-start.3 = (f32[480,1,256]{2,1,0:T(1,128)S(1)}, f32[480,1,256]{2,1,0:T(1,128)S(1)}, u32[]{:S(2)}, u32[]{:S(2)}) collective-permute-start(f32[480,1,256]{2,1,0:T(1,128)S(1)} %get-tuple-element.24.own_low), channel_id=1, source_target_pairs={{0,7},{1,0},{2,1},{3,2},{4,3},{5,4},{6,5},{7,6},{8,15},{9,8},{10,9... | collective-permute-start | bytes 1474568 | tf_op jit(solution)/shard_map/ppermute | solution.py:731
  11.5 0.0 collective-permute-start.2
  11.5 4.7 %collective-permute-start = (f32[3,32,256]{2,1,0:T(8,128)S(1)}, f32[3,32,256]{2,1,0:T(8,128)S(1)}, u32[]{:S(2)}, u32[]{:S(2)}) collective-permute-start(f32[3,32,256]{2,1,0:T(8,128)S(1)} %get-tuple-element.22.own_east), channel_id=1, source_target_pairs={{0,8},{8,16},{16,24},{1,9},{9,17},{17,25},{2,10},{10,18},{18,26},{... | collective-permute-start | bytes 294920 | tf_op jit(solution)/shard_map/ppermute | solution.py:731
  16.2 3.0 %collective-permute-start.1 = (f32[3,32,256]{2,1,0:T(8,128)S(1)}, f32[3,32,256]{2,1,0:T(8,128)S(1)}, u32[]{:S(2)}, u32[]{:S(2)}) collective-permute-start(f32[3,32,256]{2,1,0:T(8,128)S(1)} %get-tuple-element.23.own_west), channel_id=1, source_target_pairs={{8,0},{16,8},{24,16},{9,1},{17,9},{25,17},{10,2},{18,10},{26,18},{... | collective-permute-start | bytes 294920 | tf_op jit(solution)/shard_map/ppermute | solution.py:731
  19.2 0.0 copy-start
  19.2 8.9 %advance_first.1.section_in = f32[3,96,32,256]{3,2,1,0:T(8,128)S(1)} custom-call(f32[3,96,32,256]{3,2,1,0:T(8,128)S(1)} %get-tuple-element.21.field), custom_call_target="tpu_custom_call" | custom-call | flops 1000000000 | bytes 37748736 | tf_op jit(solution)/shard_map/advance_first/pallas_call | solution.py:795
  28.1 0.0 collective-permute-done.ghost_low
  28.1 0.0 collective-permute-done.1.ghost_high
  28.1 0.0 collective-permute-done.3.got_high
  28.1 3.1 %collective-permute-done.2.got_low = f32[480,1,256]{2,1,0:T(1,128)S(1)} collective-permute-done((f32[480,1,256]{2,1,0:T(1,128)S(1)}, f32[480,1,256]{2,1,0:T(1,128)S(1)}, u32[]{:S(2)}, u32[]{:S(2)}) %collective-permute-start.2) | collective-permute-done | bytes 491552 | tf_op jit(solution)/shard_map/ppermute | solution.py:731
  31.2 0.0 copy-done
  31.2 6.5 %spread_sample.1 = (f32[3,96,32,256]{3,2,1,0:T(8,128)S(1)}, f32[3,96,32,256]{3,2,1,0:T(8,128)}, bf16[128,256,256]{2,1,0:T(8,128)(2,1)}, f32[480,1,256]{2,1,0:T(1...) custom-call(f32[3,96,32,256]{3,2,1,0:T(8,128)S(1)} %advance_first.1., ...), custom_call_target="tpu_custom_call", output_to_operand_aliasing={{0}: (0, {})} | custom-call | flops 2000000000 | bytes 37748736 | tf_op jit(solution)/shard_map/spread_sample/pallas_call | solution.py:806
  37.6 3.5 %all-to-all-start = ((f32[8,2,24,1,256]{4,3,2,1,0:T(1,128)}), f32[8,2,24,1,256]{4,3,2,1,0:T(1,128)S(1)}, u32[]{:S(2)}, u32[]{:S(2)}) async-start(f32[8,2,24,1,256]{4,3,2,1,0:T(1,128)} %get-tuple-element.38), calls=%async_computation | async-start | bytes 786432 | tf_op jit(solution)/shard_map/all_to_all | solution.py:824
  41.1 4.2 %collective-permute-start.7 = (f32[480,1,256]{2,1,0:T(1,128)S(1)}, f32[480,1,256]{2,1,0:T(1,128)S(1)}, u32[]{:S(2)}, u32[]{:S(2)}) collective-permute-start(f32[480,1,256]{2,1,0:T(1,128)S(1)} %get-tuple-element.34.own_low), channel_id=1, source_target_pairs={{0,7},{1,0},{2,1},{3,2},{4,3},{5,4},{6,5},{7,6},{8,15},{9,8},{10,9... | collective-permute-start | bytes 1474568 | tf_op jit(solution)/shard_map/ppermute | solution.py:731
  45.3 0.0 collective-permute-start.6
  45.3 9.0 %collective-permute-start.4 = (f32[3,32,256]{2,1,0:T(8,128)S(1)}, f32[3,32,256]{2,1,0:T(8,128)S(1)}, u32[]{:S(2)}, u32[]{:S(2)}) collective-permute-start(f32[3,32,256]{2,1,0:T(8,128)S(1)} %get-tuple-element.32.own_east), channel_id=1, source_target_pairs={{0,8},{8,16},{16,24},{1,9},{9,17},{17,25},{2,10},{10,18},{18,26},{... | collective-permute-start | bytes 294920 | tf_op jit(solution)/shard_map/ppermute | solution.py:731
  54.3 1.9 %collective-permute-start.5 = (f32[3,32,256]{2,1,0:T(8,128)S(1)}, f32[3,32,256]{2,1,0:T(8,128)S(1)}, u32[]{:S(2)}, u32[]{:S(2)}) collective-permute-start(f32[3,32,256]{2,1,0:T(8,128)S(1)} %get-tuple-element.33.own_west), channel_id=1, source_target_pairs={{8,0},{16,8},{24,16},{9,1},{17,9},{25,17},{10,2},{18,10},{26,18},{... | collective-permute-start | bytes 294920 | tf_op jit(solution)/shard_map/ppermute | solution.py:731
  56.3 12.2 %advance_second.1 = (f32[3,96,32,256]{3,2,1,0:T(8,128)}, f32[8,128]{1,0:T(8,128)S(1)}) custom-call(f32[3,96,32,256]{3,2,1,0:T(8,128)} %get-tuple-element.30.section_hbm, f32[3,96,32,256]{3,2,1,0:T(8,128)} %velocity.3), custom_call_target="tpu_custom_call" | custom-call | flops 1000000000 | bytes 37748736 | tf_op jit(solution)/shard_map/advance_second/pallas_call | solution.py:827
  68.5 0.0 collective-permute-done.4.after_low.ghost_low
  68.5 0.0 collective-permute-done.5.after_high.ghost_high
  68.5 0.0 all-to-all-done.parts
  68.5 0.8 share_force.1.after
  69.3 5.7 %all-to-all-start.1 = ((f32[8,24,1,256]{3,2,1,0:T(1,128)}), f32[8,24,1,256]{3,2,1,0:T(1,128)S(1)}, u32[]{:S(2)}, u32[]{:S(2)}) async-start(f32[8,24,1,256]{3,2,1,0:T(1,128)} %share_force.1.after), calls=%async_computation.1 | async-start | bytes 393216 | tf_op jit(solution)/shard_map/all_to_all | solution.py:849
  75.0 0.0 collective-permute-done.7.got_high
  75.0 0.0 collective-permute-done.6.got_low
  75.0 9.3 %spread_next.1 = f32[3,96,32,256]{3,2,1,0:T(8,128)} custom-call(f32[3,96,32,256]{3,2,1,0:T(8,128)} %get-tuple-element.31.following, f32[3,32,256]{2,1,0:T(8,128)S(1)} %copy-done, f32[3,32,256]{2,1,0:T(8,128)S(1)} %collective-permute-done.4.after_low.ghost_low, f32[3,32,256]{2,1,0:T(8,128)S(1)} %collective-permute-done.5.after_high.ghost_high, ...), custom_call_target="tpu_custom_call" | custom-call | flops 2000000000 | bytes 37748736 | tf_op jit(solution)/shard_map/spread_next/pallas_call | solution.py:851
  84.4 0.0 all-to-all-done.1
  84.4 0.7 copy.9
Async XLA Ops:
  6.7 21.4 %collective-permute-start.3 = (f32[480,1,256]{2,1,0:T(1,128)S(1)}, f32[480,1,256]{2,1,0:T(1,128)S(1)}, u32[]{:S(2)}, u32[]{:S(2)}) collective-permute-start(f32[480,1,256]{2,1,0:T(1,128)S(1)} %get-tuple-element.24.own_low), channel_id=1, source_target_pairs={{0,7},{1,0},{2,1},{3,2},{4,3},{5,4},{6,5},{7,6},{8,15},{9,8},{10,9... | collective-permute-start | bytes 1474568 | tf_op jit(solution)/shard_map/ppermute | solution.py:731
  11.5 19.7 %collective-permute-start.2 = (f32[480,1,256]{2,1,0:T(1,128)S(1)}, f32[480,1,256]{2,1,0:T(1,128)S(1)}, u32[]{:S(2)}, u32[]{:S(2)}) collective-permute-start(f32[480,1,256]{2,1,0:T(1,128)S(1)} %get-tuple-element.25.own_high), channel_id=1, source_target_pairs={{0,1},{1,2},{2,3},{3,4},{4,5},{5,6},{6,7},{7,0},{8,9},{9,10},{10,1... | collective-permute-start | bytes 1474568 | tf_op jit(solution)/shard_map/ppermute | solution.py:731
  11.5 16.5 %collective-permute-start = (f32[3,32,256]{2,1,0:T(8,128)S(1)}, f32[3,32,256]{2,1,0:T(8,128)S(1)}, u32[]{:S(2)}, u32[]{:S(2)}) collective-permute-start(f32[3,32,256]{2,1,0:T(8,128)S(1)} %get-tuple-element.22.own_east), channel_id=1, source_target_pairs={{0,8},{8,16},{16,24},{1,9},{9,17},{17,25},{2,10},{10,18},{18,26},{... | collective-permute-start | bytes 294920 | tf_op jit(solution)/shard_map/ppermute | solution.py:731
  16.2 11.9 %collective-permute-start.1 = (f32[3,32,256]{2,1,0:T(8,128)S(1)}, f32[3,32,256]{2,1,0:T(8,128)S(1)}, u32[]{:S(2)}, u32[]{:S(2)}) collective-permute-start(f32[3,32,256]{2,1,0:T(8,128)S(1)} %get-tuple-element.23.own_west), channel_id=1, source_target_pairs={{8,0},{16,8},{24,16},{9,1},{17,9},{25,17},{10,2},{18,10},{26,18},{... | collective-permute-start | bytes 294920 | tf_op jit(solution)/shard_map/ppermute | solution.py:731
  19.2 12.0 %copy-start = (f32[3,32,256]{2,1,0:T(8,128)S(1)}, f32[3,32,256]{2,1,0:T(8,128)}, u32[]{:S(2)}) copy-start(f32[3,32,256]{2,1,0:T(8,128)} %inflow.3) | copy-start | bytes 294916
  37.6 30.9 %all-to-all-start = ((f32[8,2,24,1,256]{4,3,2,1,0:T(1,128)}), f32[8,2,24,1,256]{4,3,2,1,0:T(1,128)S(1)}, u32[]{:S(2)}, u32[]{:S(2)}) async-start(f32[8,2,24,1,256]{4,3,2,1,0:T(1,128)} %get-tuple-element.38), calls=%async_computation | async-start | bytes 786432 | tf_op jit(solution)/shard_map/all_to_all | solution.py:824
  41.1 33.9 %collective-permute-start.7 = (f32[480,1,256]{2,1,0:T(1,128)S(1)}, f32[480,1,256]{2,1,0:T(1,128)S(1)}, u32[]{:S(2)}, u32[]{:S(2)}) collective-permute-start(f32[480,1,256]{2,1,0:T(1,128)S(1)} %get-tuple-element.34.own_low), channel_id=1, source_target_pairs={{0,7},{1,0},{2,1},{3,2},{4,3},{5,4},{6,5},{7,6},{8,15},{9,8},{10,9... | collective-permute-start | bytes 1474568 | tf_op jit(solution)/shard_map/ppermute | solution.py:731
  45.3 29.8 %collective-permute-start.6 = (f32[480,1,256]{2,1,0:T(1,128)S(1)}, f32[480,1,256]{2,1,0:T(1,128)S(1)}, u32[]{:S(2)}, u32[]{:S(2)}) collective-permute-start(f32[480,1,256]{2,1,0:T(1,128)S(1)} %get-tuple-element.35.own_high), channel_id=1, source_target_pairs={{0,1},{1,2},{2,3},{3,4},{4,5},{5,6},{6,7},{7,0},{8,9},{9,10},{10,1... | collective-permute-start | bytes 1474568 | tf_op jit(solution)/shard_map/ppermute | solution.py:731
  45.3 23.2 %collective-permute-start.4 = (f32[3,32,256]{2,1,0:T(8,128)S(1)}, f32[3,32,256]{2,1,0:T(8,128)S(1)}, u32[]{:S(2)}, u32[]{:S(2)}) collective-permute-start(f32[3,32,256]{2,1,0:T(8,128)S(1)} %get-tuple-element.32.own_east), channel_id=1, source_target_pairs={{0,8},{8,16},{16,24},{1,9},{9,17},{17,25},{2,10},{10,18},{18,26},{... | collective-permute-start | bytes 294920 | tf_op jit(solution)/shard_map/ppermute | solution.py:731
  54.3 14.1 %collective-permute-start.5 = (f32[3,32,256]{2,1,0:T(8,128)S(1)}, f32[3,32,256]{2,1,0:T(8,128)S(1)}, u32[]{:S(2)}, u32[]{:S(2)}) collective-permute-start(f32[3,32,256]{2,1,0:T(8,128)S(1)} %get-tuple-element.33.own_west), channel_id=1, source_target_pairs={{8,0},{16,8},{24,16},{9,1},{17,9},{25,17},{10,2},{18,10},{26,18},{... | collective-permute-start | bytes 294920 | tf_op jit(solution)/shard_map/ppermute | solution.py:731
  69.3 15.1 %all-to-all-start.1 = ((f32[8,24,1,256]{3,2,1,0:T(1,128)}), f32[8,24,1,256]{3,2,1,0:T(1,128)S(1)}, u32[]{:S(2)}, u32[]{:S(2)}) async-start(f32[8,24,1,256]{3,2,1,0:T(1,128)} %share_force.1.after), calls=%async_computation.1 | async-start | bytes 393216 | tf_op jit(solution)/shard_map/all_to_all | solution.py:849

commit v7 on v6

--- a/solution.py
+++ b/solution.py
@@ -172,11 +172,17 @@
             pack[n] = pack[n] + jnp.where(keep, rows[c], 0.0)
 
 
-def pack_edges(field, edge_west, edge_east, pack_low, pack_high):
+def is_even(axis):
+    return lax.rem(lax.axis_index(axis), 2) == 0
+
+
+def pack_edges(field, edge_near, edge_far, pack_low, pack_high):
     cells_x, cells_y, depth = field.shape[1:]
+    even = is_even("gx")
     for c in range(3):
-        edge_west[c] = field[c, 0]
-        edge_east[c] = field[c, cells_x - 1]
+        west, east = field[c, 0], field[c, cells_x - 1]
+        edge_near[c] = jnp.where(even, east, west)
+        edge_far[c] = jnp.where(even, west, east)
 
     def step(t, carry):
         cells = [(c, t * BATCH + k) for k in range(BATCH) for c in range(3)]
@@ -193,7 +199,7 @@
 
 def load_sample(
     velocity, positions, tiles_hbm, coefs_hbm, counts,
-    field, pack_low, pack_high, edge_west, edge_east, weight_y, weight_z, strength, point_y, plan,
+    field, pack_low, pack_high, edge_near, edge_far, weight_y, weight_z, strength, point_y, plan,
     point_z, hubs, tiles, places, coefs, table, small_sems, plan_sem, sems,
 ):
     cells_x, cells_y, depth = field.shape[1:]
@@ -292,24 +298,27 @@
         return carry
 
     lax.fori_loop(0, 3 * records // SUB, copy_rows, 0)
-    pack_edges(field, edge_west, edge_east, pack_low, pack_high)
-
-
-def fix_west(factor, target, own, inflow, ghost):
-    first = lax.axis_index("gx") == 0
+    pack_edges(field, edge_near, edge_far, pack_low, pack_high)
+
+
+def fix_sides(factor, target, own_near, own_far, inflow, ghost_near, ghost_far, west_side):
+    near = is_even("gx") != west_side
+
+    def side(one, other, c):
+        return jnp.where(near, one[c], other[c])
+
+    sign = 1.0 if west_side else -1.0
+    end = 0 if west_side else target.shape[1] - 1
+    place = lax.axis_index("gx")
+    spread = factor * TIME_STEP * VISCOSITY
+    coef = spread + (sign * 0.5 * factor * TIME_STEP) * side(own_near, own_far, 0)
     for c in range(3):
-        west = jnp.where(first, inflow[c], ghost[c])
-        coef = factor * TIME_STEP * VISCOSITY + (0.5 * factor * TIME_STEP) * own[0]
-        target[c, 0] = target[c, 0] + (west - own[c]) * coef
-
-
-def fix_east(factor, target, own, ghost):
-    last = lax.axis_index("gx") == lax.axis_size("gx") - 1
-    end = target.shape[1] - 1
-    for c in range(3):
-        east = jnp.where(last, own[c], ghost[c])
-        coef = factor * TIME_STEP * VISCOSITY - (0.5 * factor * TIME_STEP) * own[0]
-        target[c, end] = target[c, end] + (east - own[c]) * coef
+        own, ghost = side(own_near, own_far, c), side(ghost_near, ghost_far, c)
+        if west_side:
+            ghost = jnp.where(place == 0, inflow[c], ghost)
+        else:
+            ghost = jnp.where(place == lax.axis_size("gx") - 1, own, ghost)
+        target[c, end] = target[c, end] + (ghost - own) * coef
 
 
 def fix_rows(factor, target, own_low, own_high, got_low, got_high, t):
@@ -377,9 +386,9 @@
 
 
 def spread_sample(
-    section_in, inflow, ghost_low, ghost_high, own_low, own_high, own_west, own_east, got_low, got_high,
+    section_in, inflow, ghost_near, ghost_far, own_low, own_high, own_near, own_far, got_low, got_high,
     plan, weight_y, weight_z, strength,
-    section, section_out, stored_z, pack_low, pack_high, edge_west, edge_east,
+    section, section_out, stored_z, pack_low, pack_high, edge_near, edge_far,
     share_out, sem, sem_z,
 ):
     cells_x = section.shape[1]
@@ -406,8 +415,9 @@
         fix_rows(1.0, section, own_low, own_high, got_low, got_high, t)
         return carry
 
-    fix_west(1.0, section, own_west, inflow, ghost_low)
-    fix_east(1.0, section, own_east, ghost_high)
+    sides = (own_near, own_far, inflow, ghost_near, ghost_far)
+    fix_sides(1.0, section, *sides, True)
+    fix_sides(1.0, section, *sides, False)
     lax.fori_loop(0, cells_x // SUB, fix_step, 0)
 
     def spread_step(t, carry):
@@ -418,7 +428,7 @@
     lax.fori_loop(0, groups_of(plan), spread_step, 0)
     copy = pltpu.make_async_copy(section, section_out, sem)
     copy.start()
-    pack_edges(section, edge_west, edge_east, pack_low, pack_high)
+    pack_edges(section, edge_near, edge_far, pack_low, pack_high)
 
     def clear(n, carry):
         for k in range(SUB):
@@ -477,12 +487,13 @@
 
 
 def spread_next(
-    following, inflow, ghost_low, ghost_high, own_low, own_high, own_west, own_east, got_low, got_high,
+    following, inflow, ghost_near, ghost_far, own_low, own_high, own_near, own_far, got_low, got_high,
     plan, point_y, stored_z, strength, after,
     result, field, weight_z, in_sems, out_sems, sem_z,
 ):
     chunks = field.shape[1] // CHUNK
     factor = 0.5
+    sides = (own_near, own_far, inflow, ghost_near, ghost_far)
 
     def chunk_in(k):
         planes = pl.ds(k * CHUNK, CHUNK)
@@ -501,11 +512,11 @@
 
             @pl.when(k == 0)
             def _():
-                fix_west(factor, field, own_west, inflow, ghost_low)
+                fix_sides(factor, field, *sides, True)
 
             @pl.when(k == chunks - 1)
             def _():
-                fix_east(factor, field, own_east, ghost_high)
+                fix_sides(factor, field, *sides, False)
 
             return carry
 
@@ -669,74 +680,93 @@
     cells_x = section.shape[1]
     blocks = cells_x // BLOCK
 
-    def planes(k):
-        return pl.ds(k * BLOCK, BLOCK)
+    def copy(source, target, first, count, sem):
+        some = pl.ds(first, count)
+        return pltpu.make_async_copy(source.at[:, some], target.at[:, some], sem)
 
     def section_in(k):
-        if isinstance(k, int) and k in (0, blocks):
-            some = pl.ds(0 if k == 0 else cells_x - PLANES, PLANES)
-        else:
-            some = pl.ds(k * BLOCK - PLANES, BLOCK)
-        return pltpu.make_async_copy(section_hbm.at[:, some], section.at[:, some], in_sems.at[k])
+        return copy(section_hbm, section, k * BLOCK, BLOCK, in_sems.at[k])
 
     def old_in(k):
-        return pltpu.make_async_copy(
-            velocity.at[:, planes(k)], field.at[:, planes(k)], old_sems.at[k]
+        return copy(velocity, field, k * BLOCK, BLOCK, old_sems.at[k])
+
+    def block_out(k):
+        return copy(result, following, k * BLOCK, BLOCK, out_sems.at[k])
+
+    halves = range(BLOCK // PLANES)
+    head = [
+        (
+            copy(section_hbm, section, n * PLANES, PLANES, in_sems.at[n * blocks]),
+            copy(velocity, field, n * PLANES, PLANES, old_sems.at[n * blocks]),
         )
-
-    def block_out(k):
-        return pltpu.make_async_copy(
-            result.at[:, planes(k)], following.at[:, planes(k)], out_sems.at[k]
-        )
+        for n in halves
+    ]
+    last = blocks - 1
+    tail = [
+        copy(result, following, last * BLOCK + n * PLANES, PLANES, out_sems.at[last + n])
+        for n in halves
+    ]
 
     def finish(c, i, rows, cols, value):
         return value + 0.5 * field[c, i, rows, cols]
 
-    for k in range(blocks + 1):
+    head[0][0].start()
+    head[1][0].start()
+    head[0][1].start()
+    head[1][1].start()
+    for k in range(1, blocks):
         section_in(k).start()
-        if k > 0:
-            old_in(k - 1).start()
+        old_in(k).start()
     token[...] = jnp.zeros_like(token)
     fill_shifts(shifts)
-    section_in(0).wait()
+
+    def work(i, n):
+        advance_batch(i, n, 0.5, section, shifts, (slot_a, slot_b), result, finish)
+
+    head[0][0].wait()
     along_depth(0, section, shifts, slot_a)
+    head[1][0].wait()
+    head[0][1].wait()
+    work(0, 0)
+    section_in(1).wait()
+    head[1][1].wait()
+    work(PLANES, 1)
+    block_out(0).start()
 
     def step(t, carry):
-        @pl.when(t + 1 < blocks)
-        def _():
-            section_in(t + 1).wait()
-
-        @pl.when(t + 1 == blocks)
-        def _():
-            section_in(blocks).wait()
-
+        section_in(t + 1).wait()
         old_in(t).wait()
-        for n in range(BLOCK // PLANES):
-            advance_batch(
-                t * BLOCK + n * PLANES, n, 0.5, section, shifts, (slot_a, slot_b), result, finish
-            )
+        for n in halves:
+            work(t * BLOCK + n * PLANES, n)
         block_out(t).start()
         return carry
 
-    lax.fori_loop(0, blocks, step, 0)
-    for k in range(blocks):
+    lax.fori_loop(1, last, step, 0)
+    old_in(last).wait()
+    for n in halves:
+        work(last * BLOCK + n * PLANES, n)
+        tail[n].start()
+    for k in range(last):
         block_out(k).wait()
-
-
-def shifted(x, axis, step, periodic):
+    for out in tail:
+        out.wait()
+
+
+def shifted(x, axis, step):
     count = lax.axis_size(axis)
-    pairs = [(i, (i + step) % count) for i in range(count)]
-    if not periodic:
-        pairs = [(s, t) for s, t in pairs if t - s == step]
-    return lax.ppermute(x, axis, pairs)
-
-
-def exchange(pack_low, pack_high, edge_west, edge_east):
-    got_low = shifted(pack_high, "gy", 1, True)
-    got_high = shifted(pack_low, "gy", -1, True)
-    ghost_low = shifted(edge_east, "gx", 1, False)
-    ghost_high = shifted(edge_west, "gx", -1, False)
-    return ghost_low, ghost_high, got_low, got_high
+    return lax.ppermute(x, axis, [(i, (i + step) % count) for i in range(count)])
+
+
+def swapped(x, axis, first):
+    count = lax.axis_size(axis)
+    pairs = [(i, i + 1) for i in range(first, count - 1, 2)]
+    return lax.ppermute(x, axis, pairs + [(t, s) for s, t in pairs])
+
+
+def exchange(pack_low, pack_high, edge_near, edge_far):
+    got_low = shifted(pack_high, "gy", 1)
+    got_high = shifted(pack_low, "gy", -1)
+    return swapped(edge_near, "gx", 0), swapped(edge_far, "gx", 1), got_low, got_high
 
 
 def local(velocity, inflow, positions, tiles, coefs, counts):

time: 85.4 us -> 84.8 us (level); the launches traced: 85.1 us -> 83.2 us
  starting transfers between devices: 36.8 us -> 32.1 us
  waiting for transfers between devices: 3.1 us -> 5.44 us
    ppermute x8, starting transfers between devices: 27.6 us -> 18.8 us  [the longest x4 9.39 us: swapped(): return lax.ppermute(x, axis, pairs + [(t, s) for s, t in pairs])]
    all_to_all x1, starting transfers between devices: 3.49 us -> 7.64 us  [local(): shares = lax.all_to_all(shares, 'gy', 0, 0)]
    ppermute x8, waiting for transfers between devices: 3.1 us -> 5.44 us  [the longest x4 5.43 us: shifted(): lax.ppermute(x, axis, [(i, (i + step) % count) for i in range(count)])]
    pallas_call x1, Pallas kernels: 5.42 us -> 6.35 us  [local(): pl.pallas_call(load_sample, out_shape=(held, pack, pack, edge, edge, pltp...]
  transfers between devices with their start and end apart: 10 -> 10, of which waited for: 1 -> 2; matrix products, arithmetic and copies ran while one was open for 0% -> 0% of each run, Pallas kernels for 37% -> 36%
where the time goes in v7:
time: 84.8 us; the launch traced here: 83.2 us
  Pallas kernels  43.5 us (51%)
  starting transfers between devices  32.1 us (38%)
  waiting for transfers between devices  5.44 us (6%)
  between operations  1.41 us (2%)
    pallas_call x1, Pallas kernels, local(): pl.pallas_call(advance_second, out_shape=(stored, array((SUB, LANES), f32...  11.7 us
    ppermute x4, starting transfers between devices, swapped(): return lax.ppermute(x, axis, pairs + [(t, s) for s, t in pairs])  9.39 us
    ppermute x4, starting transfers between devices, shifted(): lax.ppermute(x, axis, [(i, (i + step) % count) for i in range(count)])  9.39 us
    pallas_call x1, Pallas kernels, local(): pl.pallas_call(advance_first, out_shape=held, in_specs=[WHOLE], out_specs...  8.86 us
    pallas_call x1, Pallas kernels, local(): pl.pallas_call(spread_next, out_shape=stored, in_specs=[ANYWHERE] + [WHOL...  8.51 us
    all_to_all x1, starting transfers between devices, local(): shares = lax.all_to_all(shares, 'gy', 0, 0)  7.64 us
    pallas_call x1, Pallas kernels, local(): pl.pallas_call(spread_sample, out_shape=(held, stored, pltpu.HBM(z_shape,...  7.22 us
    pallas_call x1, Pallas kernels, local(): pl.pallas_call(load_sample, out_shape=(held, pack, pack, edge, edge, pltp...  6.35 us
  transfers between devices with their start and end apart: 10, of which 2 were waited for; matrix products, arithmetic and copies ran while one was open for 0% of the time, Pallas kernels for 36%

profile of v7, /device:TPU:1, one launch (start us, length us, event | category | flops | bytes accessed | tf_op | source)
XLA Modules:
  0.0 83.2 jit_solution(10509132326095222103)
XLA Ops:
  1.3 6.3 %load_sample.1 = (f32[3,96,32,256]{3,2,1,0:T(8,128)S(1)}, f32[480,1,256]{2,1,0:T(1,128)S(1)}, f32[480,1,256]{2,1,0:T(1,128)S(1)}, f32[3,32,256]{2,1,0:T(8,128)S(...) custom-call(f32[3,96,32,256]{3,2,1,0:T(8,128)} %velocity.3, ...), custom_call_target="tpu_custom_call" | custom-call | flops 2000000000 | bytes 37748736 | tf_op jit(solution)/shard_map/load_sample/pallas_call | solution.py:797
  7.6 5.2 %collective-permute-start.3 = (f32[480,1,256]{2,1,0:T(1,128)S(1)}, f32[480,1,256]{2,1,0:T(1,128)S(1)}, u32[]{:S(2)}, u32[]{:S(2)}) collective-permute-start(f32[480,1,256]{2,1,0:T(1,128)S(1)} %get-tuple-element.24.own_low), channel_id=1, source_target_pairs={{0,7},{1,0},{2,1},{3,2},{4,3},{5,4},{6,5},{7,6},{8,15},{9,8},{10,9... | collective-permute-start | bytes 1474568 | tf_op jit(solution)/shard_map/ppermute | solution.py:757
  12.9 0.0 collective-permute-start.2
  12.9 2.6 %collective-permute-start = (f32[3,32,256]{2,1,0:T(8,128)S(1)}, f32[3,32,256]{2,1,0:T(8,128)S(1)}, u32[]{:S(2)}, u32[]{:S(2)}) collective-permute-start(f32[3,32,256]{2,1,0:T(8,128)S(1)} %get-tuple-element.22.own_near), channel_id=1, source_target_pairs={{0,8},{16,24},{8,0},{24,16},{1,9},{17,25},{9,1},{25,17},{2,10},{18... | collective-permute-start | bytes 294920 | tf_op jit(solution)/shard_map/ppermute | solution.py:763
  15.4 1.9 %collective-permute-start.1 = (f32[3,32,256]{2,1,0:T(8,128)S(1)}, f32[3,32,256]{2,1,0:T(8,128)S(1)}, u32[]{:S(2)}, u32[]{:S(2)}) collective-permute-start(f32[3,32,256]{2,1,0:T(8,128)S(1)} %get-tuple-element.23.own_far), channel_id=1, source_target_pairs={{8,16},{16,8},{9,17},{17,9},{10,18},{18,10},{11,19},{19,11},{12,20... | collective-permute-start | bytes 294920 | tf_op jit(solution)/shard_map/ppermute | solution.py:763
  17.3 0.0 copy-start
  17.4 8.9 %advance_first.1.section_in = f32[3,96,32,256]{3,2,1,0:T(8,128)S(1)} custom-call(f32[3,96,32,256]{3,2,1,0:T(8,128)S(1)} %get-tuple-element.21.field), custom_call_target="tpu_custom_call" | custom-call | flops 1000000000 | bytes 37748736 | tf_op jit(solution)/shard_map/advance_first/pallas_call | solution.py:825
  26.2 0.0 collective-permute-done.ghost_near
  26.2 0.0 collective-permute-done.1.ghost_far
  26.2 3.8 %collective-permute-done.3.got_high = f32[480,1,256]{2,1,0:T(1,128)S(1)} collective-permute-done((f32[480,1,256]{2,1,0:T(1,128)S(1)}, f32[480,1,256]{2,1,0:T(1,128)S(1)}, u32[]{:S(2)}, u32[]{:S(2)}) %collective-permute-start.3) | collective-permute-done | bytes 491552 | tf_op jit(solution)/shard_map/ppermute | solution.py:757
  30.0 1.7 %collective-permute-done.2.got_low = f32[480,1,256]{2,1,0:T(1,128)S(1)} collective-permute-done((f32[480,1,256]{2,1,0:T(1,128)S(1)}, f32[480,1,256]{2,1,0:T(1,128)S(1)}, u32[]{:S(2)}, u32[]{:S(2)}) %collective-permute-start.2) | collective-permute-done | bytes 491552 | tf_op jit(solution)/shard_map/ppermute | solution.py:757
  31.7 0.0 copy-done
  31.7 7.2 %spread_sample.1 = (f32[3,96,32,256]{3,2,1,0:T(8,128)S(1)}, f32[3,96,32,256]{3,2,1,0:T(8,128)}, bf16[128,256,256]{2,1,0:T(8,128)(2,1)}, f32[480,1,256]{2,1,0:T(1...) custom-call(f32[3,96,32,256]{3,2,1,0:T(8,128)S(1)} %advance_first.1., ...), custom_call_target="tpu_custom_call", output_to_operand_aliasing={{0}: (0, {})} | custom-call | flops 2000000000 | bytes 37748736 | tf_op jit(solution)/shard_map/spread_sample/pallas_call | solution.py:836
  38.9 7.6 %all-to-all-start = ((f32[8,2,24,1,256]{4,3,2,1,0:T(1,128)}), f32[8,2,24,1,256]{4,3,2,1,0:T(1,128)S(1)}, u32[]{:S(2)}, u32[]{:S(2)}) async-start(f32[8,2,24,1,256]{4,3,2,1,0:T(1,128)} %get-tuple-element.38), calls=%async_computation | async-start | bytes 786432 | tf_op jit(solution)/shard_map/all_to_all | solution.py:854
  46.5 4.2 %collective-permute-start.7 = (f32[480,1,256]{2,1,0:T(1,128)S(1)}, f32[480,1,256]{2,1,0:T(1,128)S(1)}, u32[]{:S(2)}, u32[]{:S(2)}) collective-permute-start(f32[480,1,256]{2,1,0:T(1,128)S(1)} %get-tuple-element.34.own_low), channel_id=1, source_target_pairs={{0,7},{1,0},{2,1},{3,2},{4,3},{5,4},{6,5},{7,6},{8,15},{9,8},{10,9... | collective-permute-start | bytes 1474568 | tf_op jit(solution)/shard_map/ppermute | solution.py:757
  50.7 0.0 collective-permute-start.6
  50.7 3.0 %collective-permute-start.4 = (f32[3,32,256]{2,1,0:T(8,128)S(1)}, f32[3,32,256]{2,1,0:T(8,128)S(1)}, u32[]{:S(2)}, u32[]{:S(2)}) collective-permute-start(f32[3,32,256]{2,1,0:T(8,128)S(1)} %get-tuple-element.32.own_near), channel_id=1, source_target_pairs={{0,8},{16,24},{8,0},{24,16},{1,9},{17,25},{9,1},{25,17},{2,10},{18... | collective-permute-start | bytes 294920 | tf_op jit(solution)/shard_map/ppermute | solution.py:763
  53.7 1.9 %collective-permute-start.5 = (f32[3,32,256]{2,1,0:T(8,128)S(1)}, f32[3,32,256]{2,1,0:T(8,128)S(1)}, u32[]{:S(2)}, u32[]{:S(2)}) collective-permute-start(f32[3,32,256]{2,1,0:T(8,128)S(1)} %get-tuple-element.33.own_far), channel_id=1, source_target_pairs={{8,16},{16,8},{9,17},{17,9},{10,18},{18,10},{11,19},{19,11},{12,20... | collective-permute-start | bytes 294920 | tf_op jit(solution)/shard_map/ppermute | solution.py:763
  55.6 11.7 %advance_second.1 = (f32[3,96,32,256]{3,2,1,0:T(8,128)}, f32[8,128]{1,0:T(8,128)S(1)}) custom-call(f32[3,96,32,256]{3,2,1,0:T(8,128)} %get-tuple-element.30.section_hbm, f32[3,96,32,256]{3,2,1,0:T(8,128)} %velocity.3), custom_call_target="tpu_custom_call" | custom-call | flops 1000000000 | bytes 37748736 | tf_op jit(solution)/shard_map/advance_second/pallas_call | solution.py:857
  67.4 0.0 collective-permute-done.4.after_low.ghost_near
  67.4 0.0 collective-permute-done.5.after_high.ghost_far
  67.4 0.0 all-to-all-done.parts
  67.4 0.8 share_force.1.after
  68.2 5.7 %all-to-all-start.1 = ((f32[8,24,1,256]{3,2,1,0:T(1,128)}), f32[8,24,1,256]{3,2,1,0:T(1,128)S(1)}, u32[]{:S(2)}, u32[]{:S(2)}) async-start(f32[8,24,1,256]{3,2,1,0:T(1,128)} %share_force.1.after), calls=%async_computation.1 | async-start | bytes 393216 | tf_op jit(solution)/shard_map/all_to_all | solution.py:879
  73.9 0.0 collective-permute-done.7.got_high
  73.9 0.0 collective-permute-done.6.got_low
  73.9 8.5 %spread_next.1 = f32[3,96,32,256]{3,2,1,0:T(8,128)} custom-call(f32[3,96,32,256]{3,2,1,0:T(8,128)} %get-tuple-element.31.following, f32[3,32,256]{2,1,0:T(8,128)S(1)} %copy-done, f32[3,32,256]{2,1,0:T(8,128)S(1)} %collective-permute-done.4.after_low.ghost_near, f32[3,32,256]{2,1,0:T(8,128)S(1)} %collective-permute-done.5.after_high.ghost_far, ...), custom_call_target="tpu_custom_call" | custom-call | flops 2000000000 | bytes 37748736 | tf_op jit(solution)/shard_map/spread_next/pallas_call | solution.py:881
  82.5 0.0 all-to-all-done.1
  82.5 0.7 copy.9
Async XLA Ops:
  7.6 22.4 %collective-permute-start.3 = (f32[480,1,256]{2,1,0:T(1,128)S(1)}, f32[480,1,256]{2,1,0:T(1,128)S(1)}, u32[]{:S(2)}, u32[]{:S(2)}) collective-permute-start(f32[480,1,256]{2,1,0:T(1,128)S(1)} %get-tuple-element.24.own_low), channel_id=1, source_target_pairs={{0,7},{1,0},{2,1},{3,2},{4,3},{5,4},{6,5},{7,6},{8,15},{9,8},{10,9... | collective-permute-start | bytes 1474568 | tf_op jit(solution)/shard_map/ppermute | solution.py:757
  12.9 18.8 %collective-permute-start.2 = (f32[480,1,256]{2,1,0:T(1,128)S(1)}, f32[480,1,256]{2,1,0:T(1,128)S(1)}, u32[]{:S(2)}, u32[]{:S(2)}) collective-permute-start(f32[480,1,256]{2,1,0:T(1,128)S(1)} %get-tuple-element.25.own_high), channel_id=1, source_target_pairs={{0,1},{1,2},{2,3},{3,4},{4,5},{5,6},{6,7},{7,0},{8,9},{9,10},{10,1... | collective-permute-start | bytes 1474568 | tf_op jit(solution)/shard_map/ppermute | solution.py:757
  12.9 13.4 %collective-permute-start = (f32[3,32,256]{2,1,0:T(8,128)S(1)}, f32[3,32,256]{2,1,0:T(8,128)S(1)}, u32[]{:S(2)}, u32[]{:S(2)}) collective-permute-start(f32[3,32,256]{2,1,0:T(8,128)S(1)} %get-tuple-element.22.own_near), channel_id=1, source_target_pairs={{0,8},{16,24},{8,0},{24,16},{1,9},{17,25},{9,1},{25,17},{2,10},{18... | collective-permute-start | bytes 294920 | tf_op jit(solution)/shard_map/ppermute | solution.py:763
  15.4 10.8 %collective-permute-start.1 = (f32[3,32,256]{2,1,0:T(8,128)S(1)}, f32[3,32,256]{2,1,0:T(8,128)S(1)}, u32[]{:S(2)}, u32[]{:S(2)}) collective-permute-start(f32[3,32,256]{2,1,0:T(8,128)S(1)} %get-tuple-element.23.own_far), channel_id=1, source_target_pairs={{8,16},{16,8},{9,17},{17,9},{10,18},{18,10},{11,19},{19,11},{12,20... | collective-permute-start | bytes 294920 | tf_op jit(solution)/shard_map/ppermute | solution.py:763
  17.3 14.3 %copy-start = (f32[3,32,256]{2,1,0:T(8,128)S(1)}, f32[3,32,256]{2,1,0:T(8,128)}, u32[]{:S(2)}) copy-start(f32[3,32,256]{2,1,0:T(8,128)} %inflow.3) | copy-start | bytes 294916
  38.9 28.5 %all-to-all-start = ((f32[8,2,24,1,256]{4,3,2,1,0:T(1,128)}), f32[8,2,24,1,256]{4,3,2,1,0:T(1,128)S(1)}, u32[]{:S(2)}, u32[]{:S(2)}) async-start(f32[8,2,24,1,256]{4,3,2,1,0:T(1,128)} %get-tuple-element.38), calls=%async_computation | async-start | bytes 786432 | tf_op jit(solution)/shard_map/all_to_all | solution.py:854
  46.5 27.4 %collective-permute-start.7 = (f32[480,1,256]{2,1,0:T(1,128)S(1)}, f32[480,1,256]{2,1,0:T(1,128)S(1)}, u32[]{:S(2)}, u32[]{:S(2)}) collective-permute-start(f32[480,1,256]{2,1,0:T(1,128)S(1)} %get-tuple-element.34.own_low), channel_id=1, source_target_pairs={{0,7},{1,0},{2,1},{3,2},{4,3},{5,4},{6,5},{7,6},{8,15},{9,8},{10,9... | collective-permute-start | bytes 1474568 | tf_op jit(solution)/shard_map/ppermute | solution.py:757
  50.7 23.2 %collective-permute-start.6 = (f32[480,1,256]{2,1,0:T(1,128)S(1)}, f32[480,1,256]{2,1,0:T(1,128)S(1)}, u32[]{:S(2)}, u32[]{:S(2)}) collective-permute-start(f32[480,1,256]{2,1,0:T(1,128)S(1)} %get-tuple-element.35.own_high), channel_id=1, source_target_pairs={{0,1},{1,2},{2,3},{3,4},{4,5},{5,6},{6,7},{7,0},{8,9},{9,10},{10,1... | collective-permute-start | bytes 1474568 | tf_op jit(solution)/shard_map/ppermute | solution.py:757
  50.7 16.7 %collective-permute-start.4 = (f32[3,32,256]{2,1,0:T(8,128)S(1)}, f32[3,32,256]{2,1,0:T(8,128)S(1)}, u32[]{:S(2)}, u32[]{:S(2)}) collective-permute-start(f32[3,32,256]{2,1,0:T(8,128)S(1)} %get-tuple-element.32.own_near), channel_id=1, source_target_pairs={{0,8},{16,24},{8,0},{24,16},{1,9},{17,25},{9,1},{25,17},{2,10},{18... | collective-permute-start | bytes 294920 | tf_op jit(solution)/shard_map/ppermute | solution.py:763
  53.7 13.7 %collective-permute-start.5 = (f32[3,32,256]{2,1,0:T(8,128)S(1)}, f32[3,32,256]{2,1,0:T(8,128)S(1)}, u32[]{:S(2)}, u32[]{:S(2)}) collective-permute-start(f32[3,32,256]{2,1,0:T(8,128)S(1)} %get-tuple-element.33.own_far), channel_id=1, source_target_pairs={{8,16},{16,8},{9,17},{17,9},{10,18},{18,10},{11,19},{19,11},{12,20... | collective-permute-start | bytes 294920 | tf_op jit(solution)/shard_map/ppermute | solution.py:763
  68.2 14.3 %all-to-all-start.1 = ((f32[8,24,1,256]{3,2,1,0:T(1,128)}), f32[8,24,1,256]{3,2,1,0:T(1,128)S(1)}, u32[]{:S(2)}, u32[]{:S(2)}) async-start(f32[8,24,1,256]{3,2,1,0:T(1,128)} %share_force.1.after), calls=%async_computation.1 | async-start | bytes 393216 | tf_op jit(solution)/shard_map/all_to_all | solution.py:879

commit v8 on v7

--- a/solution.py
+++ b/solution.py
@@ -23,7 +23,7 @@
 BLOCK = 2 * PLANES
 CHUNK = 16
 TILES = 8
-VMEM_LIMIT = 8 * 2**20
+VMEM_LIMIT = 6 * 2**20
 
 WHOLE = pl.BlockSpec(memory_space=pltpu.VMEM)
 SCALAR = pl.BlockSpec(memory_space=pltpu.SMEM)
@@ -176,13 +176,16 @@
     return lax.rem(lax.axis_index(axis), 2) == 0
 
 
-def pack_edges(field, edge_near, edge_far, pack_low, pack_high):
-    cells_x, cells_y, depth = field.shape[1:]
+def pack_sides(field, edge_near, edge_far):
     even = is_even("gx")
     for c in range(3):
-        west, east = field[c, 0], field[c, cells_x - 1]
+        west, east = field[c, 0], field[c, field.shape[1] - 1]
         edge_near[c] = jnp.where(even, east, west)
         edge_far[c] = jnp.where(even, west, east)
+
+
+def pack_rows(field, low_out, high_out, first, last):
+    cells_x, cells_y = field.shape[1:3]
 
     def step(t, carry):
         cells = [(c, t * BATCH + k) for k in range(BATCH) for c in range(3)]
@@ -190,22 +193,21 @@
             (field[c, i, pl.ds(0, 1), :], field[c, i, pl.ds(cells_y - 1, 1), :]) for c, i in cells
         ]
         for (c, i), (low, high) in zip(cells, rows):
-            pack_low[c * cells_x + i] = low
-            pack_high[c * cells_x + i] = high
-        return carry
-
-    lax.fori_loop(0, cells_x // BATCH, step, 0)
-
-
-def load_sample(
+            low_out[c * cells_x + i] = low
+            high_out[c * cells_x + i] = high
+        return carry
+
+    lax.fori_loop(first // BATCH, last // BATCH, step, 0)
+
+
+def load_field(
     velocity, positions, tiles_hbm, coefs_hbm, counts,
-    field, pack_low, pack_high, edge_near, edge_far, weight_y, weight_z, strength, point_y, plan,
-    point_z, hubs, tiles, places, coefs, table, small_sems, plan_sem, sems,
+    field, edge_low, edge_high, edge_near, edge_far, strength, point_y, point_z, plan,
+    hubs, tiles, places, coefs, table, small_sems, plan_sem, sems,
 ):
     cells_x, cells_y, depth = field.shape[1:]
     records, points = coefs.shape
     chunks = cells_x // CHUNK
-    first_row = 3 * cells_x
     start = lax.axis_index("gx") * cells_x
 
     def chunk(k):
@@ -240,12 +242,6 @@
     plan_copy = pltpu.make_async_copy(table, plan, plan_sem)
     plan_copy.start()
 
-    def clear(n, carry):
-        for k in range(SUB):
-            pack_low[first_row + n * SUB + k] = jnp.zeros((1, points), jnp.float32)
-        return carry
-
-    lax.fori_loop(0, 3 * records // SUB, clear, 0)
     small[3].wait()
     for first in range(0, records, SUB):
         here = range(first, first + SUB)
@@ -255,7 +251,31 @@
         ]
         for r, (y, z, coef) in zip(here, rows):
             point_y[r], point_z[r], strength[r] = y, z, coef
+
+    def arrived(k, carry):
+        chunk(k).wait()
+        pack_rows(field, edge_low, edge_high, k * CHUNK, (k + 1) * CHUNK)
+        return carry
+
+    lax.fori_loop(0, chunks, arrived, 0)
+    pack_sides(field, edge_near, edge_far)
     plan_copy.wait()
+
+
+def clear_rows(pack, first, last):
+    def clear(n, carry):
+        for k in range(SUB):
+            pack[first + n * SUB + k] = jnp.zeros(pack.shape[1:], jnp.float32)
+        return carry
+
+    lax.fori_loop(0, (last - first) // SUB, clear, 0)
+
+
+def sample_first(field, plan, point_y, point_z, weight_y, weight_z, partial):
+    cells_y = field.shape[2]
+    total_y = cells_y * lax.axis_size("gy")
+    base = lax.axis_index("gy") * cells_y
+    clear_rows(partial, 0, partial.shape[0])
 
     def weigh(t, carry):
         made = []
@@ -272,33 +292,13 @@
 
     lax.fori_loop(0, (found(plan) + 1) // 2, weigh, 0)
 
-    def wait_to(ready, wanted):
-        def step(k, carry):
-            chunk(k).wait()
-            return carry
-
-        lax.fori_loop(ready, wanted, step, 0)
-        return jnp.maximum(ready, wanted)
-
-    def step(t, ready):
+    def step(t, carry):
         picks, keeps = group(plan, t)
-        ready = wait_to(ready, (picks[-1][2] + RAD) // CHUNK + 1)
         rows = sampled_rows(field, weight_y, weight_z, picks)
-        add_rows(pack_low, first_row, picks, rows, keeps)
-        return ready
-
-    ready = lax.fori_loop(0, groups_of(plan), step, jnp.int32(0))
-    wait_to(ready, chunks)
-
-    def copy_rows(t, carry):
-        rows = [first_row + t * SUB + k for k in range(SUB)]
-        values = [pack_low[n] for n in rows]
-        for n, value in zip(rows, values):
-            pack_high[n] = value
-        return carry
-
-    lax.fori_loop(0, 3 * records // SUB, copy_rows, 0)
-    pack_edges(field, edge_near, edge_far, pack_low, pack_high)
+        add_rows(partial, 0, picks, rows, keeps)
+        return carry
+
+    lax.fori_loop(0, groups_of(plan), step, 0)
 
 
 def fix_sides(factor, target, own_near, own_far, inflow, ghost_near, ghost_far, west_side):
@@ -346,13 +346,12 @@
             target[c, i, rows, :] = value
 
 
-def slabs_of(weight_of, weight_z, strength, own, low, high, cells, scales, picks):
-    cells_x, cells_y, depth = cells
+def slabs_of(weight_of, weight_z, strength, first_row, own, low, high, cells_y, scales, picks):
     count = 3 * cells_y
     across = (((1,), (1,)), ((), ()))
     spread = []
     for (t, r, hub, cols), scale in zip(picks, scales):
-        rows = [3 * cells_x + 3 * r + c for c in range(3)]
+        rows = [first_row + 3 * r + c for c in range(3)]
         total = [own[n] + (low[n] + high[n]) for n in rows]
         speed = jnp.sqrt(total[0] * total[0] + total[1] * total[1] + total[2] * total[2])
         pull = strength[r] * (-scale) * speed
@@ -377,17 +376,17 @@
             field[c, hub + d, :, cols] = value
 
 
-def spread_group(t, scale, field, plan, points, own, low, high):
+def spread_group(t, scale, field, plan, points, first_row, own, low, high):
     picks, keeps = group(plan, t)
     scales = [jnp.where(keep, scale, 0.0) for keep in keeps]
-    slabs = slabs_of(*points, own, low, high, field.shape[1:], scales, picks)
+    slabs = slabs_of(*points, first_row, own, low, high, field.shape[2], scales, picks)
     for (_, _, hub, cols), slab in zip(picks, slabs):
         add_slab(field, slab, hub, cols)
 
 
 def spread_sample(
     section_in, inflow, ghost_near, ghost_far, own_low, own_high, own_near, own_far, got_low, got_high,
-    plan, weight_y, weight_z, strength,
+    own, part_low, part_high, plan, weight_y, weight_z, strength,
     section, section_out, stored_z, pack_low, pack_high, edge_near, edge_far,
     share_out, sem, sem_z,
 ):
@@ -422,20 +421,15 @@
 
     def spread_step(t, carry):
         points = (lambda n, r: weight_y[n], weight_z, strength)
-        spread_group(t, TIME_STEP, section, plan, points, own_low, got_low, got_high)
+        spread_group(t, TIME_STEP, section, plan, points, 0, own, part_low, part_high)
         return carry
 
     lax.fori_loop(0, groups_of(plan), spread_step, 0)
     copy = pltpu.make_async_copy(section, section_out, sem)
     copy.start()
-    pack_edges(section, edge_near, edge_far, pack_low, pack_high)
-
-    def clear(n, carry):
-        for k in range(SUB):
-            pack_low[first_row + n * SUB + k] = jnp.zeros_like(own_low[0])
-        return carry
-
-    lax.fori_loop(0, 3 * records // SUB, clear, 0)
+    pack_sides(section, edge_near, edge_far)
+    pack_rows(section, pack_low, pack_high, 0, cells_x)
+    clear_rows(pack_low, first_row, first_row + 3 * records)
 
     def sample_step(t, carry):
         picks, keeps = group(plan, t)
@@ -446,7 +440,7 @@
     lax.fori_loop(0, groups_of(plan), sample_step, 0)
 
     def copy_rows(r, carry):
-        old = [own_low[first_row + 3 * r + c] for c in range(3)]
+        old = [own[3 * r + c] for c in range(3)]
         new = [pack_low[first_row + 3 * r + c] for c in range(3)]
         for c in range(3):
             pack_high[first_row + 3 * r + c] = new[c]
@@ -559,7 +553,9 @@
         ready = wait_to(ready, (picks[-1][2] + RAD) // CHUNK + 1)
         sent = send_to(sent, (picks[0][2] - RAD) // CHUNK)
         points = (weight_of, weight_z, strength)
-        spread_group(t, factor * TIME_STEP, field, plan, points, own_low, got_low, got_high)
+        first_row = 3 * field.shape[1]
+        packs = (own_low, got_low, got_high)
+        spread_group(t, factor * TIME_STEP, field, plan, points, first_row, *packs)
         return ready, sent
 
     zero = jnp.int32(0)
@@ -658,7 +654,7 @@
         advance(i, k, factor, field, now, target, finish)
 
 
-def advance_first(field, section, shifts, slot_a, slot_b):
+def advance_first(field, after, section, shifts, slot_a, slot_b):
     fill_shifts(shifts)
     along_depth(0, field, shifts, slot_a)
 
@@ -794,18 +790,17 @@
     unit_sems = pltpu.SemaphoreType.DMA((units // TILES,))
     chunk_sems = pltpu.SemaphoreType.DMA((chunks,))
 
-    field, *own_a, weight_y, weight_z, strength, point_y, plan = pl.pallas_call(
-        load_sample,
+    halo = array((3 * cells_x, 1, points), f32)
+    field, *own_a, strength, point_y, point_z, plan = pl.pallas_call(
+        load_field,
         out_shape=(
-            held, pack, pack, edge, edge,
-            pltpu.VMEM(y_shape, f32), pltpu.VMEM(z_shape, jnp.bfloat16),
-            array(per_record, f32), array(per_record, i32),
+            held, halo, halo, edge, edge,
+            array(per_record, f32), array(per_record, i32), array(per_record, i32),
             array((SUB, units), i32),
         ),
         in_specs=[ANYWHERE] * 4 + [SCALAR],
-        out_specs=(WHOLE,) * 9 + (SCALAR,),
+        out_specs=(WHOLE,) * 8 + (SCALAR,),
         scratch_shapes=[
-            pltpu.VMEM(per_record, i32),
             pltpu.VMEM((records, LANES), i32),
             pltpu.VMEM((2, records), i32),
             pltpu.VMEM((2, records, points), i32),
@@ -816,22 +811,37 @@
             chunk_sems,
         ],
         compiler_params=params(),
-        cost_estimate=cost(2 * 10**9, 4 * size),
-        name="load_sample",
+        cost_estimate=cost(10**9, size),
+        name="load_field",
     )(streamed(velocity), streamed(positions), streamed(tiles), streamed(coefs), counts)
+    field = resident(field)
+    ghosts_a = exchange(*own_a)
+
+    weight_y, weight_z, partial = pl.pallas_call(
+        sample_first,
+        out_shape=(
+            pltpu.VMEM(y_shape, f32), pltpu.VMEM(z_shape, jnp.bfloat16),
+            array((3 * records, 1, points), f32),
+        ),
+        in_specs=[WHOLE, SCALAR, WHOLE, WHOLE],
+        out_specs=(WHOLE,) * 3,
+        compiler_params=params(),
+        cost_estimate=cost(2 * 10**9, size),
+        name="sample_first",
+    )(field, plan, point_y, point_z)
     weight_y, weight_z = resident(weight_y), resident(weight_z)
-    ghosts_a = exchange(*own_a)
+    parts_a = (partial, shifted(partial, "gy", 1), shifted(partial, "gy", -1))
 
     section = pl.pallas_call(
         advance_first,
         out_shape=held,
-        in_specs=[WHOLE],
+        in_specs=[WHOLE, ANYWHERE],
         out_specs=WHOLE,
         scratch_shapes=products,
         compiler_params=params(),
         cost_estimate=cost(10**9, 4 * size),
         name="advance_first",
-    )(resident(field))
+    )(field, partial)
 
     _, section, stored_z, *own_b, shares = pl.pallas_call(
         spread_sample,
@@ -840,7 +850,7 @@
             pack, pack, edge, edge,
             array((groups_y, 2, 3 * share, 1, points), f32),
         ),
-        in_specs=[WHOLE] * 10 + [SCALAR] + [WHOLE] * 3,
+        in_specs=[WHOLE] * 13 + [SCALAR] + [WHOLE] * 3,
         out_specs=(WHOLE,) + (ANYWHERE,) * 2 + (WHOLE,) * 5,
         input_output_aliases={0: 0},
         scratch_shapes=[pltpu.SemaphoreType.DMA, unit_sems],
@@ -849,7 +859,7 @@
         name="spread_sample",
     )(
         resident(section), inflow, *ghosts_a[:2], *own_a, *ghosts_a[2:],
-        plan, weight_y, weight_z, strength,
+        *parts_a, plan, weight_y, weight_z, strength,
     )
     shares = lax.all_to_all(shares, "gy", 0, 0)
     ghosts_b = exchange(*own_b)

time: 84.8 us -> 83.1 us (0.980)
  the two profiles are of different devices: /device:TPU:1 before, /device:TPU:0 now
where the time goes in v8:
time: 83.1 us; the launch traced here: 83 us
  Pallas kernels  44.7 us (54%)
  starting transfers between devices  31.9 us (38%)
  waiting for transfers between devices  4.29 us (5%)
  between operations  1.39 us (2%)
    ppermute x6, starting transfers between devices, shifted(): lax.ppermute(x, axis, [(i, (i + step) % count) for i in range(count)])  15.1 us
    pallas_call x1, Pallas kernels, local(): pl.pallas_call(advance_second, out_shape=(stored, array((SUB, LANES), f32...  11.7 us
    pallas_call x1, Pallas kernels, local(): pl.pallas_call(advance_first, out_shape=held, in_specs=[WHOLE, ANYWHERE],...  10.3 us
    pallas_call x1, Pallas kernels, local(): pl.pallas_call(spread_next, out_shape=stored, in_specs=[ANYWHERE] + [WHOL...  9.42 us
    all_to_all x1, starting transfers between devices, local(): all_forces = lax.all_to_all(forces, 'gy', 0, 0)  8.69 us
    pallas_call x1, Pallas kernels, local(): pl.pallas_call(spread_sample, out_shape=(held, stored, pltpu.HBM(z_shape,...  6.57 us
    all_to_all x1, starting transfers between devices, local(): shares = lax.all_to_all(shares, 'gy', 0, 0)  6.15 us
    pallas_call x1, Pallas kernels, local(): pl.pallas_call(load_field, out_shape=(held, halo, halo, edge, edge, array...  4.66 us
  transfers between devices with their start and end apart: 12, of which 3 were waited for; matrix products, arithmetic and copies ran while one was open for 0% of the time, Pallas kernels for 40%

profile of v8, /device:TPU:0, one launch (start us, length us, event | category | flops | bytes accessed | tf_op | source)
XLA Modules:
  0.0 83.0 jit_solution(7902300011512385450)
XLA Ops:
  1.3 4.7 %load_field.1 = (f32[3,96,32,256]{3,2,1,0:T(8,128)S(1)}, f32[288,1,256]{2,1,0:T(1,128)S(1)}, f32[288,1,256]{2,1,0:T(1,128)S(1)}, f32[3,32,256]{2,1,0:T(8,128)S(1...) custom-call(f32[3,96,32,256]{3,2,1,0:T(8,128)} %velocity.3, ...), custom_call_target="tpu_custom_call" | custom-call | flops 1000000000 | bytes 9437184 | tf_op jit(solution)/shard_map/load_field/pallas_call | solution.py:794
  5.9 0.5 collective-permute-start
  6.5 5.6 %collective-permute-start.3 = (f32[288,1,256]{2,1,0:T(1,128)S(1)}, f32[288,1,256]{2,1,0:T(1,128)S(1)}, u32[]{:S(2)}, u32[]{:S(2)}) collective-permute-start(f32[288,1,256]{2,1,0:T(1,128)S(1)} %get-tuple-element.30.own_low), channel_id=1, source_target_pairs={{0,7},{1,0},{2,1},{3,2},{4,3},{5,4},{6,5},{7,6},{8,15},{9,8},{10,9... | collective-permute-start | bytes 884744 | tf_op jit(solution)/shard_map/ppermute | solution.py:753
  12.1 0.0 collective-permute-start.2
  12.1 1.2 %sample_first.1 = (f32[128,32,256]{2,1,0:T(8,128)S(1)}, bf16[128,256,256]{2,1,0:T(8,128)(2,1)S(1)}, f32[192,1,256]{2,1,0:T(1,128)S(1)}) custom-call(f32[3,96,32,256]{3,2,1,0:T(8,128)S(1)} %get-tuple-element.23.field, s32[8,128]{1,0:T(8,128)S(1)} %get-tuple-element.24.plan, s32[64,1,256]{2,1,0:T(1,128)S(1)} %get-tuple-element.25.point_y, ...), custom_call_target="tpu_custom_call" | custom-call | flops 2000000000 | bytes 9437184 | tf_op jit(solution)/shard_map/sample_first/pallas_call | solution.py:820
  13.2 4.8 %collective-permute-start.5 = (f32[192,1,256]{2,1,0:T(1,128)S(1)}, f32[192,1,256]{2,1,0:T(1,128)S(1)}, u32[]{:S(2)}, u32[]{:S(2)}) collective-permute-start(f32[192,1,256]{2,1,0:T(1,128)S(1)} %get-tuple-element.27.after.own), channel_id=1, source_target_pairs={{0,7},{1,0},{2,1},{3,2},{4,3},{5,4},{6,5},{7,6},{8,15},{9,8},{10,9... | collective-permute-start | bytes 589832 | tf_op jit(solution)/shard_map/ppermute | solution.py:753
  18.0 0.0 collective-permute-start.4
  18.0 0.0 collective-permute-done.ghost_near
  18.0 0.0 copy-start
  18.0 0.8 collective-permute-start.1
  18.8 10.3 %advance_first.1.section_in = f32[3,96,32,256]{3,2,1,0:T(8,128)S(1)} custom-call(f32[3,96,32,256]{3,2,1,0:T(8,128)S(1)} %get-tuple-element.23.field, f32[192,1,256]{2,1,0:T(1,128)S(1)} %get-tuple-element.27.after.own), custom_call_target="tpu_custom_call" | custom-call | flops 1000000000 | bytes 37748736 | tf_op jit(solution)/shard_map/advance_first/pallas_call | solution.py:835
  29.2 0.0 collective-permute-done.1.ghost_far
  29.2 1.8 %collective-permute-done.5.part_high = f32[192,1,256]{2,1,0:T(1,128)S(1)} collective-permute-done((f32[192,1,256]{2,1,0:T(1,128)S(1)}, f32[192,1,256]{2,1,0:T(1,128)S(1)}, u32[]{:S(2)}, u32[]{:S(2)}) %collective-permute-start.5) | collective-permute-done | bytes 196640 | tf_op jit(solution)/shard_map/ppermute | solution.py:753
  30.9 0.6 collective-permute-done.4.part_low
  31.6 0.0 collective-permute-done.3.got_high
  31.6 0.0 collective-permute-done.2.got_low
  31.6 0.0 copy-done
  31.6 6.6 %spread_sample.1 = (f32[3,96,32,256]{3,2,1,0:T(8,128)S(1)}, f32[3,96,32,256]{3,2,1,0:T(8,128)}, bf16[128,256,256]{2,1,0:T(8,128)(2,1)}, f32[480,1,256]{2,1,0:T(1...) custom-call(f32[3,96,32,256]{3,2,1,0:T(8,128)S(1)} %advance_first.1., ...), custom_call_target="tpu_custom_call", output_to_operand_aliasing={{0}: (0, {})} | custom-call | flops 2000000000 | bytes 37748736 | tf_op jit(solution)/shard_map/spread_sample/pallas_call | solution.py:846
  38.1 6.1 %all-to-all-start = ((f32[8,2,24,1,256]{4,3,2,1,0:T(1,128)}), f32[8,2,24,1,256]{4,3,2,1,0:T(1,128)S(1)}, u32[]{:S(2)}, u32[]{:S(2)}) async-start(f32[8,2,24,1,256]{4,3,2,1,0:T(1,128)} %get-tuple-element.42), calls=%async_computation | async-start | bytes 786432 | tf_op jit(solution)/shard_map/all_to_all | solution.py:864
  44.3 4.7 %collective-permute-start.9 = (f32[480,1,256]{2,1,0:T(1,128)S(1)}, f32[480,1,256]{2,1,0:T(1,128)S(1)}, u32[]{:S(2)}, u32[]{:S(2)}) collective-permute-start(f32[480,1,256]{2,1,0:T(1,128)S(1)} %get-tuple-element.39.own_low), channel_id=1, source_target_pairs={{0,7},{1,0},{2,1},{3,2},{4,3},{5,4},{6,5},{7,6},{8,15},{9,8},{10,9... | collective-permute-start | bytes 1474568 | tf_op jit(solution)/shard_map/ppermute | solution.py:753
  49.0 0.0 collective-permute-start.8
  49.0 0.0 collective-permute-start.6
  49.0 0.7 collective-permute-start.7
  49.7 11.7 %advance_second.1 = (f32[3,96,32,256]{3,2,1,0:T(8,128)}, f32[8,128]{1,0:T(8,128)S(1)}) custom-call(f32[3,96,32,256]{3,2,1,0:T(8,128)} %get-tuple-element.35.section_hbm, f32[3,96,32,256]{3,2,1,0:T(8,128)} %velocity.3), custom_call_target="tpu_custom_call" | custom-call | flops 1000000000 | bytes 37748736 | tf_op jit(solution)/shard_map/advance_second/pallas_call | solution.py:867
  61.4 0.0 collective-permute-done.6.after_low.ghost_near
  61.4 0.0 collective-permute-done.7.after_high.ghost_far
  61.4 0.0 all-to-all-done.parts
  61.5 0.8 share_force.1.after
  62.3 8.7 %all-to-all-start.1 = ((f32[8,24,1,256]{3,2,1,0:T(1,128)}), f32[8,24,1,256]{3,2,1,0:T(1,128)S(1)}, u32[]{:S(2)}, u32[]{:S(2)}) async-start(f32[8,24,1,256]{3,2,1,0:T(1,128)} %share_force.1.after), calls=%async_computation.1 | async-start | bytes 393216 | tf_op jit(solution)/shard_map/all_to_all | solution.py:889
  71.0 1.9 %collective-permute-done.9.got_high = f32[480,1,256]{2,1,0:T(1,128)S(1)} collective-permute-done((f32[480,1,256]{2,1,0:T(1,128)S(1)}, f32[480,1,256]{2,1,0:T(1,128)S(1)}, u32[]{:S(2)}, u32[]{:S(2)}) %collective-permute-start.9) | collective-permute-done | bytes 491552 | tf_op jit(solution)/shard_map/ppermute | solution.py:753
  72.8 0.0 collective-permute-done.8.got_low
  72.8 9.4 %spread_next.1 = f32[3,96,32,256]{3,2,1,0:T(8,128)} custom-call(f32[3,96,32,256]{3,2,1,0:T(8,128)} %get-tuple-element.36.following, f32[3,32,256]{2,1,0:T(8,128)S(1)} %copy-done, f32[3,32,256]{2,1,0:T(8,128)S(1)} %collective-permute-done.6.after_low.ghost_near, f32[3,32,256]{2,1,0:T(8,128)S(1)} %collective-permute-done.7.after_high.ghost_far, ...), custom_call_target="tpu_custom_call" | custom-call | flops 2000000000 | bytes 37748736 | tf_op jit(solution)/shard_map/spread_next/pallas_call | solution.py:891
  82.3 0.0 all-to-all-done.1
  82.3 0.7 copy.9
Async XLA Ops:
  5.9 12.1 %collective-permute-start = (f32[3,32,256]{2,1,0:T(8,128)S(1)}, f32[3,32,256]{2,1,0:T(8,128)S(1)}, u32[]{:S(2)}, u32[]{:S(2)}) collective-permute-start(f32[3,32,256]{2,1,0:T(8,128)S(1)} %get-tuple-element.28.own_near), channel_id=1, source_target_pairs={{0,8},{16,24},{8,0},{24,16},{1,9},{17,25},{9,1},{25,17},{2,10},{18... | collective-permute-start | bytes 294920 | tf_op jit(solution)/shard_map/ppermute | solution.py:759
  6.5 25.1 %collective-permute-start.3 = (f32[288,1,256]{2,1,0:T(1,128)S(1)}, f32[288,1,256]{2,1,0:T(1,128)S(1)}, u32[]{:S(2)}, u32[]{:S(2)}) collective-permute-start(f32[288,1,256]{2,1,0:T(1,128)S(1)} %get-tuple-element.30.own_low), channel_id=1, source_target_pairs={{0,7},{1,0},{2,1},{3,2},{4,3},{5,4},{6,5},{7,6},{8,15},{9,8},{10,9... | collective-permute-start | bytes 884744 | tf_op jit(solution)/shard_map/ppermute | solution.py:753
  12.1 19.5 %collective-permute-start.2 = (f32[288,1,256]{2,1,0:T(1,128)S(1)}, f32[288,1,256]{2,1,0:T(1,128)S(1)}, u32[]{:S(2)}, u32[]{:S(2)}) collective-permute-start(f32[288,1,256]{2,1,0:T(1,128)S(1)} %get-tuple-element.31.own_high), channel_id=1, source_target_pairs={{0,1},{1,2},{2,3},{3,4},{4,5},{5,6},{6,7},{7,0},{8,9},{9,10},{10,1... | collective-permute-start | bytes 884744 | tf_op jit(solution)/shard_map/ppermute | solution.py:753
  13.2 17.7 %collective-permute-start.5 = (f32[192,1,256]{2,1,0:T(1,128)S(1)}, f32[192,1,256]{2,1,0:T(1,128)S(1)}, u32[]{:S(2)}, u32[]{:S(2)}) collective-permute-start(f32[192,1,256]{2,1,0:T(1,128)S(1)} %get-tuple-element.27.after.own), channel_id=1, source_target_pairs={{0,7},{1,0},{2,1},{3,2},{4,3},{5,4},{6,5},{7,6},{8,15},{9,8},{10,9... | collective-permute-start | bytes 589832 | tf_op jit(solution)/shard_map/ppermute | solution.py:753
  18.0 13.6 %collective-permute-start.4 = (f32[192,1,256]{2,1,0:T(1,128)S(1)}, f32[192,1,256]{2,1,0:T(1,128)S(1)}, u32[]{:S(2)}, u32[]{:S(2)}) collective-permute-start(f32[192,1,256]{2,1,0:T(1,128)S(1)} %get-tuple-element.27.after.own), channel_id=1, source_target_pairs={{0,1},{1,2},{2,3},{3,4},{4,5},{5,6},{6,7},{7,0},{8,9},{9,10},{10,1... | collective-permute-start | bytes 589832 | tf_op jit(solution)/shard_map/ppermute | solution.py:753
  18.0 13.6 %copy-start = (f32[3,32,256]{2,1,0:T(8,128)S(1)}, f32[3,32,256]{2,1,0:T(8,128)}, u32[]{:S(2)}) copy-start(f32[3,32,256]{2,1,0:T(8,128)} %inflow.3) | copy-start | bytes 294916
  18.0 11.1 %collective-permute-start.1 = (f32[3,32,256]{2,1,0:T(8,128)S(1)}, f32[3,32,256]{2,1,0:T(8,128)S(1)}, u32[]{:S(2)}, u32[]{:S(2)}) collective-permute-start(f32[3,32,256]{2,1,0:T(8,128)S(1)} %get-tuple-element.29.own_far), channel_id=1, source_target_pairs={{8,16},{16,8},{9,17},{17,9},{10,18},{18,10},{11,19},{19,11},{12,20... | collective-permute-start | bytes 294920 | tf_op jit(solution)/shard_map/ppermute | solution.py:759
  38.1 23.3 %all-to-all-start = ((f32[8,2,24,1,256]{4,3,2,1,0:T(1,128)}), f32[8,2,24,1,256]{4,3,2,1,0:T(1,128)S(1)}, u32[]{:S(2)}, u32[]{:S(2)}) async-start(f32[8,2,24,1,256]{4,3,2,1,0:T(1,128)} %get-tuple-element.42), calls=%async_computation | async-start | bytes 786432 | tf_op jit(solution)/shard_map/all_to_all | solution.py:864
  44.3 28.5 %collective-permute-start.9 = (f32[480,1,256]{2,1,0:T(1,128)S(1)}, f32[480,1,256]{2,1,0:T(1,128)S(1)}, u32[]{:S(2)}, u32[]{:S(2)}) collective-permute-start(f32[480,1,256]{2,1,0:T(1,128)S(1)} %get-tuple-element.39.own_low), channel_id=1, source_target_pairs={{0,7},{1,0},{2,1},{3,2},{4,3},{5,4},{6,5},{7,6},{8,15},{9,8},{10,9... | collective-permute-start | bytes 1474568 | tf_op jit(solution)/shard_map/ppermute | solution.py:753
  49.0 23.8 %collective-permute-start.8 = (f32[480,1,256]{2,1,0:T(1,128)S(1)}, f32[480,1,256]{2,1,0:T(1,128)S(1)}, u32[]{:S(2)}, u32[]{:S(2)}) collective-permute-start(f32[480,1,256]{2,1,0:T(1,128)S(1)} %get-tuple-element.40.own_high), channel_id=1, source_target_pairs={{0,1},{1,2},{2,3},{3,4},{4,5},{5,6},{6,7},{7,0},{8,9},{9,10},{10,1... | collective-permute-start | bytes 1474568 | tf_op jit(solution)/shard_map/ppermute | solution.py:753
  49.0 12.4 %collective-permute-start.6 = (f32[3,32,256]{2,1,0:T(8,128)S(1)}, f32[3,32,256]{2,1,0:T(8,128)S(1)}, u32[]{:S(2)}, u32[]{:S(2)}) collective-permute-start(f32[3,32,256]{2,1,0:T(8,128)S(1)} %get-tuple-element.37.own_near), channel_id=1, source_target_pairs={{0,8},{16,24},{8,0},{24,16},{1,9},{17,25},{9,1},{25,17},{2,10},{18... | collective-permute-start | bytes 294920 | tf_op jit(solution)/shard_map/ppermute | solution.py:759
  49.0 12.4 %collective-permute-start.7 = (f32[3,32,256]{2,1,0:T(8,128)S(1)}, f32[3,32,256]{2,1,0:T(8,128)S(1)}, u32[]{:S(2)}, u32[]{:S(2)}) collective-permute-start(f32[3,32,256]{2,1,0:T(8,128)S(1)} %get-tuple-element.38.own_far), channel_id=1, source_target_pairs={{8,16},{16,8},{9,17},{17,9},{10,18},{18,10},{11,19},{19,11},{12,20... | collective-permute-start | bytes 294920 | tf_op jit(solution)/shard_map/ppermute | solution.py:759
  62.3 20.0 %all-to-all-start.1 = ((f32[8,24,1,256]{3,2,1,0:T(1,128)}), f32[8,24,1,256]{3,2,1,0:T(1,128)S(1)}, u32[]{:S(2)}, u32[]{:S(2)}) async-start(f32[8,24,1,256]{3,2,1,0:T(1,128)} %share_force.1.after), calls=%async_computation.1 | async-start | bytes 393216 | tf_op jit(solution)/shard_map/all_to_all | solution.py:889
